TPU v7x, 256 devices: a whole 4x4x8 slice. The times are simulated.
256 devices in a mesh: gx: 8 (over z), gy: 4 (over y_lo, core), gz: 8 (over y_hi, x).
Axes of the slice: x: 4, y: 4 (y_hi: 2, y_lo: 2; y = y_hi * 2 + y_lo), z: 8, core: 2. Of those that a mesh axis runs over, the one named last changes fastest.
Arguments:
- strain: float32 [3, 256, 128, 2048], P(None, 'gx', 'gy', 'gz'), may hold values from -6 to 6
- plastic_old: float32 [256, 128, 2048], P('gx', 'gy', 'gz'), may hold values from -8 to 0
- alpha_old: float32 [256, 128, 2048], P('gx', 'gy', 'gz'), may hold values from 0 to 1.2
- kappa_old: float32 [256, 128, 2048], P('gx', 'gy', 'gz'), may hold values from 2.8 to 4.2
- flags: int32 [256, 128, 8], P('gx', 'gy', 'gz'), may hold values from 0 to 1, as said below
Outputs:
- internal_force: float32 [256, 128, 2048], P('gx', 'gy', 'gz')
- kappa_new: float32 [256, 128, 2048], P('gx', 'gy', 'gz')
Inputs may be any that keep to these rules, and one draw needn't show every extreme that they name: `flags`: at most 512 blocks of one device are active; on the devices at the lowest position along the first dimension exactly 512 are.
All inputs are finite; a program needn't handle non-finite values.
Results may differ from a plain program's by a relative error of at most 0.000057.
Values sent between devices are 32-bit elements; how exact they have to be, the bound alone decides.
No kernel may reach another device: no remote copies, remote signals or barrier semaphores. Data moves between devices by JAX's collectives and lax.ppermute only.
A program may use at most 64 MiB of HBM per device.

v0:
```python
import math

import jax
import jax.numpy as jnp
from jax import lax
from jax.sharding import PartitionSpec as P

REACH = 6
RM_ITERS = 2


length_scale = 3.0


def padded_2(cells, sides, width):
    for axis, dim in sides:
        count = lax.axis_size(axis)
        ends = count - 1
        head = lax.slice_in_dim(cells, 0, width, axis=dim)
        tail = lax.slice_in_dim(cells, cells.shape[dim] - width, cells.shape[dim], axis=dim)
        cells = jnp.concatenate(
            [
                lax.ppermute(tail, axis, [(i, (i + 1) % count) for i in range(ends)]),
                cells,
                lax.ppermute(head, axis, [((i + 1) % count, i) for i in range(ends)]),
            ],
            axis=dim,
        )
    return cells


def shifted(block, axis, distance):
    devices = range(lax.axis_size(axis))
    route = [(i - distance, i) for i in devices if i - distance in devices]
    return lax.ppermute(block, axis, route)


def gauss(offset):
    return math.exp(-offset * offset / (2.0 * length_scale * length_scale))


def band_matrix(length):
    rows_index = jnp.arange(length + 2 * REACH)[:, None]
    cols_index = jnp.arange(length)[None, :]
    offset = (rows_index - cols_index - REACH).astype(jnp.float32)
    values = jnp.exp(-offset * offset / (2.0 * length_scale * length_scale))
    return jnp.where(jnp.abs(offset) <= REACH, values, 0.0)


def along_first(field):
    return jnp.einsum(
        "fjyz,ji->fiyz",
        field,
        band_matrix(field.shape[1] - 2 * REACH),
        precision=lax.Precision.HIGHEST,
    )


def along_second(field):
    return jnp.einsum(
        "fxjz,ji->fxiz",
        field,
        band_matrix(field.shape[2] - 2 * REACH),
        precision=lax.Precision.HIGHEST,
    )


def along_third(field):
    return jnp.einsum(
        "fxyj,ji->fxyi",
        field,
        band_matrix(field.shape[3] - 2 * REACH),
        precision=lax.Precision.HIGHEST,
    )


def reach_total(place, count, local):
    position = place * local + jnp.arange(local, dtype=jnp.int32)
    extent = count * local
    total = jnp.zeros((local,), jnp.float32)
    for offset in range(-REACH, REACH + 1):
        inside = (position + offset >= 0) & (position + offset < extent)
        total = total + gauss(offset) * inside.astype(jnp.float32)
    return total


def newton_plastic(trial, alpha_old):
    increment = jnp.zeros(trial.shape, jnp.float32)
    for repeat in range(RM_ITERS):
        hardened = alpha_old + increment
        soft = 0.5 * jnp.exp(-5.0 * hardened)
        excess = trial - increment - (1.0 + 0.5 * hardened - soft)
        increment = jnp.maximum(increment + excess / (1.5 + 5.0 * soft), 0.0)
    return increment


def assemble(first, second, third):
    shape = first.shape
    nodes = jnp.zeros((shape[0] + 1, shape[1] + 1, shape[2] + 1), jnp.float32)
    for side_x in (0, 1):
        for side_y in (0, 1):
            for side_z in (0, 1):
                term = 0.25 * (
                    (2 * side_x - 1) * first + (2 * side_y - 1) * second + (2 * side_z - 1) * third
                )
                nodes = nodes + jnp.pad(
                    term, ((side_x, 1 - side_x), (side_y, 1 - side_y), (side_z, 1 - side_z))
                )
    return nodes


def body(strain, plastic_old, alpha_old, kappa_old, flags):
    width_x, width_y, width_z = plastic_old.shape
    local_drive = strain[0] * strain[0] + strain[1] * strain[1] + strain[2] * strain[2]
    trial = strain[0] - plastic_old
    increment = newton_plastic(trial, alpha_old) * flags.astype(jnp.float32)
    fields = jnp.stack([local_drive, increment])
    padded = padded_2(fields, (("gx", 1), ("gy", 2), ("gz", 3)), REACH)
    summed = along_first(along_second(along_third(padded)))
    total_x = reach_total(lax.axis_index("gx"), lax.axis_size("gx"), width_x)
    total_y = reach_total(lax.axis_index("gy"), lax.axis_size("gy"), width_y)
    total_z = reach_total(lax.axis_index("gz"), lax.axis_size("gz"), width_z)
    weight_total = total_x[:, None, None] * total_y[None, :, None] * total_z[None, None, :]
    avg_drive = summed[0] / weight_total
    avg_plastic = summed[1] / weight_total
    kappa_new = jnp.maximum(kappa_old, avg_drive + 4.0 * avg_plastic)
    integrity = jnp.exp(-jnp.maximum(kappa_new - 3.2, 0.0) / 3.0)
    nodes = assemble(
        integrity * (strain[0] - plastic_old - increment),
        integrity * strain[1],
        integrity * strain[2],
    )
    moved = shifted(nodes[width_x], "gx", 1)
    nodes = nodes[:width_x].at[0].add(moved)
    moved = shifted(nodes[:, width_y], "gy", 1)
    nodes = nodes[:, :width_y].at[:, 0].add(moved)
    moved = shifted(nodes[:, :, width_z], "gz", 1)
    nodes = nodes[:, :, :width_z].at[:, :, 0].add(moved)
    return (nodes, kappa_new)


def solution(mesh):
    in_specs = (
        P(None, "gx", "gy", "gz"),
        P("gx", "gy", "gz"),
        P("gx", "gy", "gz"),
        P("gx", "gy", "gz"),
        P("gx", "gy", "gz"),
    )
    out_specs = (P("gx", "gy", "gz"), P("gx", "gy", "gz"))
    return jax.shard_map(body, mesh=mesh, in_specs=in_specs, out_specs=out_specs, check_vma=False)
```

profile of v0, /device:TPU:120, one launch (start us, length us, event | category | flops | bytes accessed | tf_op | source)
XLA Modules:
  0.0 123.1 jit_solution(14483252526098263491)
XLA Ops:
  0.6 0.0 copy-start.1
  0.6 0.0 copy-start.5
  0.7 0.9 convert_element_type.35
  1.5 2.2 %multiply_add_fusion = f32[1,32,32,256]{3,2,1,0:T(8,128)S(1)} fusion(f32[3,32,32,256]{3,2,1,0:T(8,128)} %param.11), kind=kLoop, calls=%fused_computation.43 | loop fusion | flops 1310720 | bytes 4194304 | tf_op jit(solution)/shard_map/add | solution.py:114
  3.7 0.0 copy-done.1
  3.7 0.0 copy-done.5
  3.7 2.3 %maximum_multiply_fusion = f32[32,32,256]{2,1,0:T(8,128)S(1)} fusion(f32[32,32,256]{2,1,0:T(8,128)S(1)} %copy-done.5, f32[32,32]{1,0:T(8,128)S(1)} %bitcast.57, f32[32,32,256]{2,1,0:T(8,128)S(1)} %copy-done.1, f32[3,32,32,256]{3,2,1,0:T(8,128)} %param.11), kind=kLoop, calls=%fused_computation.42 | loop fusion | flops 6553600 | bytes 4198400 | tf_op jit(solution)/shard_map/mul | solution.py:116
  6.0 0.1 pad_maximum_fusion.6
  6.1 5.0 %collective-permute-start = (f32[2,6,32,256]{3,2,1,0:T(8,128)S(1)}, f32[2,6,32,256]{3,2,1,0:T(8,128)S(1)}, u32[]{:S(2)}, u32[]{:S(2)}) collective-permute-start(f32[2,6,32,256]{3,2,1,0:T(8,128)S(1)} %get-tuple-element.58), channel_id=1, source_target_pairs={{0,32},{32,64},{64,96},{96,128},{128,160},{160,192},{192,224},{1,3... | collective-permute-start | bytes 1179656 | tf_op jit(solution)/shard_map/ppermute | solution.py:23
  11.2 1.9 %collective-permute-start.1 = (f32[2,6,32,256]{3,2,1,0:T(8,128)S(1)}, f32[2,6,32,256]{3,2,1,0:T(8,128)S(1)}, u32[]{:S(2)}, u32[]{:S(2)}) collective-permute-start(f32[2,6,32,256]{3,2,1,0:T(8,128)S(1)} %get-tuple-element.59), channel_id=1, source_target_pairs={{32,0},{64,32},{96,64},{128,96},{160,128},{192,160},{224,192},{33,... | collective-permute-start | bytes 1179656 | tf_op jit(solution)/shard_map/ppermute | solution.py:25
  13.1 6.4 %collective-permute-done = f32[2,6,32,256]{3,2,1,0:T(8,128)S(1)} collective-permute-done((f32[2,6,32,256]{3,2,1,0:T(8,128)S(1)}, f32[2,6,32,256]{3,2,1,0:T(8,128)S(1)}, u32[]{:S(2)}, u32[]{:S(2)}) %collective-permute-start) | collective-permute-done | bytes 393248 | tf_op jit(solution)/shard_map/ppermute | solution.py:23
  19.5 5.3 %collective-permute-done.1 = f32[2,6,32,256]{3,2,1,0:T(8,128)S(1)} collective-permute-done((f32[2,6,32,256]{3,2,1,0:T(8,128)S(1)}, f32[2,6,32,256]{3,2,1,0:T(8,128)S(1)}, u32[]{:S(2)}, u32[]{:S(2)}) %collective-permute-start.1) | collective-permute-done | bytes 393248 | tf_op jit(solution)/shard_map/ppermute | solution.py:25
  24.8 0.1 pad_maximum_fusion.4
  25.0 1.2 copy.42
  26.2 1.9 %collective-permute-start.2 = (f32[2,44,6,256]{3,0,2,1:T(2,128)}, f32[2,44,6,256]{3,0,2,1:T(2,128)}, u32[]{:S(2)}, u32[]{:S(2)}) collective-permute-start(f32[2,44,6,256]{3,0,2,1:T(2,128)} %copy.42), channel_id=1, source_target_pairs={{0,8},{8,16},{16,24},{1,9},{9,17},{17,25},{2,10},{10,18},{18,26},{... | collective-permute-start | bytes 1622024 | tf_op jit(solution)/shard_map/ppermute | solution.py:23
  28.1 1.2 copy.43
  29.3 3.6 %collective-permute-start.3 = (f32[2,44,6,256]{3,0,2,1:T(2,128)}, f32[2,44,6,256]{3,0,2,1:T(2,128)}, u32[]{:S(2)}, u32[]{:S(2)}) collective-permute-start(f32[2,44,6,256]{3,0,2,1:T(2,128)} %copy.43), channel_id=1, source_target_pairs={{8,0},{16,8},{24,16},{9,1},{17,9},{25,17},{10,2},{18,10},{26,18},{... | collective-permute-start | bytes 1622024 | tf_op jit(solution)/shard_map/ppermute | solution.py:25
  33.0 0.1 broadcast_multiply_fusion
  33.1 4.1 %collective-permute-done.2 = f32[2,44,6,256]{3,0,2,1:T(2,128)} collective-permute-done((f32[2,44,6,256]{3,0,2,1:T(2,128)}, f32[2,44,6,256]{3,0,2,1:T(2,128)}, u32[]{:S(2)}, u32[]{:S(2)}) %collective-permute-start.2) | collective-permute-done | bytes 540704 | tf_op jit(solution)/shard_map/ppermute | solution.py:23
  37.2 1.1 copy.44
  38.3 0.0 copy-start.2
  38.3 1.8 %collective-permute-done.3 = f32[2,44,6,256]{3,0,2,1:T(2,128)} collective-permute-done((f32[2,44,6,256]{3,0,2,1:T(2,128)}, f32[2,44,6,256]{3,0,2,1:T(2,128)}, u32[]{:S(2)}, u32[]{:S(2)}) %collective-permute-start.3) | collective-permute-done | bytes 540704 | tf_op jit(solution)/shard_map/ppermute | solution.py:25
  40.1 1.1 copy.45
  41.3 0.0 copy-done.2
  41.3 0.0 copy-start.3
  41.3 0.8 copy-done.3
  42.1 1.7 %pad_maximum_fusion = f32[2,44,44,256]{3,2,1,0:T(8,128)S(1)} fusion(f32[2,44,6,256]{3,2,1,0:T(8,128)S(1)} %copy.45, f32[2,6,32,256]{3,2,1,0:T(8,128)} %copy-done.4, f32[1,32,32,256]{3,2,1,0:T(8,128)S(1)} %bitcast.54, f32[1,32,32,256]{3,2,1,0:T(8,128)S(1)} %multiply_add_fusion, f32[2,6,32,256]{3,2,1,0:T(8,128)S(1)} %collective-permute-done, ...), kind=kLoop, calls=%fused_computation.16 | loop fusion | flops 4956160 | bytes 7929856 | tf_op jit(solution)/shard_map/concatenate | solution.py:21
  43.9 2.7 %fusion.100 = (f32[2,44,44,6]{3,2,1,0:T(8,128)}, f32[2,44,44,6]{3,2,1,0:T(8,128)}) fusion(f32[2,44,44,256]{3,2,1,0:T(8,128)S(1)} %pad_maximum_fusion), kind=kLoop, calls=%fused_computation.178 | loop fusion | bytes 371712 | tf_op jit(solution)/shard_map/slice | solution.py:20
  46.6 2.8 %copy.46 = f32[2,44,44,6]{2,0,3,1:T(2,128)} copy(f32[2,44,44,6]{3,2,1,0:T(8,128)} %get-tuple-element.47) | data formatting | bytes 185856 | tf_op jit(solution)/shard_map/slice | solution.py:20
  49.4 3.4 %collective-permute-start.4 = (f32[2,44,44,6]{2,0,3,1:T(2,128)}, f32[2,44,44,6]{2,0,3,1:T(2,128)}, u32[]{:S(2)}, u32[]{:S(2)}) collective-permute-start(f32[2,44,44,6]{2,0,3,1:T(2,128)} %copy.46), channel_id=1, source_target_pairs={{0,1},{1,2},{2,3},{3,4},{4,5},{5,6},{6,7},{8,9},{9,10},{10,11},{11... | collective-permute-start | bytes 278792 | tf_op jit(solution)/shard_map/ppermute | solution.py:23
  52.8 2.8 %copy.47 = f32[2,44,44,6]{2,0,3,1:T(2,128)} copy(f32[2,44,44,6]{3,2,1,0:T(8,128)} %get-tuple-element.48) | data formatting | bytes 185856 | tf_op jit(solution)/shard_map/slice | solution.py:19
  55.6 6.2 %collective-permute-start.5 = (f32[2,44,44,6]{2,0,3,1:T(2,128)}, f32[2,44,44,6]{2,0,3,1:T(2,128)}, u32[]{:S(2)}, u32[]{:S(2)}) collective-permute-start(f32[2,44,44,6]{2,0,3,1:T(2,128)} %copy.47), channel_id=1, source_target_pairs={{1,0},{2,1},{3,2},{4,3},{5,4},{6,5},{7,6},{9,8},{10,9},{11,10},{12... | collective-permute-start | bytes 278792 | tf_op jit(solution)/shard_map/ppermute | solution.py:25
  61.8 0.6 fusion.61
  62.4 0.0 collective-permute-done.4
  62.4 2.8 %copy.48 = f32[2,44,44,6]{3,2,1,0:T(8,128)} copy(f32[2,44,44,6]{2,0,3,1:T(2,128)} %collective-permute-done.4) | data formatting | bytes 185856 | tf_op jit(solution)/shard_map/ppermute | solution.py:23
  65.3 0.6 collective-permute-done.5
  65.9 2.9 %copy.49 = f32[2,44,44,6]{3,2,1,0:T(8,128)} copy(f32[2,44,44,6]{2,0,3,1:T(2,128)} %collective-permute-done.5) | data formatting | bytes 185856 | tf_op jit(solution)/shard_map/ppermute | solution.py:25
  68.7 14.7 %fusion = f32[2,44,44,256]{3,2,1,0:T(8,128)S(1)} fusion(f32[2,44,44,6]{3,2,1,0:T(8,128)} %copy.49, f32[2,44,6,256]{3,2,1,0:T(8,128)} %copy-done.3, f32[2,6,32,256]{3,2,1,0:T(8,128)} %copy-done.4, f32[1,32,32,256]{3,2,1,0:T(8,128)S(1)} %bitcast.55, f32[1,32,32,256]{3,2,1,0:T(8,128)S(1)} %multiply_add_fusion, f32[2,6,32,256]{3,2,1,0:T(8,128)S(1)} %collective-permute-done, ...), kind=kOutput, calls=%fused_computation | convolution fusion | flops 3195683328 | bytes 8115712 | tf_op jit(solution)/shard_map/fxyj,ji->fxyi/dot_general | solution.py:69
  83.4 2.8 %convolution_bitcast_fusion = f32[2,44,32,256]{3,2,1,0:T(8,128)S(1)} fusion(f32[2,44,44,256]{3,2,1,0:T(8,128)S(1)} %fusion), kind=kOutput, calls=%fused_computation.21 | convolution fusion | flops 380645760 | bytes 6848512 | tf_op jit(solution)/shard_map/fxjz,ji->fxiz/dot_general | solution.py:60
  86.2 3.7 %fusion.16 = f32[32,2,32,256]{3,0,2,1:T(8,128)S(1)} fusion(f32[2,44,32,256]{3,2,1,0:T(8,128)S(1)} %convolution_bitcast_fusion), kind=kOutput, calls=%fused_computation.17 | convolution fusion | flops 276836736 | bytes 4980736 | tf_op jit(solution)/shard_map/fjyz,ji->fiyz/dot_general | solution.py:51
  89.9 0.0 copy-start
  89.9 0.0 copy-start.6
  90.0 1.2 copy.64
  91.2 0.6 copy-done
  91.8 0.3 copy-done.6
  92.1 1.9 %add_multiply_fusion.7 = (f32[32,32,256]{2,1,0:T(8,128)S(1)}, f32[32,32,256]{2,1,0:T(8,128)S(1)}, f32[32,32,256]{2,1,0:T(8,128)S(1)}, f32[32,32,256]{2,1,0:T(8,128)S(1)}, f32[32,32,256]{2,1,0:T(8,128)}) fusion(f32[3,32,32,256]{3,2,1,0:T(8,128)S(1)} %copy-done, f32[32,32,256]{2,1,0:T(8,128)S(1)} %maximum_multiply_fusion, f32[32,32,256]{2,1,0:T(8,128)S(1)} %copy-done.1, ...), kind=kLoop, calls=%fused_computation.39 | loop fusion | flops 5505024 | bytes 13636608 | tf_op jit(solution)/shard_map/mul | solution.py:103
  94.0 1.0 add_multiply_fusion.6
  95.0 2.1 %pad_add_fusion = f32[33,33,257]{2,1,0:T(8,128)S(1)} fusion(f32[32,32,256]{2,1,0:T(8,128)S(1)} %get-tuple-element.52, f32[32,32,256]{2,1,0:T(8,128)S(1)} %get-tuple-element.51, f32[32,32,256]{2,1,0:T(8,128)S(1)} %get-tuple-element.53, f32[32,32,256]{2,1,0:T(8,128)S(1)} %get-tuple-element.50, f32[32,32,256]{2,1,0:T(8,128)S(1)} %get-tuple-element.54, ...), kind=kLoop, calls=%fused_computation.20 | loop fusion | flops 1959111 | bytes 9508100 | tf_op jit(solution)/shard_map/add | solution.py:106
  97.1 1.9 %collective-permute-start.6 = (f32[33,257]{1,0:T(8,128)S(1)}, f32[33,257]{1,0:T(8,128)S(1)}, u32[]{:S(2)}, u32[]{:S(2)}) collective-permute-start(f32[33,257]{1,0:T(8,128)S(1)} %slice_bitcast_fusion.2), channel_id=1, source_target_pairs={{0,32},{32,64},{64,96},{96,128},{128,160},{160,192},{192,224},{1,3... | collective-permute-start | bytes 101780 | tf_op jit(solution)/shard_map/ppermute | solution.py:35
  99.1 0.1 slice.151
  99.2 4.1 %collective-permute-done.6 = f32[33,257]{1,0:T(8,128)S(1)} collective-permute-done((f32[33,257]{1,0:T(8,128)S(1)}, f32[33,257]{1,0:T(8,128)S(1)}, u32[]{:S(2)}, u32[]{:S(2)}) %collective-permute-start.6) | collective-permute-done | bytes 33956 | tf_op jit(solution)/shard_map/ppermute | solution.py:35
  103.3 0.1 fusion.101
  103.3 1.9 %collective-permute-start.7 = (f32[32,257]{1,0:T(8,128)S(1)}, f32[32,257]{1,0:T(8,128)S(1)}, u32[]{:S(2)}, u32[]{:S(2)}) collective-permute-start(f32[32,257]{1,0:T(8,128)S(1)} %bitcast.58), channel_id=1, source_target_pairs={{0,8},{8,16},{16,24},{1,9},{9,17},{17,25},{2,10},{10,18},{18,26},{... | collective-permute-start | bytes 98696 | tf_op jit(solution)/shard_map/ppermute | solution.py:35
  105.3 0.2 slice.154
  105.5 3.3 %collective-permute-done.7 = f32[32,257]{1,0:T(8,128)S(1)} collective-permute-done((f32[32,257]{1,0:T(8,128)S(1)}, f32[32,257]{1,0:T(8,128)S(1)}, u32[]{:S(2)}, u32[]{:S(2)}) %collective-permute-start.7) | collective-permute-done | bytes 32928 | tf_op jit(solution)/shard_map/ppermute | solution.py:35
  108.8 0.1 copy.53
  108.8 1.9 %scatter-add.11 = f32[32,32,257]{2,1,0:T(8,128)S(1)} dynamic-update-slice(f32[32,32,257]{2,1,0:T(8,128)S(1)} %slice.154, f32[32,1,257]{2,1,0:T(1,128)S(1)} %copy.53, s32[]{:T(128)} %constant.204.clone.1, s32[]{:T(128)} %constant.204.clone.1, s32[]{:T(128)} %constant.204.clone.1) | dynamic-update-slice | bytes 65796 | tf_op jit(solution)/shard_map/scatter-add | solution.py:136
  110.7 0.2 slice_reduce_fusion
  111.0 1.9 %collective-permute-start.8 = (f32[32,32]{1,0:T(8,128)S(1)}, f32[32,32]{1,0:T(8,128)S(1)}, u32[]{:S(2)}, u32[]{:S(2)}) collective-permute-start(f32[32,32]{1,0:T(8,128)S(1)} %slice_reduce_fusion), channel_id=1, source_target_pairs={{0,1},{1,2},{2,3},{3,4},{4,5},{5,6},{6,7},{8,9},{9,10},{10,11},{11... | collective-permute-start | bytes 12296 | tf_op jit(solution)/shard_map/ppermute | solution.py:35
  112.9 1.1 slice.157
  113.9 6.7 %collective-permute-done.8 = f32[32,32]{1,0:T(8,128)S(1)} collective-permute-done((f32[32,32]{1,0:T(8,128)S(1)}, f32[32,32]{1,0:T(8,128)S(1)}, u32[]{:S(2)}, u32[]{:S(2)}) %collective-permute-start.8) | collective-permute-done | bytes 4128 | tf_op jit(solution)/shard_map/ppermute | solution.py:35
  120.7 0.3 copy.54
  120.9 0.1 slice_add_fusion
  121.0 2.1 %scatter-add.14 = f32[32,32,256]{2,1,0:T(8,128)} dynamic-update-slice(f32[32,32,256]{2,1,0:T(8,128)} %slice.157, f32[32,32,1]{2,1,0:T(8,128)S(1)} %slice_add_fusion, s32[]{:T(128)} %constant.204.clone.1, s32[]{:T(128)} %constant.204.clone.1, s32[]{:T(128)} %constant.204.clone.1) | dynamic-update-slice | bytes 8196 | tf_op jit(solution)/shard_map/scatter-add | solution.py:138
  (9 shorter events, 0.1 us)
Async XLA Ops:
  0.6 3.1 %copy-start.1 = (f32[32,32,256]{2,1,0:T(8,128)S(1)}, f32[32,32,256]{2,1,0:T(8,128)}, u32[]{:S(2)}) copy-start(f32[32,32,256]{2,1,0:T(8,128)} %param.12) | copy-start | bytes 3145732
  0.6 3.1 %copy-start.5 = (f32[32,32,256]{2,1,0:T(8,128)S(1)}, f32[32,32,256]{2,1,0:T(8,128)}, u32[]{:S(2)}) copy-start(f32[32,32,256]{2,1,0:T(8,128)} %param.13) | copy-start | bytes 3145732
  6.1 13.4 %collective-permute-start = (f32[2,6,32,256]{3,2,1,0:T(8,128)S(1)}, f32[2,6,32,256]{3,2,1,0:T(8,128)S(1)}, u32[]{:S(2)}, u32[]{:S(2)}) collective-permute-start(f32[2,6,32,256]{3,2,1,0:T(8,128)S(1)} %get-tuple-element.58), channel_id=1, source_target_pairs={{0,32},{32,64},{64,96},{96,128},{128,160},{160,192},{192,224},{1,3... | collective-permute-start | bytes 1179656 | tf_op jit(solution)/shard_map/ppermute | solution.py:23
  11.2 13.7 %collective-permute-start.1 = (f32[2,6,32,256]{3,2,1,0:T(8,128)S(1)}, f32[2,6,32,256]{3,2,1,0:T(8,128)S(1)}, u32[]{:S(2)}, u32[]{:S(2)}) collective-permute-start(f32[2,6,32,256]{3,2,1,0:T(8,128)S(1)} %get-tuple-element.59), channel_id=1, source_target_pairs={{32,0},{64,32},{96,64},{128,96},{160,128},{192,160},{224,192},{33,... | collective-permute-start | bytes 1179656 | tf_op jit(solution)/shard_map/ppermute | solution.py:25
  24.8 4.5 %copy-start.4 = (f32[2,6,32,256]{3,2,1,0:T(8,128)}, f32[2,6,32,256]{3,2,1,0:T(8,128)S(1)}, u32[]{:S(2)}) copy-start(f32[2,6,32,256]{3,2,1,0:T(8,128)S(1)} %collective-permute-done.1) | copy-start | bytes 1179652
  26.2 11.0 %collective-permute-start.2 = (f32[2,44,6,256]{3,0,2,1:T(2,128)}, f32[2,44,6,256]{3,0,2,1:T(2,128)}, u32[]{:S(2)}, u32[]{:S(2)}) collective-permute-start(f32[2,44,6,256]{3,0,2,1:T(2,128)} %copy.42), channel_id=1, source_target_pairs={{0,8},{8,16},{16,24},{1,9},{9,17},{17,25},{2,10},{10,18},{18,26},{... | collective-permute-start | bytes 1622024 | tf_op jit(solution)/shard_map/ppermute | solution.py:23
  29.3 10.8 %collective-permute-start.3 = (f32[2,44,6,256]{3,0,2,1:T(2,128)}, f32[2,44,6,256]{3,0,2,1:T(2,128)}, u32[]{:S(2)}, u32[]{:S(2)}) collective-permute-start(f32[2,44,6,256]{3,0,2,1:T(2,128)} %copy.43), channel_id=1, source_target_pairs={{8,0},{16,8},{24,16},{9,1},{17,9},{25,17},{10,2},{18,10},{26,18},{... | collective-permute-start | bytes 1622024 | tf_op jit(solution)/shard_map/ppermute | solution.py:25
  38.3 3.0 %copy-start.2 = (f32[2,44,6,256]{3,2,1,0:T(8,128)}, f32[2,44,6,256]{3,2,1,0:T(8,128)S(1)}, u32[]{:S(2)}) copy-start(f32[2,44,6,256]{3,2,1,0:T(8,128)S(1)} %copy.44) | copy-start | bytes 1622020
  41.3 0.9 copy-start.3
  49.4 13.0 %collective-permute-start.4 = (f32[2,44,44,6]{2,0,3,1:T(2,128)}, f32[2,44,44,6]{2,0,3,1:T(2,128)}, u32[]{:S(2)}, u32[]{:S(2)}) collective-permute-start(f32[2,44,44,6]{2,0,3,1:T(2,128)} %copy.46), channel_id=1, source_target_pairs={{0,1},{1,2},{2,3},{3,4},{4,5},{5,6},{6,7},{8,9},{9,10},{10,11},{11... | collective-permute-start | bytes 278792 | tf_op jit(solution)/shard_map/ppermute | solution.py:23
  55.6 10.3 %collective-permute-start.5 = (f32[2,44,44,6]{2,0,3,1:T(2,128)}, f32[2,44,44,6]{2,0,3,1:T(2,128)}, u32[]{:S(2)}, u32[]{:S(2)}) collective-permute-start(f32[2,44,44,6]{2,0,3,1:T(2,128)} %copy.47), channel_id=1, source_target_pairs={{1,0},{2,1},{3,2},{4,3},{5,4},{6,5},{7,6},{9,8},{10,9},{11,10},{12... | collective-permute-start | bytes 278792 | tf_op jit(solution)/shard_map/ppermute | solution.py:25
  89.9 1.9 %copy-start = (f32[3,32,32,256]{3,2,1,0:T(8,128)S(1)}, f32[3,32,32,256]{3,2,1,0:T(8,128)}, u32[]{:S(2)}) copy-start(f32[3,32,32,256]{3,2,1,0:T(8,128)} %param.11) | copy-start | bytes 9437188
  89.9 2.2 %copy-start.6 = (f32[32,32,256]{2,1,0:T(8,128)S(1)}, f32[32,32,256]{2,1,0:T(8,128)}, u32[]{:S(2)}) copy-start(f32[32,32,256]{2,1,0:T(8,128)} %param.14) | copy-start | bytes 3145732
  89.9 2.2 %copy-start.7 = (f32[256]{0:T(256)S(1)}, f32[256]{0:T(256)}, u32[]{:S(2)}) copy-start(f32[256]{0:T(256)} %fusion.61) | copy-start | bytes 3076
  97.1 6.1 %collective-permute-start.6 = (f32[33,257]{1,0:T(8,128)S(1)}, f32[33,257]{1,0:T(8,128)S(1)}, u32[]{:S(2)}, u32[]{:S(2)}) collective-permute-start(f32[33,257]{1,0:T(8,128)S(1)} %slice_bitcast_fusion.2), channel_id=1, source_target_pairs={{0,32},{32,64},{64,96},{96,128},{128,160},{160,192},{192,224},{1,3... | collective-permute-start | bytes 101780 | tf_op jit(solution)/shard_map/ppermute | solution.py:35
  103.3 5.4 %collective-permute-start.7 = (f32[32,257]{1,0:T(8,128)S(1)}, f32[32,257]{1,0:T(8,128)S(1)}, u32[]{:S(2)}, u32[]{:S(2)}) collective-permute-start(f32[32,257]{1,0:T(8,128)S(1)} %bitcast.58), channel_id=1, source_target_pairs={{0,8},{8,16},{16,24},{1,9},{9,17},{17,25},{2,10},{10,18},{18,26},{... | collective-permute-start | bytes 98696 | tf_op jit(solution)/shard_map/ppermute | solution.py:35
  111.0 9.7 %collective-permute-start.8 = (f32[32,32]{1,0:T(8,128)S(1)}, f32[32,32]{1,0:T(8,128)S(1)}, u32[]{:S(2)}, u32[]{:S(2)}) collective-permute-start(f32[32,32]{1,0:T(8,128)S(1)} %slice_reduce_fusion), channel_id=1, source_target_pairs={{0,1},{1,2},{2,3},{3,4},{4,5},{5,6},{6,7},{8,9},{9,10},{10,11},{11... | collective-permute-start | bytes 12296 | tf_op jit(solution)/shard_map/ppermute | solution.py:35
where the time goes:
time: 124 us; the launch traced here: 123 us
  waiting for transfers between devices  32.3 us (26%)
  starting transfers between devices  27.9 us (22%)
  local copies, waits for them, and re-layouts  27.7 us (22%)
  matrix products  21.2 us (17%)
  other arithmetic  13.1 us (11%)
    dot_general x1, matrix products, along_third(): jnp.einsum('fxyj,ji->fxyi', field, band_matrix(field.shape[3] - 2 * REACH...  14.7 us
    ppermute x3, waiting for transfers between devices, shifted(): return lax.ppermute(block, axis, route)  14.1 us
    ppermute x3, starting transfers between devices, padded_2(): lax.ppermute(head, axis, [((i + 1) % count, i) for i in range(ends)])  11.8 us
    ppermute x3, waiting for transfers between devices, padded_2(): lax.ppermute(tail, axis, [(i, (i + 1) % count) for i in range(ends)])  10.5 us
    ppermute x3, starting transfers between devices, padded_2(): lax.ppermute(tail, axis, [(i, (i + 1) % count) for i in range(ends)])  10.3 us
    ppermute x3, waiting for transfers between devices, padded_2(): lax.ppermute(head, axis, [((i + 1) % count, i) for i in range(ends)])  7.77 us
    slice x3, local copies, waits for them, and re-layouts, padded_2(): lax.slice_in_dim(cells, cells.shape[dim] - width, cells.shape[dim], axis=...  6.71 us
    ppermute x3, starting transfers between devices, shifted(): return lax.ppermute(block, axis, route)  5.76 us
  transfers between devices with their start and end apart: 9, of which 8 were waited for; matrix products, arithmetic and copies ran while one was open for 8% of the time, Pallas kernels for 0%

commit v1 on v0

v1 whole, which is shorter than its diff:
```python
import functools
import math

import jax
import jax.numpy as jnp
import numpy as np
from jax import lax
from jax.experimental import pallas as pl
from jax.experimental.pallas import tpu as pltpu
from jax.sharding import PartitionSpec as P

REACH = 6
RM_ITERS = 2
LENGTH_SCALE = 3.0
HIGHEST = lax.Precision.HIGHEST
F32 = jnp.float32
VMEM_LIMIT = 40 * 1024 * 1024
INTERPRET = False


def gauss(offset):
    return math.exp(-offset * offset / (2.0 * LENGTH_SCALE * LENGTH_SCALE))


def band(offset):
    return gauss(offset) if abs(offset) <= REACH else 0.0


def z_band(width):
    return np.array([[band(i - k) for k in range(width)] for i in range(width)], np.float32)


def z_low_rows():
    out = np.zeros((240, 128), np.float32)
    for c in range(7):
        for k in range(128):
            out[112 + c, k] = band(k - (c - 7))
    return out


def z_high_rows():
    out = np.zeros((240, 128), np.float32)
    for c in range(6):
        for k in range(128):
            out[112 + c, k] = band(128 + c - k)
    return out


def plane_from_low():
    out = np.zeros((40, 128), np.float32)
    for g in range(8):
        for c in range(7):
            out[g, 16 * g + c] = band(c - 6)
        for e in range(4):
            out[8 * (1 + e) + g, 16 * g + 7 + e] = 1.0
    return out


def plane_from_own():
    out = np.zeros((40, 128), np.float32)
    for g in range(8):
        for c in range(6):
            out[g, 16 * g + c] = band(c + 1)
    return out


def rows_matrix():
    out = np.zeros((40, 48), np.float32)
    for r in range(33):
        at = r if r < 32 else -1
        for k in range(1, 46):
            out[r, k] = band(k - 8 - at)
    return out


def plane_y_matrices():
    own = np.zeros((256, 256), np.float32)
    low = np.zeros((256, 256), np.float32)
    high = np.zeros((256, 256), np.float32)
    for y in range(-1, 32):
        for l in range(32):
            own[l, y + 1] = band(l - y)
            low[l, y + 1] = band(l - 32 - y) if l >= 25 else 0.0
            high[l, y + 1] = band(32 + l - y) if l < 6 else 0.0
    for c in range(1, 5):
        for y in range(32):
            own[32 * c + y, 40 * c + y + 1] = 1.0
        low[32 * c + 31, 40 * c] = 1.0
    return own, low, high


def lanes(shape):
    return lax.broadcasted_iota(jnp.int32, shape, len(shape) - 1)


def rows(shape):
    return lax.broadcasted_iota(jnp.int32, shape, len(shape) - 2)


def inverse_total(position, extent):
    total = jnp.zeros(position.shape, F32)
    for offset in range(-REACH, REACH + 1):
        inside = (position + offset >= 0) & (position + offset < extent)
        total = total + jnp.where(inside, F32(gauss(offset)), F32(0.0))
    return 1.0 / total


def newton_plastic(trial, alpha_old):
    increment = jnp.zeros(trial.shape, F32)
    for _ in range(RM_ITERS):
        hardened = alpha_old + increment
        soft = 0.5 * jnp.exp(-5.0 * hardened)
        excess = trial - increment - (1.0 + 0.5 * hardened - soft)
        increment = jnp.maximum(increment + excess / (1.5 + 5.0 * soft), 0.0)
    return increment


def integrity_of(kappa):
    return jnp.exp(-jnp.maximum(kappa - 3.2, 0.0) / 3.0)


def by_parity(even, first, second, use):
    @pl.when(even)
    def _():
        use(first, second)

    @pl.when(jnp.logical_not(even))
    def _():
        use(second, first)


CHUNK = 8


def local_kernel(
    where_ref, strain, plastic, alpha, kappa, flags,
    field, free, yext, xext, z_a, z_b, flags_t, up, low,
):
    step = pl.program_id(0)

    @pl.when(step == 0)
    def _():
        eye = (rows((32, 32)) == lanes((32, 32))).astype(F32)
        flags_t[...] = lax.dot_general(
            eye, flags[...].astype(F32), (((1,), (1,)), ((), ())), preferred_element_type=F32
        )
        up[...] = jnp.zeros_like(up)
        low[...] = jnp.zeros_like(low)

    lane = lanes((128, 128))
    for half in range(CHUNK // 4):
        for i in range(4):
            x = half * 4 + i
            here = (rows((32, 256)) == step * CHUNK + x).astype(F32)
            flag = jnp.dot(flags_t[...], here, preferred_element_type=F32)
            s0, s1, s2 = strain[0, x], strain[1, x], strain[2, x]
            trial = s0 - plastic[x]
            increment = newton_plastic(trial, alpha[x]) * flag
            field[x] = s0 * s0 + s1 * s1 + s2 * s2 + 4.0 * increment
            free[x] = trial - increment
        g = step * (CHUNK // 4) + half
        part = pl.ds(half * 4, 4)

        def high_half(ref):
            return ref[part, :, 128:256].reshape(128, 128)

        packed = jnp.where(lane < 7, pltpu.roll(high_half(field), 7, 1), 0.0)
        extras = (free, strain.at[1], strain.at[2], kappa)
        for e, ref in enumerate(extras):
            packed = jnp.where(lane == 7 + e, pltpu.roll(high_half(ref), 8 + e, 1), packed)
        up[...] += pltpu.roll(packed, 16 * g, 1)
        first = jnp.where(lane < 6, field[part, :, 0:128].reshape(128, 128), 0.0)
        low[...] += pltpu.roll(first, 16 * g, 1)
    for x in range(CHUNK):
        for e, ref in enumerate((free, strain.at[1], strain.at[2], kappa)):
            yext[e, pl.ds(x, 1), :] = ref[x, 31:32, :]

    @pl.when(step == pl.num_programs(0) - 1)
    def _():
        for e, ref in enumerate((free, strain.at[1], strain.at[2], kappa)):
            xext[e] = ref[CHUNK - 1]

        def store(upper, lower):
            upper[...] = up[...]
            lower[...] = low[...]

        by_parity(lax.rem(where_ref[2], 2) == 0, z_a, z_b, store)


def z_kernel(
    where_ref, field, yext, sent_a, sent_b, got_a, got_b, bz, t_low, t_high, w_low, w_own,
    smooth, plane, y_a, y_b, z_low, z_high, own_low, head_rows, tail_rows,
):
    def choose(upper, lower):
        z_high[...] = upper[0][...]
        z_low[...] = lower[0][...]
        own_low[...] = lower[1][...]

    by_parity(lax.rem(where_ref[2], 2) == 0, (got_a, sent_a), (got_b, sent_b), choose)
    for g in range(8):
        part = field[4 * g : 4 * g + 4].reshape(128, 256)
        main = jnp.dot(part, bz[...], precision=HIGHEST, preferred_element_type=F32)
        start = 112 - 16 * g
        first = jnp.dot(
            z_low[...], t_low[start : start + 128], precision=HIGHEST, preferred_element_type=F32
        )
        last = jnp.dot(
            z_high[...], t_high[start : start + 128], precision=HIGHEST, preferred_element_type=F32
        )
        smooth[4 * g : 4 * g + 4, :, 0:128] = (main[:, 0:128] + first).reshape(4, 32, 128)
        smooth[4 * g : 4 * g + 4, :, 128:256] = (main[:, 128:256] + last).reshape(4, 32, 128)
    contract = (((1,), (1,)), ((), ()))
    turned = lax.dot_general(
        w_low[...], z_low[...], contract, precision=HIGHEST, preferred_element_type=F32
    ) + lax.dot_general(
        w_own[...], own_low[...], contract, precision=HIGHEST, preferred_element_type=F32
    )
    lane = lanes((8, 128))
    for b in range(4):
        head = jnp.zeros((8, 128), F32)
        for c in range(4):
            moved = pltpu.roll(turned[8 * c : 8 * c + 8], (32 * (c - b)) % 128, 1)
            head = jnp.where(lane // 32 == c, moved, head)
        tail = jnp.where(lane < 32, pltpu.roll(turned[32:40], (-32 * b) % 128, 1), 0.0)
        head_rows[pl.ds(b, 8, stride=4), :] = head
        tail_rows[pl.ds(b, 8, stride=4), :] = tail
    plane[:, 0:128] = head_rows[...]
    plane[:, 128:256] = tail_rows[...]

    def store(upper, lower):
        for j in range(7):
            upper[j] = smooth[:, 25 + j, :]
        for e in range(4):
            upper[7 + e] = yext[e]
        upper[11] = plane[...]
        for j in range(6):
            lower[j] = smooth[:, j, :]
        lower[11] = plane[...]

    by_parity(lax.rem(where_ref[1], 2) == 0, y_a, y_b, store)


def y_kernel(
    where_ref, smooth, plane, xext, got_a, got_b, my, v_own, v_low, v_high,
    out, out_face, out_plane, face_ext, x_a, x_b, ext, plane_low, plane_high,
):
    for x in range(32):
        ext[x, 8:40, :] = smooth[x]
        ext[x, 0:8, :] = jnp.zeros((8, 256), F32)
        ext[x, 40:48, :] = jnp.zeros((8, 256), F32)

    def choose(upper, lower):
        for j in range(7):
            ext[:, 1 + j, :] = lower[j]
        for j in range(6):
            ext[:, 40 + j, :] = upper[j]
        for e in range(4):
            face_ext[e] = lower[7 + e]
        plane_low[...] = lower[11]
        plane_high[...] = upper[11]

    by_parity(lax.rem(where_ref[1], 2) == 0, got_a, got_b, choose)
    for x in range(32):
        both = jnp.dot(my[...], ext[x], precision=HIGHEST, preferred_element_type=F32)
        out[x] = both[0:32]
        out_face[x : x + 1, :] = both[32:33]
    total = jnp.dot(plane[...], v_own[...], precision=HIGHEST, preferred_element_type=F32)
    total += jnp.dot(plane_low[...], v_low[...], precision=HIGHEST, preferred_element_type=F32)
    total += jnp.dot(plane_high[...], v_high[...], precision=HIGHEST, preferred_element_type=F32)
    out_plane[...] = total

    def store(upper, lower):
        for j in range(7):
            upper[j] = out[25 + j]
        for e in range(4):
            upper[7 + e] = xext[e]
        upper[11] = jnp.zeros((32, 256), F32)
        upper[11, 0:8, :] = out_face[24:32, :]
        for e in range(4):
            upper[11, 8 + e : 9 + e, :] = face_ext[e, 31:32, :]
        upper[11, 16:24, :] = out_plane[24:32, :]
        for j in range(6):
            lower[j] = out[j]
        lower[11] = jnp.zeros((32, 256), F32)
        lower[11, 0:8, :] = out_face[0:8, :]
        lower[11, 16:24, :] = out_plane[0:8, :]

    by_parity(lax.rem(where_ref[0], 2) == 0, x_a, x_b, store)


def final_kernel(
    extents, where_ref, strain, free, kappa, smooth, face, plane, face_ext, got_a, got_b, mx,
    force, kappa_new,
    ext, face_all, plane_all, side, before, face_e, face_a, column, inv_x, inv_yz,
):
    step = pl.program_id(0)
    nx, ny, nz = extents
    ix, iy, iz = where_ref[0], where_ref[1], where_ref[2]

    def layer(at):
        total = gauss(0) * ext[at + 7]
        for a in range(1, REACH + 1):
            total = total + gauss(a) * (ext[at + 7 - a] + ext[at + 7 + a])
        return total

    @pl.when(step == 0)
    def _():
        def choose(upper, lower):
            for j in range(7):
                ext[j] = lower[j]
            for j in range(6):
                ext[39 + j] = upper[j]
            face_all[0:8, :] = lower[11, 0:8, :]
            face_all[40:48, :] = upper[11, 0:8, :]
            plane_all[0:8, :] = lower[11, 16:24, :]
            plane_all[40:48, :] = upper[11, 16:24, :]
            for e in range(4):
                side[e, 32:33, :] = lower[11, 8 + e : 9 + e, :]
                before[e] = lower[7 + e]

        for e in range(4):
            side[e, 0:32, :] = face_ext[e]
            side[e, 32:40, :] = jnp.zeros((8, 256), F32)
        by_parity(lax.rem(ix, 2) == 0, got_a, got_b, choose)
        for x in range(32):
            ext[7 + x] = smooth[x]
        face_all[8:40, :] = face[...]
        plane_all[8:40, :] = plane[...]

        shape = (40, 256)
        r = rows(shape)
        invx = inverse_total(ix * 32 + jnp.where(r < 32, r, -1), nx)
        inv_x[...] = invx
        small = (32, 256)
        invz = inverse_total(iz * 256 + lanes(small), nz)
        inv_yz[...] = inverse_total(iy * 32 + rows(small), ny) * invz

        at_y = inverse_total(jnp.full((1, 256), iy * 32 - 1, jnp.int32), ny)
        avg = jnp.dot(mx[...], face_all[...], precision=HIGHEST, preferred_element_type=F32)
        kap = jnp.maximum(side[3], avg * (invx * (at_y * invz[0:1, :])))
        integ = integrity_of(kap)
        row = rows(shape)

        def previous(value):
            return jnp.where(row == 0, value[32:33, :], pltpu.roll(value, 1, 0))

        t0, t1, t2 = integ * side[0], integ * side[1], integ * side[2]
        a0 = previous(t0) - t0
        a1 = previous(t1) + t1
        a2 = previous(t2) + t2
        face_e[...] = (a0 + a1)[0:32]
        face_a[...] = a2[0:32]

        avg = jnp.dot(mx[...], plane_all[...], precision=HIGHEST, preferred_element_type=F32)
        own = plane_all[8:48, :]
        own = jnp.where(row == 32, plane_all[7:8, :], own)

        def value(c):
            return pltpu.roll(own, (256 - 40 * c) % 256, 1)

        lane = lanes(shape)
        at_z = inverse_total(jnp.full((1, 256), iz * 256 - 1, jnp.int32), nz)
        invy = inverse_total(iy * 32 - 1 + jnp.minimum(lane, 32), ny)
        kap = jnp.maximum(value(4), avg * (invx * (invy * at_z)))
        integ = integrity_of(kap)
        t0, t1, t2 = integ * value(1), integ * value(2), integ * value(3)
        a0 = previous(t0) - t0
        a1 = previous(t1) + t1
        a2 = previous(t2) + t2
        e, f = a0 + a1, a0 - a1
        parts = e + a2 + pltpu.roll(f + a2, 255, 1)
        parts = jnp.where(lane < 32, parts, 0.0)
        eye = (rows((32, 128)) == lanes((32, 128))).astype(F32)
        pad = jnp.concatenate([parts[0:32, 0:128], jnp.zeros((96, 128), F32)], axis=0)
        column[...] = lax.dot_general(
            eye, pad, (((1,), (1,)), ((), ())), precision=HIGHEST, preferred_element_type=F32
        )

        kap = jnp.maximum(before[3], layer(-1) * (inv_x[32:33, :] * inv_yz[...]))
        integ = integrity_of(kap)
        for e in range(3):
            before[e] = integ * before[e]

    first_row = rows((32, 256)) == 0
    first_lane = lanes((32, 128)) == 0

    @pl.loop(0, CHUNK)
    def _(i):
        x = step * CHUNK + i
        kap = jnp.maximum(kappa[i], layer(x) * (inv_x[pl.ds(x, 1), :] * inv_yz[...]))
        kappa_new[i] = kap
        integ = integrity_of(kap)
        s0, s1, s2 = integ * free[i], integ * strain[1, i], integ * strain[2, i]
        a0 = before[0] - s0
        a1 = before[1] + s1
        a2 = before[2] + s2
        before[0] = s0
        before[1] = s1
        before[2] = s2
        e, f = a0 + a1, a0 - a1
        b = f + jnp.where(first_row, face_e[pl.ds(x, 1), :], pltpu.roll(e, 1, 0))
        c = a2 + jnp.where(first_row, face_a[pl.ds(x, 1), :], pltpu.roll(a2, 1, 0))
        p, q = b + c, b - c
        moved = pltpu.roll(p, 1, 1)
        edge = pltpu.roll(column[...], lax.rem(128 - x, 128), 1)
        force[i, :, 0:128] = 0.25 * (q[:, 0:128] + jnp.where(first_lane, edge, moved[:, 0:128]))
        force[i, :, 128:256] = 0.25 * (q[:, 128:256] + moved[:, 128:256])


def swap(first, second, axis):
    count = lax.axis_size(axis)

    def route(start):
        out = []
        for i in range(start, count - 1, 2):
            out += [(i, i + 1), (i + 1, i)]
        return out

    return lax.ppermute(first, axis, route(0)), lax.ppermute(second, axis, route(1))


def shape_of(*dims):
    return jax.ShapeDtypeStruct(dims, F32)


VM = pl.BlockSpec(memory_space=pltpu.VMEM)
SM = pl.BlockSpec(memory_space=pltpu.SMEM)


def call(kernel, name, **kwargs):
    return pl.pallas_call(
        kernel,
        name=name,
        interpret=INTERPRET,
        compiler_params=pltpu.CompilerParams(vmem_limit_bytes=VMEM_LIMIT),
        **kwargs,
    )


def body(strain, plastic_old, alpha_old, kappa_old, flags):
    where = jnp.stack([lax.axis_index(a) for a in ("gx", "gy", "gz")]).astype(jnp.int32)
    cells = pl.BlockSpec((CHUNK, 32, 256), lambda s: (s, 0, 0))
    three = pl.BlockSpec((3, CHUNK, 32, 256), lambda s: (0, s, 0, 0))

    def whole(*dims):
        return pl.BlockSpec(dims, lambda s: (0,) * len(dims))

    field, free, yext, xext, z_a, z_b = call(
        local_kernel,
        "local",
        grid=(32 // CHUNK,),
        in_specs=[SM, three, cells, cells, cells, whole(32, 32)],
        out_specs=[
            cells, cells, pl.BlockSpec((4, CHUNK, 256), lambda s: (0, s, 0)),
            whole(4, 32, 256), whole(128, 128), whole(128, 128),
        ],
        out_shape=[
            shape_of(32, 32, 256), shape_of(32, 32, 256), shape_of(4, 32, 256),
            shape_of(4, 32, 256), shape_of(128, 128), shape_of(128, 128),
        ],
        scratch_shapes=[
            pltpu.VMEM((32, 32), F32), pltpu.VMEM((128, 128), F32), pltpu.VMEM((128, 128), F32),
        ],
    )(where, strain, plastic_old, alpha_old, kappa_old, flags.reshape(32, 32))
    got_a, got_b = swap(z_a, z_b, "gz")

    smooth, plane, y_a, y_b = call(
        z_kernel,
        "along_z",
        in_specs=[SM] + [VM] * 11,
        out_specs=[VM] * 4,
        out_shape=[
            shape_of(32, 32, 256), shape_of(32, 256), shape_of(12, 32, 256), shape_of(12, 32, 256),
        ],
        scratch_shapes=[pltpu.VMEM((128, 128), F32)] * 3 + [pltpu.VMEM((32, 128), F32)] * 2,
    )(
        where, field, yext, z_a, z_b, got_a, got_b,
        z_band(256), z_low_rows(), z_high_rows(), plane_from_low(), plane_from_own(),
    )
    got_a, got_b = swap(y_a, y_b, "gy")

    smooth, face, plane, face_ext, x_a, x_b = call(
        y_kernel,
        "along_y",
        in_specs=[SM] + [VM] * 9,
        out_specs=[VM] * 6,
        out_shape=[
            shape_of(32, 32, 256), shape_of(32, 256), shape_of(32, 256), shape_of(4, 32, 256),
            shape_of(12, 32, 256), shape_of(12, 32, 256),
        ],
        scratch_shapes=[
            pltpu.VMEM((32, 48, 256), F32), pltpu.VMEM((32, 256), F32), pltpu.VMEM((32, 256), F32),
        ],
    )(where, smooth, plane, xext, got_a, got_b, rows_matrix(), *plane_y_matrices())
    got_a, got_b = swap(x_a, x_b, "gx")

    extents = (
        32 * lax.axis_size("gx"), 32 * lax.axis_size("gy"), 256 * lax.axis_size("gz"),
    )
    force, kappa_new = call(
        functools.partial(final_kernel, extents),
        "along_x",
        grid=(32 // CHUNK,),
        in_specs=[
            SM, three, cells, cells, whole(32, 32, 256), whole(32, 256), whole(32, 256),
            whole(4, 32, 256), whole(12, 32, 256), whole(12, 32, 256), whole(40, 48),
        ],
        out_specs=[cells, cells],
        out_shape=[shape_of(32, 32, 256), shape_of(32, 32, 256)],
        scratch_shapes=[
            pltpu.VMEM((45, 32, 256), F32), pltpu.VMEM((48, 256), F32), pltpu.VMEM((48, 256), F32),
            pltpu.VMEM((4, 40, 256), F32), pltpu.VMEM((4, 32, 256), F32),
            pltpu.VMEM((32, 256), F32), pltpu.VMEM((32, 256), F32), pltpu.VMEM((32, 128), F32),
            pltpu.VMEM((40, 256), F32), pltpu.VMEM((32, 256), F32),
        ],
    )(where, strain, free, kappa_old, smooth, face, plane, face_ext, got_a, got_b, rows_matrix())
    return (force, kappa_new)


def solution(mesh):
    in_specs = (
        P(None, "gx", "gy", "gz"),
        P("gx", "gy", "gz"),
        P("gx", "gy", "gz"),
        P("gx", "gy", "gz"),
        P("gx", "gy", "gz"),
    )
    out_specs = (P("gx", "gy", "gz"), P("gx", "gy", "gz"))
    return jax.shard_map(body, mesh=mesh, in_specs=in_specs, out_specs=out_specs, check_vma=False)
```

time: 124 us -> 55.7 us (0.45)
  local copies, waits for them, and re-layouts: 27.7 us -> 6.34 us
  matrix products: 21.2 us -> 0 us
  Pallas kernels: 0 us -> 15.7 us
  waiting for transfers between devices: 32.3 us -> 17 us
  other arithmetic: 13.1 us -> 0.08 us
  starting transfers between devices: 27.9 us -> 15.3 us
    dot_general x3 -> x0, matrix products: 21.2 us -> none  [the longest x1 14.7 us: along_third(): jnp.einsum('fxyj,ji->fxyi', field, band_matrix(field.shape[3] - 2 * REACH...]
    pallas_call x0 -> x4, Pallas kernels: none -> 15.7 us  [the longest x1 6.66 us: body(): call(functools.partial(final_kernel, extents), 'along_x', grid=(32 // CHU...]
    ppermute x9 -> x6, waiting for transfers between devices: 32.3 us -> 17 us  [the longest x3 15.3 us: swap(): lax.ppermute(second, axis, route(1))]
    ppermute x9 -> x6, starting transfers between devices: 27.9 us -> 15.3 us  [the longest x3 13.5 us: swap(): lax.ppermute(second, axis, route(1))]
    slice x10 -> x0, local copies, waits for them, and re-layouts: 12.3 us -> none  [the longest x3 6.71 us: padded_2(): lax.slice_in_dim(cells, cells.shape[dim] - width, cells.shape[dim], axis=...]
    ppermute x4 -> x0, local copies, waits for them, and re-layouts: 7.98 us -> none  [the longest x2 3.99 us: padded_2(): lax.ppermute(head, axis, [((i + 1) % count, i) for i in range(ends)])]
    mul x4 -> x0, other arithmetic: 5.29 us -> none  [the longest x2 2.91 us: assemble(): 0.25 * ((2 * side_x - 1) * first + (2 * side_y - 1) * second + (2 * side_...]
    add x6 -> x0, other arithmetic: 4.99 us -> none  [the longest x1 2.18 us: body(): strain[0] * strain[0] + strain[1] * strain[1] + strain[2] * strain[2]]
  transfers between devices with their start and end apart: 9 -> 6, of which waited for: 8 -> 4; matrix products, arithmetic and copies ran while one was open for 8% -> 0% of each run, Pallas kernels for 0% -> 0%
where the time goes in v1:
time: 55.7 us; the launch traced here: 55.3 us
  waiting for transfers between devices  17 us (31%)
  Pallas kernels  15.7 us (28%)
  starting transfers between devices  15.3 us (27%)
  local copies, waits for them, and re-layouts  6.34 us (11%)
  between operations  0.81 us (1%)
    ppermute x3, waiting for transfers between devices, swap(): lax.ppermute(second, axis, route(1))  15.3 us
    ppermute x3, starting transfers between devices, swap(): lax.ppermute(second, axis, route(1))  13.5 us
    pallas_call x1, Pallas kernels, body(): call(functools.partial(final_kernel, extents), 'along_x', grid=(32 // CHU...  6.66 us
    unnamed x32, local copies, waits for them, and re-layouts  6.34 us
    pallas_call x1, Pallas kernels, body(): call(local_kernel, 'local', grid=(32 // CHUNK,), in_specs=[SM, three, cel...  3.4 us
    pallas_call x1, Pallas kernels, body(): call(z_kernel, 'along_z', in_specs=[SM] + [VM] * 11, out_specs=[VM] * 4,...  3.13 us
    pallas_call x1, Pallas kernels, body(): call(y_kernel, 'along_y', in_specs=[SM] + [VM] * 9, out_specs=[VM] * 6, o...  2.46 us
    ppermute x3, starting transfers between devices, swap(): lax.ppermute(first, axis, route(0))  1.84 us
  transfers between devices with their start and end apart: 6, of which 4 were waited for; matrix products, arithmetic and copies ran while one was open for 0% of the time, Pallas kernels for 0%

profile of v1, /device:TPU:120, one launch (start us, length us, event | category | flops | bytes accessed | tf_op | source)
XLA Modules:
  0.0 55.3 jit_solution(15582593315824113100)
XLA Ops:
  0.6 0.1 pad_add_fusion.where_ref
  0.7 0.0 copy-start
  0.7 1.9 %copy-done = f32[3,32,32,256]{3,2,1,0:T(8,128)S(1)} copy-done((f32[3,32,32,256]{3,2,1,0:T(8,128)S(1)}, f32[3,32,32,256]{3,2,1,0:T(8,128)}, u32[]{:S(2)}) %copy-start) | copy-done | bytes 3145752
  2.6 0.0 copy-start.2
  2.6 1.2 %copy-done.2 = f32[32,32,256]{2,1,0:T(8,128)S(1)} copy-done((f32[32,32,256]{2,1,0:T(8,128)S(1)}, f32[32,32,256]{2,1,0:T(8,128)}, u32[]{:S(2)}) %copy-start.2) | copy-done | bytes 1048600
  3.8 0.0 copy-start.4
  3.8 1.2 %copy-done.4 = f32[32,32,256]{2,1,0:T(8,128)S(1)} copy-done((f32[32,32,256]{2,1,0:T(8,128)S(1)}, f32[32,32,256]{2,1,0:T(8,128)}, u32[]{:S(2)}) %copy-start.4) | copy-done | bytes 1048600
  5.1 0.0 copy-start.5
  5.1 1.2 %copy-done.5 = f32[32,32,256]{2,1,0:T(8,128)S(1)} copy-done((f32[32,32,256]{2,1,0:T(8,128)S(1)}, f32[32,32,256]{2,1,0:T(8,128)}, u32[]{:S(2)}) %copy-start.5) | copy-done | bytes 1048600
  6.3 0.0 copy-start.15
  6.3 0.7 %copy-done.15 = s32[32,32,1]{1,2,0:T(1,128)S(1)} copy-done((s32[32,32,1]{1,2,0:T(1,128)S(1)}, s32[32,32,1]{1,2,0:T(1,128)}, u32[]{:S(2)}) %copy-start.15) | copy-done | bytes 4120
  7.0 0.0 copy-start.9
  7.0 0.0 copy-start.10
  7.0 0.0 copy-start.11
  7.0 0.0 copy-start.13
  7.0 0.0 copy-start.14
  7.0 0.0 copy-start.6
  7.0 0.0 copy-start.7
  7.0 0.0 copy-start.8
  7.1 0.0 copy-start.12
  7.1 3.4 %local.1 = (f32[32,32,256]{2,1,0:T(8,128)S(1)}, f32[32,32,256]{2,1,0:T(8,128)S(1)}, f32[4,32,256]{2,1,0:T(8,128)S(1)}, f32[4,32,256]{2,1,0:T(8,128)S(1)}, f32[12...) custom-call(s32[3]{0:T(128)S(1)} %pad_add_fusion.where_ref, f32[3,32,32,256]{3,2,1,0:T(8,128)S(1)} %copy-done, ...), custom_call_target="tpu_custom_call" | custom-call | tf_op jit(solution)/shard_map/local/pallas_call | solution.py:448
  10.5 0.0 copy-start.1
  10.5 0.0 copy-start.3
  10.5 1.6 %collective-permute-start = (f32[128,128]{1,0:T(8,128)S(1)}, f32[128,128]{1,0:T(8,128)S(1)}, u32[]{:S(2)}, u32[]{:S(2)}) collective-permute-start(f32[128,128]{1,0:T(8,128)S(1)} %get-tuple-element.21.sent_a), channel_id=1, source_target_pairs={{0,1},{1,0},{2,3},{3,2},{4,5},{5,4},{6,7},{7,6},{8,9},{9,8},{10,11... | collective-permute-start | bytes 196616 | tf_op jit(solution)/shard_map/ppermute | solution.py:419
  12.1 4.8 %collective-permute-start.1 = (f32[128,128]{1,0:T(8,128)S(1)}, f32[128,128]{1,0:T(8,128)S(1)}, u32[]{:S(2)}, u32[]{:S(2)}) collective-permute-start(f32[128,128]{1,0:T(8,128)S(1)} %get-tuple-element.22.sent_b), channel_id=1, source_target_pairs={{1,2},{2,1},{3,4},{4,3},{5,6},{6,5},{9,10},{10,9},{11,12},{12,11},... | collective-permute-start | bytes 196616 | tf_op jit(solution)/shard_map/ppermute | solution.py:419
  16.9 0.0 collective-permute-done.got_a
  16.9 4.9 %collective-permute-done.1.got_b = f32[128,128]{1,0:T(8,128)S(1)} collective-permute-done((f32[128,128]{1,0:T(8,128)S(1)}, f32[128,128]{1,0:T(8,128)S(1)}, u32[]{:S(2)}, u32[]{:S(2)}) %collective-permute-start.1) | collective-permute-done | bytes 65568 | tf_op jit(solution)/shard_map/ppermute | solution.py:419
  21.8 0.0 copy-done.9
  21.8 0.0 copy-done.10
  21.8 0.0 copy-done.11
  21.9 0.0 copy-done.13
  21.9 0.0 copy-done.14
  21.9 3.1 %along_z.1 = (f32[32,32,256]{2,1,0:T(8,128)S(1)}, f32[32,256]{1,0:T(8,128)S(1)}, f32[12,32,256]{2,1,0:T(8,128)S(1)}, f32[12,32,256]{2,1,0:T(8,128)S(1)}) custom-call(s32[3]{0:T(128)S(1)} %pad_add_fusion.where_ref, f32[32,32,256]{2,1,0:T(8,128)S(1)} %get-tuple-element.19.field, f32[4,32,256]{2,1,0:T(8,128)S(1)} %get-tuple-element.20.yext, ...), custom_call_target="tpu_custom_call" | custom-call | tf_op jit(solution)/shard_map/along_z/pallas_call | solution.py:467
  25.0 0.1 collective-permute-start.2
  25.1 2.7 %collective-permute-start.3 = (f32[12,32,256]{2,1,0:T(8,128)S(1)}, f32[12,32,256]{2,1,0:T(8,128)S(1)}, u32[]{:S(2)}, u32[]{:S(2)}) collective-permute-start(f32[12,32,256]{2,1,0:T(8,128)S(1)} %get-tuple-element.27), channel_id=1, source_target_pairs={{8,16},{16,8},{9,17},{17,9},{10,18},{18,10},{11,19},{19,11},{12,20... | collective-permute-start | bytes 1179656 | tf_op jit(solution)/shard_map/ppermute | solution.py:419
  27.9 0.0 collective-permute-done.2.got_a
  27.9 6.3 %collective-permute-done.3.got_b = f32[12,32,256]{2,1,0:T(8,128)S(1)} collective-permute-done((f32[12,32,256]{2,1,0:T(8,128)S(1)}, f32[12,32,256]{2,1,0:T(8,128)S(1)}, u32[]{:S(2)}, u32[]{:S(2)}) %collective-permute-start.3) | collective-permute-done | bytes 393248 | tf_op jit(solution)/shard_map/ppermute | solution.py:419
  34.2 0.0 copy-done.6
  34.2 0.0 copy-done.7
  34.2 0.0 copy-done.8
  34.2 0.0 copy-done.12
  34.2 2.5 %along_y.1 = (f32[32,32,256]{2,1,0:T(8,128)S(1)}, f32[32,256]{1,0:T(8,128)S(1)}, f32[32,256]{1,0:T(8,128)S(1)}, f32[4,32,256]{2,1,0:T(8,128)S(1)}, f32[12,32,256...) custom-call(s32[3]{0:T(128)S(1)} %pad_add_fusion.where_ref, f32[32,32,256]{2,1,0:T(8,128)S(1)} %get-tuple-element.23.smooth, ...), custom_call_target="tpu_custom_call" | custom-call | tf_op jit(solution)/shard_map/along_y/pallas_call | solution.py:482
  36.7 0.2 collective-permute-start.4
  36.9 6.0 %collective-permute-start.5 = (f32[12,32,256]{2,1,0:T(8,128)S(1)}, f32[12,32,256]{2,1,0:T(8,128)S(1)}, u32[]{:S(2)}, u32[]{:S(2)}) collective-permute-start(f32[12,32,256]{2,1,0:T(8,128)S(1)} %get-tuple-element.33), channel_id=1, source_target_pairs={{32,64},{64,32},{96,128},{128,96},{160,192},{192,160},{33,65},{65,... | collective-permute-start | bytes 1179656 | tf_op jit(solution)/shard_map/ppermute | solution.py:419
  42.8 1.7 %collective-permute-done.4.got_a = f32[12,32,256]{2,1,0:T(8,128)S(1)} collective-permute-done((f32[12,32,256]{2,1,0:T(8,128)S(1)}, f32[12,32,256]{2,1,0:T(8,128)S(1)}, u32[]{:S(2)}, u32[]{:S(2)}) %collective-permute-start.4) | collective-permute-done | bytes 393248 | tf_op jit(solution)/shard_map/ppermute | solution.py:419
  44.6 4.0 %collective-permute-done.5.got_b = f32[12,32,256]{2,1,0:T(8,128)S(1)} collective-permute-done((f32[12,32,256]{2,1,0:T(8,128)S(1)}, f32[12,32,256]{2,1,0:T(8,128)S(1)}, u32[]{:S(2)}, u32[]{:S(2)}) %collective-permute-start.5) | collective-permute-done | bytes 393248 | tf_op jit(solution)/shard_map/ppermute | solution.py:419
  48.6 0.0 copy-done.1
  48.6 0.0 copy-done.3
  48.6 6.7 %along_x.1 = (f32[32,32,256]{2,1,0:T(8,128)}, f32[32,32,256]{2,1,0:T(8,128)}) custom-call(s32[3]{0:T(128)S(1)} %pad_add_fusion.where_ref, f32[3,32,32,256]{3,2,1,0:T(8,128)S(1)} %copy-done.1, f32[32,32,256]{2,1,0:T(8,128)S(1)} %get-tuple-element.18.free, f32[32,32,256]{2,1,0:T(8,128)S(1)} %copy-done.3, f32[32,32,256]{2,1,0:T(8,128)S(1)} %get-tuple-element.28.smooth, ...), custom_call_target="tpu_custom_call" | custom-call | tf_op jit(solution)/shard_map/along_x/pallas_call | solution.py:500
Async XLA Ops:
  0.7 1.9 %copy-start = (f32[3,32,32,256]{3,2,1,0:T(8,128)S(1)}, f32[3,32,32,256]{3,2,1,0:T(8,128)}, u32[]{:S(2)}) copy-start(f32[3,32,32,256]{3,2,1,0:T(8,128)} %strain.3) | copy-start | bytes 9437188
  2.6 1.2 %copy-start.2 = (f32[32,32,256]{2,1,0:T(8,128)S(1)}, f32[32,32,256]{2,1,0:T(8,128)}, u32[]{:S(2)}) copy-start(f32[32,32,256]{2,1,0:T(8,128)} %kappa.3) | copy-start | bytes 3145732
  3.8 1.2 %copy-start.4 = (f32[32,32,256]{2,1,0:T(8,128)S(1)}, f32[32,32,256]{2,1,0:T(8,128)}, u32[]{:S(2)}) copy-start(f32[32,32,256]{2,1,0:T(8,128)} %plastic.1) | copy-start | bytes 3145732
  5.1 1.2 %copy-start.5 = (f32[32,32,256]{2,1,0:T(8,128)S(1)}, f32[32,32,256]{2,1,0:T(8,128)}, u32[]{:S(2)}) copy-start(f32[32,32,256]{2,1,0:T(8,128)} %alpha.1) | copy-start | bytes 3145732
  6.3 0.7 %copy-start.15 = (s32[32,32,1]{1,2,0:T(1,128)S(1)}, s32[32,32,1]{1,2,0:T(1,128)}, u32[]{:S(2)}) copy-start(s32[32,32,1]{1,2,0:T(1,128)} %param.19) | copy-start | bytes 12292
  7.0 14.8 %copy-start.9 = (f32[256,256]{1,0:T(8,128)S(1)}, f32[256,256]{1,0:T(8,128)}, u32[]{:S(2)}) copy-start(f32[256,256]{1,0:T(8,128)} %constant.30.clone.bz) | copy-start | bytes 786436
  7.0 14.8 %copy-start.10 = (f32[240,128]{1,0:T(8,128)S(1)}, f32[240,128]{1,0:T(8,128)}, u32[]{:S(2)}) copy-start(f32[240,128]{1,0:T(8,128)} %constant.32.clone.t_high) | copy-start | bytes 368644
  7.0 14.8 %copy-start.11 = (f32[240,128]{1,0:T(8,128)S(1)}, f32[240,128]{1,0:T(8,128)}, u32[]{:S(2)}) copy-start(f32[240,128]{1,0:T(8,128)} %constant.31.clone.t_low) | copy-start | bytes 368644
  7.0 14.9 %copy-start.13 = (f32[40,128]{1,0:T(8,128)S(1)}, f32[40,128]{1,0:T(8,128)}, u32[]{:S(2)}) copy-start(f32[40,128]{1,0:T(8,128)} %constant.34.clone.w_own) | copy-start | bytes 61444
  7.0 14.9 %copy-start.14 = (f32[40,128]{1,0:T(8,128)S(1)}, f32[40,128]{1,0:T(8,128)}, u32[]{:S(2)}) copy-start(f32[40,128]{1,0:T(8,128)} %constant.33.clone.w_low) | copy-start | bytes 61444
  7.0 27.2 %copy-start.6 = (f32[256,256]{1,0:T(8,128)S(1)}, f32[256,256]{1,0:T(8,128)}, u32[]{:S(2)}) copy-start(f32[256,256]{1,0:T(8,128)} %constant.38.clone.v_high) | copy-start | bytes 786436
  7.0 27.2 %copy-start.7 = (f32[256,256]{1,0:T(8,128)S(1)}, f32[256,256]{1,0:T(8,128)}, u32[]{:S(2)}) copy-start(f32[256,256]{1,0:T(8,128)} %constant.37.clone.v_low) | copy-start | bytes 786436
  7.0 27.2 %copy-start.8 = (f32[256,256]{1,0:T(8,128)S(1)}, f32[256,256]{1,0:T(8,128)}, u32[]{:S(2)}) copy-start(f32[256,256]{1,0:T(8,128)} %constant.36.clone.v_own) | copy-start | bytes 786436
  7.1 27.2 %copy-start.12 = (f32[40,48]{1,0:T(8,128)S(1)}, f32[40,48]{1,0:T(8,128)}, u32[]{:S(2)}) copy-start(f32[40,48]{1,0:T(8,128)} %constant.35.clone.my.mx) | copy-start | bytes 23044
  10.5 38.1 %copy-start.1 = (f32[3,32,32,256]{3,2,1,0:T(8,128)S(1)}, f32[3,32,32,256]{3,2,1,0:T(8,128)}, u32[]{:S(2)}) copy-start(f32[3,32,32,256]{3,2,1,0:T(8,128)} %strain.3) | copy-start | bytes 9437188
  10.5 38.1 %copy-start.3 = (f32[32,32,256]{2,1,0:T(8,128)S(1)}, f32[32,32,256]{2,1,0:T(8,128)}, u32[]{:S(2)}) copy-start(f32[32,32,256]{2,1,0:T(8,128)} %kappa.3) | copy-start | bytes 3145732
  10.5 6.4 %collective-permute-start = (f32[128,128]{1,0:T(8,128)S(1)}, f32[128,128]{1,0:T(8,128)S(1)}, u32[]{:S(2)}, u32[]{:S(2)}) collective-permute-start(f32[128,128]{1,0:T(8,128)S(1)} %get-tuple-element.21.sent_a), channel_id=1, source_target_pairs={{0,1},{1,0},{2,3},{3,2},{4,5},{5,4},{6,7},{7,6},{8,9},{9,8},{10,11... | collective-permute-start | bytes 196616 | tf_op jit(solution)/shard_map/ppermute | solution.py:419
  12.1 9.8 %collective-permute-start.1 = (f32[128,128]{1,0:T(8,128)S(1)}, f32[128,128]{1,0:T(8,128)S(1)}, u32[]{:S(2)}, u32[]{:S(2)}) collective-permute-start(f32[128,128]{1,0:T(8,128)S(1)} %get-tuple-element.22.sent_b), channel_id=1, source_target_pairs={{1,2},{2,1},{3,4},{4,3},{5,6},{6,5},{9,10},{10,9},{11,12},{12,11},... | collective-permute-start | bytes 196616 | tf_op jit(solution)/shard_map/ppermute | solution.py:419
  25.0 2.9 %collective-permute-start.2 = (f32[12,32,256]{2,1,0:T(8,128)S(1)}, f32[12,32,256]{2,1,0:T(8,128)S(1)}, u32[]{:S(2)}, u32[]{:S(2)}) collective-permute-start(f32[12,32,256]{2,1,0:T(8,128)S(1)} %get-tuple-element.26), channel_id=1, source_target_pairs={{0,8},{8,0},{16,24},{24,16},{1,9},{9,1},{17,25},{25,17},{2,10},{10... | collective-permute-start | bytes 1179656 | tf_op jit(solution)/shard_map/ppermute | solution.py:419
  25.1 9.1 %collective-permute-start.3 = (f32[12,32,256]{2,1,0:T(8,128)S(1)}, f32[12,32,256]{2,1,0:T(8,128)S(1)}, u32[]{:S(2)}, u32[]{:S(2)}) collective-permute-start(f32[12,32,256]{2,1,0:T(8,128)S(1)} %get-tuple-element.27), channel_id=1, source_target_pairs={{8,16},{16,8},{9,17},{17,9},{10,18},{18,10},{11,19},{19,11},{12,20... | collective-permute-start | bytes 1179656 | tf_op jit(solution)/shard_map/ppermute | solution.py:419
  36.7 7.9 %collective-permute-start.4 = (f32[12,32,256]{2,1,0:T(8,128)S(1)}, f32[12,32,256]{2,1,0:T(8,128)S(1)}, u32[]{:S(2)}, u32[]{:S(2)}) collective-permute-start(f32[12,32,256]{2,1,0:T(8,128)S(1)} %get-tuple-element.32), channel_id=1, source_target_pairs={{0,32},{32,0},{64,96},{96,64},{128,160},{160,128},{192,224},{224,1... | collective-permute-start | bytes 1179656 | tf_op jit(solution)/shard_map/ppermute | solution.py:419
  36.9 11.7 %collective-permute-start.5 = (f32[12,32,256]{2,1,0:T(8,128)S(1)}, f32[12,32,256]{2,1,0:T(8,128)S(1)}, u32[]{:S(2)}, u32[]{:S(2)}) collective-permute-start(f32[12,32,256]{2,1,0:T(8,128)S(1)} %get-tuple-element.33), channel_id=1, source_target_pairs={{32,64},{64,32},{96,128},{128,96},{160,192},{192,160},{33,65},{65,... | collective-permute-start | bytes 1179656 | tf_op jit(solution)/shard_map/ppermute | solution.py:419

commit v2 on v1

v2 whole, which is shorter than its diff:
```python
import functools
import math

import jax
import jax.numpy as jnp
import numpy as np
from jax import lax
from jax.experimental import pallas as pl
from jax.experimental.pallas import tpu as pltpu
from jax.sharding import PartitionSpec as P

REACH = 6
RM_ITERS = 2
LENGTH_SCALE = 3.0
HIGHEST = lax.Precision.HIGHEST
F32 = jnp.float32
VMEM_LIMIT = 40 * 1024 * 1024
INTERPRET = False


def gauss(offset):
    return math.exp(-offset * offset / (2.0 * LENGTH_SCALE * LENGTH_SCALE))


def band(offset):
    return gauss(offset) if abs(offset) <= REACH else 0.0


def z_band(width):
    return np.array([[band(i - k) for k in range(width)] for i in range(width)], np.float32)


def z_low_rows():
    out = np.zeros((240, 128), np.float32)
    for c in range(7):
        for k in range(128):
            out[112 + c, k] = band(k - (c - 7))
    return out


def z_high_rows():
    out = np.zeros((240, 128), np.float32)
    for c in range(6):
        for k in range(128):
            out[112 + c, k] = band(128 + c - k)
    return out


def plane_from_low():
    out = np.zeros((40, 128), np.float32)
    for g in range(8):
        for c in range(7):
            out[g, 16 * g + c] = band(c - 6)
        for e in range(4):
            out[8 * (1 + e) + g, 16 * g + 7 + e] = 1.0
    return out


def plane_from_own():
    out = np.zeros((40, 128), np.float32)
    for g in range(8):
        for c in range(6):
            out[g, 16 * g + c] = band(c + 1)
    return out


def rows_matrix():
    out = np.zeros((40, 48), np.float32)
    for r in range(33):
        at = r if r < 32 else -1
        for k in range(1, 46):
            out[r, k] = band(k - 8 - at)
    return out


def plane_y_matrices():
    own = np.zeros((256, 256), np.float32)
    low = np.zeros((256, 256), np.float32)
    high = np.zeros((256, 256), np.float32)
    for y in range(-1, 32):
        for l in range(32):
            own[l, y + 1] = band(l - y)
            low[l, y + 1] = band(l - 32 - y) if l >= 25 else 0.0
            high[l, y + 1] = band(32 + l - y) if l < 6 else 0.0
    for c in range(1, 5):
        for y in range(32):
            own[32 * c + y, 40 * c + y + 1] = 1.0
        low[32 * c + 31, 40 * c] = 1.0
    return own, low, high


def lanes(shape):
    return lax.broadcasted_iota(jnp.int32, shape, len(shape) - 1)


def rows(shape):
    return lax.broadcasted_iota(jnp.int32, shape, len(shape) - 2)


def inverse_total(position, extent):
    total = jnp.zeros(position.shape, F32)
    for offset in range(-REACH, REACH + 1):
        inside = (position + offset >= 0) & (position + offset < extent)
        total = total + jnp.where(inside, F32(gauss(offset)), F32(0.0))
    return 1.0 / total


def newton_plastic(trial, alpha_old):
    increment = jnp.zeros(trial.shape, F32)
    for _ in range(RM_ITERS):
        hardened = alpha_old + increment
        soft = 0.5 * jnp.exp(-5.0 * hardened)
        excess = trial - increment - (1.0 + 0.5 * hardened - soft)
        increment = jnp.maximum(increment + excess / (1.5 + 5.0 * soft), 0.0)
    return increment


def field_of(first, second, third):
    return first * first + second * second + third * third


def integrity_of(kappa):
    return jnp.exp(-jnp.maximum(kappa - 3.2, 0.0) / 3.0)


def by_parity(even, first, second, use):
    @pl.when(even)
    def _():
        use(first, second)

    @pl.when(jnp.logical_not(even))
    def _():
        use(second, first)


CONTRACT_LANES = (((1,), (1,)), ((), ()))
CHUNK = 8
CHUNKS = 4


def dot(left, right):
    return jnp.dot(left, right, precision=HIGHEST, preferred_element_type=F32)


def dot_lanes(left, right, precision=HIGHEST):
    return lax.dot_general(
        left, right, CONTRACT_LANES, precision=precision, preferred_element_type=F32
    )


def turned_flags(flags):
    eye = (rows((32, 32)) == lanes((32, 32))).astype(F32)
    return dot_lanes(eye, flags[...].astype(F32), None)


def pack_kernel(
    where_ref, strain_in, plastic_in, alpha_in, kappa_in, flags,
    strain, plastic, alpha, kappa, z_a, z_b,
    up_trial, up_alpha, up_drive, low_trial, low_alpha, low_drive, sems,
):
    copies = []
    for c in range(CHUNKS):
        part = pl.ds(c * CHUNK, CHUNK)
        pairs = [(strain_in.at[:, part], strain.at[:, part])]
        pairs += [
            (src.at[part], dst.at[part])
            for src, dst in ((plastic_in, plastic), (alpha_in, alpha), (kappa_in, kappa))
        ]
        copies.append(
            [pltpu.make_async_copy(src, dst, sems.at[c, i]) for i, (src, dst) in enumerate(pairs)]
        )
    for group in copies:
        for copy in group:
            copy.start()
    turned = turned_flags(flags)
    flag = jnp.concatenate(
        [
            jnp.dot(
                turned,
                (rows((32, 128)) == 4 * (lanes((32, 128)) // 16) + b).astype(F32),
                preferred_element_type=F32,
            )
            for b in range(4)
        ],
        axis=0,
    )
    lane = lanes((128, 128))
    for c in range(CHUNKS):
        for copy in copies[c]:
            copy.wait()
        for g in (2 * c, 2 * c + 1):
            inside = lane // 16 == g

            def tile(ref, half):
                cells = ref[4 * g : 4 * g + 4, :, 128 * half : 128 * half + 128]
                return cells.reshape(128, 128)

            def place(ref, value, move):
                moved = pltpu.roll(value, (move + 16 * g) % 128, 1) if move + 16 * g else value
                ref[...] = jnp.where(inside, moved, ref[...])

            s0, s1, s2 = (tile(strain.at[i], 1) for i in range(3))
            place(up_trial, s0 - tile(plastic, 1), 7)
            place(up_alpha, tile(alpha, 1), 7)
            place(up_drive, field_of(s0, s1, s2), 7)
            mixed = up_drive[...]
            for e, value in enumerate((s1, s2, tile(kappa, 1))):
                moved = pltpu.roll(value, (9 + e + 16 * g) % 128, 1)
                mixed = jnp.where(lane == 16 * g + 8 + e, moved, mixed)
            up_drive[...] = mixed
            s0, s1, s2 = (tile(strain.at[i], 0) for i in range(3))
            place(low_trial, s0 - tile(plastic, 0), 0)
            place(low_alpha, tile(alpha, 0), 0)
            place(low_drive, field_of(s0, s1, s2), 0)

    increment = newton_plastic(up_trial[...], up_alpha[...]) * flag
    free = pltpu.roll(up_trial[...] - increment, 1, 1)
    up_drive[...] = jnp.where(
        lane % 16 < 7,
        up_drive[...] + 4.0 * increment,
        jnp.where(lane % 16 == 7, free, up_drive[...]),
    )
    increment = newton_plastic(low_trial[...], low_alpha[...]) * flag
    low_drive[...] = low_drive[...] + 4.0 * increment

    def store(upper, lower):
        upper[...] = up_drive[...]
        lower[...] = low_drive[...]

    by_parity(lax.rem(where_ref[2], 2) == 0, z_a, z_b, store)


def inner_kernel(strain, plastic, alpha, kappa, flags, bz, smooth, free, yext, xext, turned, field):
    turned[...] = turned_flags(flags)

    @pl.loop(0, 8)
    def _(g):
        for i in range(4):
            x = 4 * g + i
            here = (rows((32, 256)) == x).astype(F32)
            flag = jnp.dot(turned[...], here, preferred_element_type=F32)
            s0 = strain[0, x]
            trial = s0 - plastic[x]
            increment = newton_plastic(trial, alpha[x]) * flag
            field[x] = field_of(s0, strain[1, x], strain[2, x]) + 4.0 * increment
            free[x] = trial - increment

    for g in range(4):
        part = field[8 * g : 8 * g + 8].reshape(256, 256)
        smooth[8 * g : 8 * g + 8] = dot(part, bz[...]).reshape(8, 32, 256)
    for e, ref in enumerate((free, strain.at[1], strain.at[2], kappa)):
        xext[e] = ref[31]
        for x in range(32):
            yext[e, x : x + 1, :] = ref[x, 31:32, :]


def z_kernel(
    where_ref, own, yext, sent_a, sent_b, got_a, got_b, t_low, t_high, w_low, w_own,
    smooth, plane, y_a, y_b, z_low, z_high, own_low, head_rows, tail_rows,
):
    def choose(upper, lower):
        z_high[...] = upper[0][...]
        z_low[...] = lower[0][...]
        own_low[...] = lower[1][...]

    by_parity(lax.rem(where_ref[2], 2) == 0, (got_a, sent_a), (got_b, sent_b), choose)
    for g in range(8):
        part = slice(4 * g, 4 * g + 4)
        start = 112 - 16 * g
        first = dot(z_low[...], t_low[start : start + 128])
        last = dot(z_high[...], t_high[start : start + 128])
        smooth[part, :, 0:128] = own[part, :, 0:128] + first.reshape(4, 32, 128)
        smooth[part, :, 128:256] = own[part, :, 128:256] + last.reshape(4, 32, 128)
    turned = dot_lanes(w_low[...], z_low[...]) + dot_lanes(w_own[...], own_low[...])
    lane = lanes((8, 128))
    for b in range(4):
        head = jnp.zeros((8, 128), F32)
        for c in range(4):
            moved = pltpu.roll(turned[8 * c : 8 * c + 8], (32 * (c - b)) % 128, 1)
            head = jnp.where(lane // 32 == c, moved, head)
        tail = jnp.where(lane < 32, pltpu.roll(turned[32:40], (-32 * b) % 128, 1), 0.0)
        head_rows[pl.ds(b, 8, stride=4), :] = head
        tail_rows[pl.ds(b, 8, stride=4), :] = tail
    plane[:, 0:128] = head_rows[...]
    plane[:, 128:256] = tail_rows[...]

    def store(upper, lower):
        for j in range(7):
            upper[j] = smooth[:, 25 + j, :]
        for e in range(4):
            upper[7 + e] = yext[e]
        upper[11] = plane[...]
        for j in range(6):
            lower[j] = smooth[:, j, :]
        lower[11] = plane[...]

    by_parity(lax.rem(where_ref[1], 2) == 0, y_a, y_b, store)


def own_rows_kernel(smooth, my, out, out_face):
    for x in range(32):
        both = dot(my[...], smooth[x])
        out[x] = both[0:32]
        out_face[x : x + 1, :] = both[32:33]


def y_kernel(
    where_ref, own, own_face, plane, xext, got_a, got_b, my, v_own, v_low, v_high,
    edges, out_face, out_plane, face_ext, halo, x_a, x_b, plane_low, plane_high,
):
    def choose(upper, lower):
        for j in range(7):
            halo[:, j, :] = lower[j]
        for j in range(6):
            halo[:, 8 + j, :] = upper[j]
        for e in range(4):
            face_ext[e] = lower[7 + e]
        plane_low[...] = lower[11]
        plane_high[...] = upper[11]

    halo[:, 0:8, :] = jnp.zeros((32, 8, 256), F32)
    halo[:, 8:16, :] = jnp.zeros((32, 8, 256), F32)
    by_parity(lax.rem(where_ref[1], 2) == 0, got_a, got_b, choose)
    for x in range(32):
        if x < 8 or x >= 24:
            both = dot(my[...], halo[x])
            edges[x if x < 8 else x - 16] = own[x] + both[0:32]
            out_face[x : x + 1, :] = own_face[x : x + 1, :] + both[32:33]
        else:
            both = dot(my[32:40, :], halo[x])
            out_face[x : x + 1, :] = own_face[x : x + 1, :] + both[0:1]
    total = dot(plane[...], v_own[...])
    total += dot(plane_low[...], v_low[...])
    total += dot(plane_high[...], v_high[...])
    out_plane[...] = total

    def store(upper, lower):
        for j in range(7):
            upper[j] = edges[9 + j]
        for e in range(4):
            upper[7 + e] = xext[e]
        upper[11] = jnp.zeros((32, 256), F32)
        upper[11, 0:8, :] = out_face[24:32, :]
        for e in range(4):
            upper[11, 8 + e : 9 + e, :] = face_ext[e, 31:32, :]
        upper[11, 16:24, :] = out_plane[24:32, :]
        for j in range(6):
            lower[j] = edges[j]
        lower[11] = jnp.zeros((32, 256), F32)
        lower[11, 0:8, :] = out_face[0:8, :]
        lower[11, 16:24, :] = out_plane[0:8, :]

    by_parity(lax.rem(where_ref[0], 2) == 0, x_a, x_b, store)


def faces(extents, at, mx, face_all, plane_all, side, face_e, face_a, column, inv_x, inv_yz):
    nx, ny, nz = extents
    ix, iy, iz = at
    shape = (40, 256)
    row, lane = rows(shape), lanes(shape)
    invx = inverse_total(ix * 32 + jnp.where(row < 32, row, -1), nx)
    inv_x[...] = invx
    small = (32, 256)
    invz = inverse_total(iz * 256 + lanes(small), nz)
    inv_yz[...] = inverse_total(iy * 32 + rows(small), ny) * invz

    def previous(value):
        return jnp.where(row == 0, value[32:33, :], pltpu.roll(value, 1, 0))

    def joined(t0, t1, t2):
        a0 = previous(t0) - t0
        a1 = previous(t1) + t1
        a2 = previous(t2) + t2
        return a0 + a1, a0 - a1, a2

    at_y = inverse_total(jnp.full((1, 256), iy * 32 - 1, jnp.int32), ny)
    kap = jnp.maximum(side[3], dot(mx[...], face_all[...]) * (invx * (at_y * invz[0:1, :])))
    integ = integrity_of(kap)
    e, _, a2 = joined(integ * side[0], integ * side[1], integ * side[2])
    face_e[...] = e[0:32]
    face_a[...] = a2[0:32]

    avg = dot(mx[...], plane_all[...])
    own = jnp.where(row == 32, plane_all[7:8, :], plane_all[8:48, :])

    def value(c):
        return pltpu.roll(own, (256 - 40 * c) % 256, 1)

    at_z = inverse_total(jnp.full((1, 256), iz * 256 - 1, jnp.int32), nz)
    invy = inverse_total(iy * 32 - 1 + jnp.minimum(lane, 32), ny)
    kap = jnp.maximum(value(4), avg * (invx * (invy * at_z)))
    integ = integrity_of(kap)
    e, f, a2 = joined(integ * value(1), integ * value(2), integ * value(3))
    parts = e + a2 + pltpu.roll(f + a2, 255, 1)
    parts = jnp.where(lane < 32, parts, 0.0)
    eye = (rows((32, 128)) == lanes((32, 128))).astype(F32)
    pad = jnp.concatenate([parts[0:32, 0:128], jnp.zeros((96, 128), F32)], axis=0)
    column[...] = dot_lanes(eye, pad)


def layer_results(x, avg, kappa, free, strain, before, face_e, face_a, column, force_at, kappa_at):
    first_row = rows((32, 256)) == 0
    first_lane = lanes((32, 128)) == 0
    kap = jnp.maximum(kappa[x], avg)
    integ = integrity_of(kap)
    s0, s1, s2 = integ * free[x], integ * strain[1, x], integ * strain[2, x]
    if force_at is not None:
        kappa_at[...] = kap
        a0 = before[0] - s0
        a1 = before[1] + s1
        a2 = before[2] + s2
        e, f = a0 + a1, a0 - a1
        b = f + jnp.where(first_row, face_e[pl.ds(x, 1), :], pltpu.roll(e, 1, 0))
        c = a2 + jnp.where(first_row, face_a[pl.ds(x, 1), :], pltpu.roll(a2, 1, 0))
        p, q = b + c, b - c
        moved = pltpu.roll(p, 1, 1)
        edge = pltpu.roll(column[...], lax.rem(128 - x, 128), 1)
        force_at[:, 0:128] = 0.25 * (q[:, 0:128] + jnp.where(first_lane, edge, moved[:, 0:128]))
        force_at[:, 128:256] = 0.25 * (q[:, 128:256] + moved[:, 128:256])
    before[0] = s0
    before[1] = s1
    before[2] = s2


def middle_kernel(
    extents, where_ref, strain, free, kappa, own, edges, halo, face, plane, face_ext, my,
    force, kappa_new, part,
    ext, face_all, plane_all, side, before, face_e, face_a, column, inv_x, inv_yz,
    force_v, kappa_v, sems,
):
    at = (where_ref[0], where_ref[1], where_ref[2])
    for x in range(32):
        if x < 8:
            ext[x] = edges[x]
        elif x >= 24:
            ext[x] = edges[x - 16]
        else:
            ext[x] = own[x] + dot(my[:, 32:48][0:32], halo[x])
    for ref, value in ((face_all, face), (plane_all, plane)):
        ref[0:8, :] = jnp.zeros((8, 256), F32)
        ref[8:40, :] = value[...]
        ref[40:48, :] = jnp.zeros((8, 256), F32)
    for e in range(4):
        side[e, 0:32, :] = face_ext[e]
        side[e, 32:40, :] = jnp.zeros((8, 256), F32)
    faces(
        extents, at, my.at[:, 48:96], face_all, plane_all, side,
        face_e, face_a, column, inv_x, inv_yz,
    )

    def layer(x):
        total = gauss(0) * ext[x]
        for a in range(1, REACH + 1):
            total = total + gauss(a) * (ext[x - a] + ext[x + a])
        return total * (inv_x[pl.ds(x, 1), :] * inv_yz[...])

    layer_results(7, layer(7), kappa, free, strain, before, None, None, None, None, None)
    copies = []
    for c in (1, 2):

        @pl.loop(0, CHUNK)
        def _(i):
            x = c * CHUNK + i
            layer_results(
                x, layer(x), kappa, free, strain, before, face_e, face_a, column,
                force_v.at[x - CHUNK], kappa_v.at[x - CHUNK],
            )

        here = pl.ds((c - 1) * CHUNK, CHUNK)
        there = pl.ds(c * CHUNK, CHUNK)
        for k, (src, dst) in enumerate(((force_v, force), (kappa_v, kappa_new))):
            copy = pltpu.make_async_copy(src.at[here], dst.at[there], sems.at[c - 1, k])
            copy.start()
            copies.append(copy)
    for i in range(18):
        x = i - 1 if i < 9 else i + 14
        total = None
        for a in range(-REACH, REACH + 1):
            if 0 <= x + a < 32:
                term = gauss(a) * ext[x + a]
                total = term if total is None else total + term
        part[i] = total
    for copy in copies:
        copy.wait()


def outer_kernel(
    extents, where_ref, strain, free, kappa, part, face, plane, face_ext, got_a, got_b, my,
    force_in, kappa_in,
    force, kappa_new,
    low, high, face_all, plane_all, side, before, face_e, face_a, column, inv_x, inv_yz,
    force_v, kappa_v, sems,
):
    at = (where_ref[0], where_ref[1], where_ref[2])

    def choose(upper, lower):
        for j in range(7):
            low[j] = lower[j]
        for j in range(6):
            high[j] = upper[j]
        face_all[0:8, :] = lower[11, 0:8, :]
        face_all[40:48, :] = upper[11, 0:8, :]
        plane_all[0:8, :] = lower[11, 16:24, :]
        plane_all[40:48, :] = upper[11, 16:24, :]
        for e in range(4):
            side[e, 32:33, :] = lower[11, 8 + e : 9 + e, :]
            before[e] = lower[7 + e]

    for e in range(4):
        side[e, 0:32, :] = face_ext[e]
        side[e, 32:40, :] = jnp.zeros((8, 256), F32)
    by_parity(lax.rem(at[0], 2) == 0, got_a, got_b, choose)
    face_all[8:40, :] = face[...]
    plane_all[8:40, :] = plane[...]
    faces(
        extents, at, my.at[:, 48:96], face_all, plane_all, side,
        face_e, face_a, column, inv_x, inv_yz,
    )

    def layer(x):
        total = part[x + 1 if x < 8 else x - 14]
        for a in range(-REACH, REACH + 1):
            if x + a < 0:
                total = total + gauss(a) * low[x + a + 7]
            elif x + a >= 32:
                total = total + gauss(a) * high[x + a - 32]
        return total * (inv_x[x % 33 : x % 33 + 1, :] * inv_yz[...])

    kap = jnp.maximum(before[3], layer(-1))
    integ = integrity_of(kap)
    for e in range(3):
        before[e] = integ * before[e]
    copies = []
    for c in (0, 3):
        if c == 3:
            layer_results(23, layer(23), kappa, free, strain, before, None, None, None, None, None)
        for i in range(CHUNK):
            x = c * CHUNK + i
            slot = i if c == 0 else CHUNK + i
            layer_results(
                x, layer(x), kappa, free, strain, before, face_e, face_a, column,
                force_v.at[slot], kappa_v.at[slot],
            )
        here = pl.ds(0 if c == 0 else CHUNK, CHUNK)
        there = pl.ds(c * CHUNK, CHUNK)
        for k, (src, dst) in enumerate(((force_v, force), (kappa_v, kappa_new))):
            copy = pltpu.make_async_copy(src.at[here], dst.at[there], sems.at[c // 3, k])
            copy.start()
            copies.append(copy)
    for copy in copies:
        copy.wait()


def swap(first, second, axis):
    count = lax.axis_size(axis)

    def route(start):
        out = []
        for i in range(start, count - 1, 2):
            out += [(i, i + 1), (i + 1, i)]
        return out

    return lax.ppermute(first, axis, route(0)), lax.ppermute(second, axis, route(1))


def shape_of(*dims):
    return jax.ShapeDtypeStruct(dims, F32)


VM = pl.BlockSpec(memory_space=pltpu.VMEM)
SM = pl.BlockSpec(memory_space=pltpu.SMEM)
HBM = pl.BlockSpec(memory_space=pltpu.HBM)
BLOCK = shape_of(32, 32, 256)
FACE = shape_of(32, 256)


def vmem(*dims):
    return pltpu.VMEM(dims, F32)


def call(kernel, name, in_specs, out_shape, out_specs=None, scratch=(), **kwargs):
    return pl.pallas_call(
        kernel,
        name=name,
        in_specs=in_specs,
        out_specs=out_specs or [VM] * len(out_shape),
        out_shape=out_shape,
        scratch_shapes=list(scratch),
        interpret=INTERPRET,
        compiler_params=pltpu.CompilerParams(vmem_limit_bytes=VMEM_LIMIT),
        **kwargs,
    )


def body(strain_in, plastic_in, alpha_in, kappa_in, flags):
    where = jnp.stack([lax.axis_index(a) for a in ("gx", "gy", "gz")]).astype(jnp.int32)
    flags = flags.reshape(32, 32)
    extents = (
        32 * lax.axis_size("gx"), 32 * lax.axis_size("gy"), 256 * lax.axis_size("gz"),
    )
    rows_all = rows_matrix()
    rows_own = np.ascontiguousarray(rows_all[:, 8:40])
    rows_halo = np.concatenate(
        [rows_all[:, 1:8], np.zeros((40, 1), np.float32), rows_all[:, 40:48]], axis=1
    )
    rows_three = np.zeros((40, 128), np.float32)
    rows_three[:, 32:48] = rows_halo
    rows_three[:, 48:96] = rows_all

    strain, plastic, alpha, kappa, z_a, z_b = call(
        pack_kernel,
        "pack",
        [SM, HBM, HBM, HBM, HBM, VM],
        [shape_of(3, 32, 32, 256), BLOCK, BLOCK, BLOCK, shape_of(128, 128), shape_of(128, 128)],
        scratch=[vmem(128, 128)] * 6 + [pltpu.SemaphoreType.DMA((CHUNKS, 4))],
    )(where, strain_in, plastic_in, alpha_in, kappa_in, flags)
    got_a, got_b = swap(z_a, z_b, "gz")
    own, free, yext, xext = call(
        inner_kernel,
        "inner",
        [VM] * 6,
        [BLOCK, BLOCK, shape_of(4, 32, 256), shape_of(4, 32, 256)],
        scratch=[vmem(32, 32), vmem(32, 32, 256)],
    )(strain, plastic, alpha, kappa, flags, z_band(256))

    smooth, plane, y_a, y_b = call(
        z_kernel,
        "along_z",
        [SM] + [VM] * 10,
        [BLOCK, FACE, shape_of(12, 32, 256), shape_of(12, 32, 256)],
        scratch=[vmem(128, 128)] * 3 + [vmem(32, 128)] * 2,
    )(
        where, own, yext, z_a, z_b, got_a, got_b,
        z_low_rows(), z_high_rows(), plane_from_low(), plane_from_own(),
    )
    got_a, got_b = swap(y_a, y_b, "gy")
    own, own_face = call(own_rows_kernel, "own_rows", [VM] * 2, [BLOCK, FACE])(smooth, rows_own)

    edges, face, plane, face_ext, halo, x_a, x_b = call(
        y_kernel,
        "along_y",
        [SM] + [VM] * 10,
        [
            shape_of(16, 32, 256), FACE, FACE, shape_of(4, 32, 256), shape_of(32, 16, 256),
            shape_of(12, 32, 256), shape_of(12, 32, 256),
        ],
        scratch=[vmem(32, 256), vmem(32, 256)],
    )(where, own, own_face, plane, xext, got_a, got_b, rows_halo, *plane_y_matrices())
    got_a, got_b = swap(x_a, x_b, "gx")

    shared = [
        vmem(48, 256), vmem(48, 256), vmem(4, 40, 256), vmem(4, 32, 256),
        vmem(32, 256), vmem(32, 256), vmem(32, 128), vmem(40, 256), vmem(32, 256),
        vmem(16, 32, 256), vmem(16, 32, 256), pltpu.SemaphoreType.DMA((2, 2)),
    ]
    force, kappa_new, part = call(
        functools.partial(middle_kernel, extents),
        "middle",
        [SM] + [VM] * 10,
        [BLOCK, BLOCK, shape_of(18, 32, 256)],
        out_specs=[HBM, HBM, VM],
        scratch=[vmem(32, 32, 256)] + shared,
    )(where, strain, free, kappa, own, edges, halo, face, plane, face_ext, rows_three)
    force, kappa_new = call(
        functools.partial(outer_kernel, extents),
        "outer",
        [SM] + [VM] * 10 + [HBM, HBM],
        [BLOCK, BLOCK],
        out_specs=[HBM, HBM],
        scratch=[vmem(7, 32, 256), vmem(6, 32, 256)] + shared,
        input_output_aliases={11: 0, 12: 1},
    )(
        where, strain, free, kappa, part, face, plane, face_ext, got_a, got_b, rows_three,
        force, kappa_new,
    )
    return (force, kappa_new)


def solution(mesh):
    in_specs = (
        P(None, "gx", "gy", "gz"),
        P("gx", "gy", "gz"),
        P("gx", "gy", "gz"),
        P("gx", "gy", "gz"),
        P("gx", "gy", "gz"),
    )
    out_specs = (P("gx", "gy", "gz"), P("gx", "gy", "gz"))
    return jax.shard_map(body, mesh=mesh, in_specs=in_specs, out_specs=out_specs, check_vma=False)
```

time: 55.7 us -> 50.2 us (0.901)
  waiting for transfers between devices: 17 us -> 8.31 us
  Pallas kernels: 15.7 us -> 18.9 us
    ppermute x3, waiting for transfers between devices: 15.3 us -> 8.3 us  [swap(): lax.ppermute(second, axis, route(1))]
    pallas_call x4 -> x7, Pallas kernels: 15.7 us -> 18.9 us  [the longest x1 4.58 us: body(): call(functools.partial(middle_kernel, extents), 'middle', [SM] + [VM] * 1...]
    ppermute x3, waiting for transfers between devices: 1.73 us -> 0.01 us  [swap(): lax.ppermute(first, axis, route(0))]
  transfers between devices with their start and end apart: 6 -> 6, of which waited for: 4 -> 3; matrix products, arithmetic and copies ran while one was open for 0% -> 0% of each run, Pallas kernels for 0% -> 17%
where the time goes in v2:
time: 50.2 us; the launch traced here: 49.7 us
  Pallas kernels  18.9 us (38%)
  starting transfers between devices  15.2 us (30%)
  waiting for transfers between devices  8.31 us (17%)
  local copies, waits for them, and re-layouts  6.35 us (13%)
  between operations  0.87 us (2%)
    ppermute x3, starting transfers between devices, swap(): lax.ppermute(second, axis, route(1))  13.4 us
    ppermute x3, waiting for transfers between devices, swap(): lax.ppermute(second, axis, route(1))  8.3 us
    unnamed x32, local copies, waits for them, and re-layouts  6.35 us
    pallas_call x1, Pallas kernels, body(): call(functools.partial(middle_kernel, extents), 'middle', [SM] + [VM] * 1...  4.58 us
    pallas_call x1, Pallas kernels, body(): call(pack_kernel, 'pack', [SM, HBM, HBM, HBM, HBM, VM], [shape_of(3, 32,...  3.21 us
    pallas_call x1, Pallas kernels, body(): call(inner_kernel, 'inner', [VM] * 6, [BLOCK, BLOCK, shape_of(4, 32, 256)...  2.92 us
    pallas_call x1, Pallas kernels, body(): call(functools.partial(outer_kernel, extents), 'outer', [SM] + [VM] * 10...  2.75 us
    pallas_call x1, Pallas kernels, body(): call(z_kernel, 'along_z', [SM] + [VM] * 10, [BLOCK, FACE, shape_of(12, 32...  2.17 us
  transfers between devices with their start and end apart: 6, of which 3 were waited for; matrix products, arithmetic and copies ran while one was open for 0% of the time, Pallas kernels for 17%

profile of v2, /device:TPU:120, one launch (start us, length us, event | category | flops | bytes accessed | tf_op | source)
XLA Modules:
  0.0 49.7 jit_solution(10018693678365642393)
XLA Ops:
  0.6 0.1 pad_add_fusion.where_ref
  0.7 0.0 copy-start
  0.7 1.9 %copy-done = f32[3,32,32,256]{3,2,1,0:T(8,128)S(1)} copy-done((f32[3,32,32,256]{3,2,1,0:T(8,128)S(1)}, f32[3,32,32,256]{3,2,1,0:T(8,128)}, u32[]{:S(2)}) %copy-start) | copy-done | bytes 3145752
  2.6 0.0 copy-start.1
  2.6 1.2 %copy-done.1 = f32[32,32,256]{2,1,0:T(8,128)S(1)} copy-done((f32[32,32,256]{2,1,0:T(8,128)S(1)}, f32[32,32,256]{2,1,0:T(8,128)}, u32[]{:S(2)}) %copy-start.1) | copy-done | bytes 1048600
  3.8 0.0 copy-start.2
  3.8 1.2 %copy-done.2 = f32[32,32,256]{2,1,0:T(8,128)S(1)} copy-done((f32[32,32,256]{2,1,0:T(8,128)S(1)}, f32[32,32,256]{2,1,0:T(8,128)}, u32[]{:S(2)}) %copy-start.2) | copy-done | bytes 1048600
  5.1 0.0 copy-start.3
  5.1 1.2 %copy-done.3 = f32[32,32,256]{2,1,0:T(8,128)S(1)} copy-done((f32[32,32,256]{2,1,0:T(8,128)S(1)}, f32[32,32,256]{2,1,0:T(8,128)}, u32[]{:S(2)}) %copy-start.3) | copy-done | bytes 1048600
  6.3 0.0 copy-start.11
  6.3 0.7 %copy-done.11 = s32[32,32,1]{1,2,0:T(1,128)S(1)} copy-done((s32[32,32,1]{1,2,0:T(1,128)S(1)}, s32[32,32,1]{1,2,0:T(1,128)}, u32[]{:S(2)}) %copy-start.11) | copy-done | bytes 4120
  7.0 0.0 copy-start.7
  7.0 3.2 %pack.1 = (f32[3,32,32,256]{3,2,1,0:T(8,128)S(1)}, f32[32,32,256]{2,1,0:T(8,128)S(1)}, f32[32,32,256]{2,1,0:T(8,128)S(1)}, f32[32,32,256]{2,1,0:T(8,128)S(1)}, f...) custom-call(s32[3]{0:T(128)S(1)} %pad_add_fusion.where_ref, f32[3,32,32,256]{3,2,1,0:T(8,128)S(1)} %copy-done, ...), custom_call_target="tpu_custom_call" | custom-call | tf_op jit(solution)/shard_map/pack/pallas_call | solution.py:610
  10.2 1.6 %collective-permute-start = (f32[128,128]{1,0:T(8,128)S(1)}, f32[128,128]{1,0:T(8,128)S(1)}, u32[]{:S(2)}, u32[]{:S(2)}) collective-permute-start(f32[128,128]{1,0:T(8,128)S(1)} %get-tuple-element.35.sent_a), channel_id=1, source_target_pairs={{0,1},{1,0},{2,3},{3,2},{4,5},{5,4},{6,7},{7,6},{8,9},{9,8},{10,11... | collective-permute-start | bytes 196616 | tf_op jit(solution)/shard_map/ppermute | solution.py:563
  11.8 4.7 %collective-permute-start.1 = (f32[128,128]{1,0:T(8,128)S(1)}, f32[128,128]{1,0:T(8,128)S(1)}, u32[]{:S(2)}, u32[]{:S(2)}) collective-permute-start(f32[128,128]{1,0:T(8,128)S(1)} %get-tuple-element.36.sent_b), channel_id=1, source_target_pairs={{1,2},{2,1},{3,4},{4,3},{5,6},{6,5},{9,10},{10,9},{11,12},{12,11},... | collective-permute-start | bytes 196616 | tf_op jit(solution)/shard_map/ppermute | solution.py:563
  16.5 0.0 copy-done.7
  16.5 0.0 copy-start.8
  16.5 0.0 copy-start.9
  16.5 0.0 copy-start.14
  16.5 0.0 copy-start.15
  16.5 0.0 copy-start.13
  16.5 0.0 copy-start.4
  16.5 0.0 copy-start.5
  16.6 0.0 copy-start.6
  16.6 0.0 copy-start.12
  16.6 2.9 %inner.1 = (f32[32,32,256]{2,1,0:T(8,128)S(1)}, f32[32,32,256]{2,1,0:T(8,128)S(1)}, f32[4,32,256]{2,1,0:T(8,128)S(1)}, f32[4,32,256]{2,1,0:T(8,128)S(1)}) custom-call(f32[3,32,32,256]{3,2,1,0:T(8,128)S(1)} %get-tuple-element.28.strain, f32[32,32,256]{2,1,0:T(8,128)S(1)} %get-tuple-element.29.plastic, f32[32,32,256]{2,1,0:T(8,128)S(1)} %get-tuple-element.30.alpha, ...), custom_call_target="tpu_custom_call" | custom-call | tf_op jit(solution)/shard_map/inner/pallas_call | solution.py:618
  19.5 0.0 copy-start.10
  19.5 0.0 collective-permute-done.got_a
  19.5 2.0 %collective-permute-done.1.got_b = f32[128,128]{1,0:T(8,128)S(1)} collective-permute-done((f32[128,128]{1,0:T(8,128)S(1)}, f32[128,128]{1,0:T(8,128)S(1)}, u32[]{:S(2)}, u32[]{:S(2)}) %collective-permute-start.1) | collective-permute-done | bytes 65568 | tf_op jit(solution)/shard_map/ppermute | solution.py:563
  21.6 0.0 copy-done.8
  21.6 0.0 copy-done.9
  21.6 0.0 copy-done.14
  21.6 0.0 copy-done.15
  21.6 2.2 %along_z.1 = (f32[32,32,256]{2,1,0:T(8,128)S(1)}, f32[32,256]{1,0:T(8,128)S(1)}, f32[12,32,256]{2,1,0:T(8,128)S(1)}, f32[12,32,256]{2,1,0:T(8,128)S(1)}) custom-call(s32[3]{0:T(128)S(1)} %pad_add_fusion.where_ref, f32[32,32,256]{2,1,0:T(8,128)S(1)} %get-tuple-element.33.own, f32[4,32,256]{2,1,0:T(8,128)S(1)} %get-tuple-element.34.yext, ...), custom_call_target="tpu_custom_call" | custom-call | tf_op jit(solution)/shard_map/along_z/pallas_call | solution.py:626
  23.8 0.1 collective-permute-start.2
  23.9 2.7 %collective-permute-start.3 = (f32[12,32,256]{2,1,0:T(8,128)S(1)}, f32[12,32,256]{2,1,0:T(8,128)S(1)}, u32[]{:S(2)}, u32[]{:S(2)}) collective-permute-start(f32[12,32,256]{2,1,0:T(8,128)S(1)} %get-tuple-element.43), channel_id=1, source_target_pairs={{8,16},{16,8},{9,17},{17,9},{10,18},{18,10},{11,19},{19,11},{12,20... | collective-permute-start | bytes 1179656 | tf_op jit(solution)/shard_map/ppermute | solution.py:563
  26.6 0.0 copy-done.13
  26.6 1.2 %own_rows.1 = (f32[32,32,256]{2,1,0:T(8,128)S(1)}, f32[32,256]{1,0:T(8,128)S(1)}) custom-call(f32[32,32,256]{2,1,0:T(8,128)S(1)} %get-tuple-element.37.smooth, f32[40,32]{1,0:T(8,128)S(1)} %copy-done.13), custom_call_target="tpu_custom_call" | custom-call | tf_op jit(solution)/shard_map/own_rows/pallas_call | solution.py:637
  27.8 0.0 collective-permute-done.2.got_a
  27.8 5.2 %collective-permute-done.3.got_b = f32[12,32,256]{2,1,0:T(8,128)S(1)} collective-permute-done((f32[12,32,256]{2,1,0:T(8,128)S(1)}, f32[12,32,256]{2,1,0:T(8,128)S(1)}, u32[]{:S(2)}, u32[]{:S(2)}) %collective-permute-start.3) | collective-permute-done | bytes 393248 | tf_op jit(solution)/shard_map/ppermute | solution.py:563
  32.9 0.0 copy-done.4
  32.9 0.0 copy-done.5
  33.0 0.0 copy-done.6
  33.0 0.0 copy-done.12
  33.0 2.1 %along_y.1 = (f32[16,32,256]{2,1,0:T(8,128)S(1)}, f32[32,256]{1,0:T(8,128)S(1)}, f32[32,256]{1,0:T(8,128)S(1)}, f32[4,32,256]{2,1,0:T(8,128)S(1)}, f32[32,16,256...) custom-call(s32[3]{0:T(128)S(1)} %pad_add_fusion.where_ref, ...), custom_call_target="tpu_custom_call" | custom-call | tf_op jit(solution)/shard_map/along_y/pallas_call | solution.py:639
  35.1 0.2 collective-permute-start.4
  35.3 6.0 %collective-permute-start.5 = (f32[12,32,256]{2,1,0:T(8,128)S(1)}, f32[12,32,256]{2,1,0:T(8,128)S(1)}, u32[]{:S(2)}, u32[]{:S(2)}) collective-permute-start(f32[12,32,256]{2,1,0:T(8,128)S(1)} %get-tuple-element.51), channel_id=1, source_target_pairs={{32,64},{64,32},{96,128},{128,96},{160,192},{192,160},{33,65},{65,... | collective-permute-start | bytes 1179656 | tf_op jit(solution)/shard_map/ppermute | solution.py:563
  41.2 0.0 copy-done.10
  41.3 4.6 %middle.1 = (f32[32,32,256]{2,1,0:T(8,128)}, f32[32,32,256]{2,1,0:T(8,128)}, f32[18,32,256]{2,1,0:T(8,128)S(1)}) custom-call(s32[3]{0:T(128)S(1)} %pad_add_fusion.where_ref, f32[3,32,32,256]{3,2,1,0:T(8,128)S(1)} %get-tuple-element.28.strain, f32[32,32,256]{2,1,0:T(8,128)S(1)} %get-tuple-element.32.free, f32[32,32,256]{2,1,0:T(8,128)S(1)} %get-tuple-element.31.kappa, ...), custom_call_target="tpu_custom_call" | custom-call | tf_op jit(solution)/shard_map/middle/pallas_call | solution.py:656
  45.8 0.0 collective-permute-done.4.got_a
  45.9 1.1 %collective-permute-done.5.got_b = f32[12,32,256]{2,1,0:T(8,128)S(1)} collective-permute-done((f32[12,32,256]{2,1,0:T(8,128)S(1)}, f32[12,32,256]{2,1,0:T(8,128)S(1)}, u32[]{:S(2)}, u32[]{:S(2)}) %collective-permute-start.5) | collective-permute-done | bytes 393248 | tf_op jit(solution)/shard_map/ppermute | solution.py:563
  47.0 2.8 %outer.1 = (f32[32,32,256]{2,1,0:T(8,128)}, f32[32,32,256]{2,1,0:T(8,128)}) custom-call(s32[3]{0:T(128)S(1)} %pad_add_fusion.where_ref, f32[3,32,32,256]{3,2,1,0:T(8,128)S(1)} %get-tuple-element.28.strain, f32[32,32,256]{2,1,0:T(8,128)S(1)} %get-tuple-element.32.free, ...), custom_call_target="tpu_custom_call", output_to_operand_aliasing={{0}: (11, {}), {1}: (12, {})} | custom-call | tf_op jit(solution)/shard_map/outer/pallas_call | solution.py:664
Async XLA Ops:
  0.7 1.9 %copy-start = (f32[3,32,32,256]{3,2,1,0:T(8,128)S(1)}, f32[3,32,32,256]{3,2,1,0:T(8,128)}, u32[]{:S(2)}) copy-start(f32[3,32,32,256]{3,2,1,0:T(8,128)} %strain_in.1) | copy-start | bytes 9437188
  2.6 1.2 %copy-start.1 = (f32[32,32,256]{2,1,0:T(8,128)S(1)}, f32[32,32,256]{2,1,0:T(8,128)}, u32[]{:S(2)}) copy-start(f32[32,32,256]{2,1,0:T(8,128)} %plastic_in.1) | copy-start | bytes 3145732
  3.8 1.2 %copy-start.2 = (f32[32,32,256]{2,1,0:T(8,128)S(1)}, f32[32,32,256]{2,1,0:T(8,128)}, u32[]{:S(2)}) copy-start(f32[32,32,256]{2,1,0:T(8,128)} %alpha_in.1) | copy-start | bytes 3145732
  5.1 1.2 %copy-start.3 = (f32[32,32,256]{2,1,0:T(8,128)S(1)}, f32[32,32,256]{2,1,0:T(8,128)}, u32[]{:S(2)}) copy-start(f32[32,32,256]{2,1,0:T(8,128)} %kappa_in.1) | copy-start | bytes 3145732
  6.3 0.7 %copy-start.11 = (s32[32,32,1]{1,2,0:T(1,128)S(1)}, s32[32,32,1]{1,2,0:T(1,128)}, u32[]{:S(2)}) copy-start(s32[32,32,1]{1,2,0:T(1,128)} %param.20) | copy-start | bytes 12292
  7.0 9.5 %copy-start.7 = (f32[256,256]{1,0:T(8,128)S(1)}, f32[256,256]{1,0:T(8,128)}, u32[]{:S(2)}) copy-start(f32[256,256]{1,0:T(8,128)} %constant.34.clone.bz) | copy-start | bytes 786436
  10.2 9.3 %collective-permute-start = (f32[128,128]{1,0:T(8,128)S(1)}, f32[128,128]{1,0:T(8,128)S(1)}, u32[]{:S(2)}, u32[]{:S(2)}) collective-permute-start(f32[128,128]{1,0:T(8,128)S(1)} %get-tuple-element.35.sent_a), channel_id=1, source_target_pairs={{0,1},{1,0},{2,3},{3,2},{4,5},{5,4},{6,7},{7,6},{8,9},{9,8},{10,11... | collective-permute-start | bytes 196616 | tf_op jit(solution)/shard_map/ppermute | solution.py:563
  11.8 9.8 %collective-permute-start.1 = (f32[128,128]{1,0:T(8,128)S(1)}, f32[128,128]{1,0:T(8,128)S(1)}, u32[]{:S(2)}, u32[]{:S(2)}) collective-permute-start(f32[128,128]{1,0:T(8,128)S(1)} %get-tuple-element.36.sent_b), channel_id=1, source_target_pairs={{1,2},{2,1},{3,4},{4,3},{5,6},{6,5},{9,10},{10,9},{11,12},{12,11},... | collective-permute-start | bytes 196616 | tf_op jit(solution)/shard_map/ppermute | solution.py:563
  16.5 5.1 %copy-start.8 = (f32[240,128]{1,0:T(8,128)S(1)}, f32[240,128]{1,0:T(8,128)}, u32[]{:S(2)}) copy-start(f32[240,128]{1,0:T(8,128)} %constant.36.clone.t_high) | copy-start | bytes 368644
  16.5 5.1 %copy-start.9 = (f32[240,128]{1,0:T(8,128)S(1)}, f32[240,128]{1,0:T(8,128)}, u32[]{:S(2)}) copy-start(f32[240,128]{1,0:T(8,128)} %constant.35.clone.t_low) | copy-start | bytes 368644
  16.5 5.1 %copy-start.14 = (f32[40,128]{1,0:T(8,128)S(1)}, f32[40,128]{1,0:T(8,128)}, u32[]{:S(2)}) copy-start(f32[40,128]{1,0:T(8,128)} %constant.38.clone.w_own) | copy-start | bytes 61444
  16.5 5.1 %copy-start.15 = (f32[40,128]{1,0:T(8,128)S(1)}, f32[40,128]{1,0:T(8,128)}, u32[]{:S(2)}) copy-start(f32[40,128]{1,0:T(8,128)} %constant.37.clone.w_low) | copy-start | bytes 61444
  16.5 10.1 %copy-start.13 = (f32[40,32]{1,0:T(8,128)S(1)}, f32[40,32]{1,0:T(8,128)}, u32[]{:S(2)}) copy-start(f32[40,32]{1,0:T(8,128)} %constant.39.clone.my) | copy-start | bytes 15364
  16.5 16.4 %copy-start.4 = (f32[256,256]{1,0:T(8,128)S(1)}, f32[256,256]{1,0:T(8,128)}, u32[]{:S(2)}) copy-start(f32[256,256]{1,0:T(8,128)} %constant.43.clone.v_high) | copy-start | bytes 786436
  16.5 16.4 %copy-start.5 = (f32[256,256]{1,0:T(8,128)S(1)}, f32[256,256]{1,0:T(8,128)}, u32[]{:S(2)}) copy-start(f32[256,256]{1,0:T(8,128)} %constant.42.clone.v_low) | copy-start | bytes 786436
  16.6 16.4 %copy-start.6 = (f32[256,256]{1,0:T(8,128)S(1)}, f32[256,256]{1,0:T(8,128)}, u32[]{:S(2)}) copy-start(f32[256,256]{1,0:T(8,128)} %constant.41.clone.v_own) | copy-start | bytes 786436
  16.6 16.4 %copy-start.12 = (f32[40,16]{1,0:T(8,128)S(1)}, f32[40,16]{1,0:T(8,128)}, u32[]{:S(2)}) copy-start(f32[40,16]{1,0:T(8,128)} %constant.40.clone.my) | copy-start | bytes 7684
  19.5 21.7 %copy-start.10 = (f32[40,128]{1,0:T(8,128)S(1)}, f32[40,128]{1,0:T(8,128)}, u32[]{:S(2)}) copy-start(f32[40,128]{1,0:T(8,128)} %constant.44.clone.my) | copy-start | bytes 61444
  23.8 4.0 %collective-permute-start.2 = (f32[12,32,256]{2,1,0:T(8,128)S(1)}, f32[12,32,256]{2,1,0:T(8,128)S(1)}, u32[]{:S(2)}, u32[]{:S(2)}) collective-permute-start(f32[12,32,256]{2,1,0:T(8,128)S(1)} %get-tuple-element.42), channel_id=1, source_target_pairs={{0,8},{8,0},{16,24},{24,16},{1,9},{9,1},{17,25},{25,17},{2,10},{10... | collective-permute-start | bytes 1179656 | tf_op jit(solution)/shard_map/ppermute | solution.py:563
  23.9 9.1 %collective-permute-start.3 = (f32[12,32,256]{2,1,0:T(8,128)S(1)}, f32[12,32,256]{2,1,0:T(8,128)S(1)}, u32[]{:S(2)}, u32[]{:S(2)}) collective-permute-start(f32[12,32,256]{2,1,0:T(8,128)S(1)} %get-tuple-element.43), channel_id=1, source_target_pairs={{8,16},{16,8},{9,17},{17,9},{10,18},{18,10},{11,19},{19,11},{12,20... | collective-permute-start | bytes 1179656 | tf_op jit(solution)/shard_map/ppermute | solution.py:563
  35.1 10.7 %collective-permute-start.4 = (f32[12,32,256]{2,1,0:T(8,128)S(1)}, f32[12,32,256]{2,1,0:T(8,128)S(1)}, u32[]{:S(2)}, u32[]{:S(2)}) collective-permute-start(f32[12,32,256]{2,1,0:T(8,128)S(1)} %get-tuple-element.50), channel_id=1, source_target_pairs={{0,32},{32,0},{64,96},{96,64},{128,160},{160,128},{192,224},{224,1... | collective-permute-start | bytes 1179656 | tf_op jit(solution)/shard_map/ppermute | solution.py:563
  35.3 11.7 %collective-permute-start.5 = (f32[12,32,256]{2,1,0:T(8,128)S(1)}, f32[12,32,256]{2,1,0:T(8,128)S(1)}, u32[]{:S(2)}, u32[]{:S(2)}) collective-permute-start(f32[12,32,256]{2,1,0:T(8,128)S(1)} %get-tuple-element.51), channel_id=1, source_target_pairs={{32,64},{64,32},{96,128},{128,96},{160,192},{192,160},{33,65},{65,... | collective-permute-start | bytes 1179656 | tf_op jit(solution)/shard_map/ppermute | solution.py:563

commit v3 on v2

--- a/solution.py
+++ b/solution.py
@@ -31,18 +31,18 @@
 
 
 def z_low_rows():
-    out = np.zeros((240, 128), np.float32)
-    for c in range(7):
-        for k in range(128):
-            out[112 + c, k] = band(k - (c - 7))
+    out = np.zeros((128, 128), np.float32)
+    for r in range(128):
+        if r % 16 < 7:
+            out[r] = [band(k - (r % 16 - 7)) for k in range(128)]
     return out
 
 
 def z_high_rows():
-    out = np.zeros((240, 128), np.float32)
-    for c in range(6):
-        for k in range(128):
-            out[112 + c, k] = band(128 + c - k)
+    out = np.zeros((128, 128), np.float32)
+    for r in range(128):
+        if r % 16 < 6:
+            out[r] = [band(128 + r % 16 - k) for k in range(128)]
     return out
 
 
@@ -73,20 +73,12 @@
     return out
 
 
-def plane_y_matrices():
-    own = np.zeros((256, 256), np.float32)
-    low = np.zeros((256, 256), np.float32)
-    high = np.zeros((256, 256), np.float32)
+def plane_y_matrix():
+    out = np.zeros((128, 128), np.float32)
     for y in range(-1, 32):
-        for l in range(32):
-            own[l, y + 1] = band(l - y)
-            low[l, y + 1] = band(l - 32 - y) if l >= 25 else 0.0
-            high[l, y + 1] = band(32 + l - y) if l < 6 else 0.0
-    for c in range(1, 5):
-        for y in range(32):
-            own[32 * c + y, 40 * c + y + 1] = 1.0
-        low[32 * c + 31, 40 * c] = 1.0
-    return own, low, high
+        for k in range(45):
+            out[k, y + 1] = band(k - 7 - y)
+    return out
 
 
 def lanes(shape):
@@ -155,9 +147,11 @@
 
 def pack_kernel(
     where_ref, strain_in, plastic_in, alpha_in, kappa_in, flags,
-    strain, plastic, alpha, kappa, z_a, z_b,
-    up_trial, up_alpha, up_drive, low_trial, low_alpha, low_drive, sems,
+    strain, plastic, alpha, kappa, turned, z_a, z_b,
+    flags_v, up_trial, up_alpha, up_drive, low_trial, low_alpha, low_drive, sems,
 ):
+    flags_copy = pltpu.make_async_copy(flags, flags_v, sems.at[CHUNKS, 0])
+    flags_copy.start()
     copies = []
     for c in range(CHUNKS):
         part = pl.ds(c * CHUNK, CHUNK)
@@ -172,11 +166,12 @@
     for group in copies:
         for copy in group:
             copy.start()
-    turned = turned_flags(flags)
+    flags_copy.wait()
+    turned[...] = turned_flags(flags_v)
     flag = jnp.concatenate(
         [
             jnp.dot(
-                turned,
+                turned[...],
                 (rows((32, 128)) == 4 * (lanes((32, 128)) // 16) + b).astype(F32),
                 preferred_element_type=F32,
             )
@@ -230,9 +225,7 @@
     by_parity(lax.rem(where_ref[2], 2) == 0, z_a, z_b, store)
 
 
-def inner_kernel(strain, plastic, alpha, kappa, flags, bz, smooth, free, yext, xext, turned, field):
-    turned[...] = turned_flags(flags)
-
+def inner_kernel(strain, plastic, alpha, kappa, turned, bz, smooth, free, yext, xext, field):
     @pl.loop(0, 8)
     def _(g):
         for i in range(4):
@@ -255,22 +248,34 @@
 
 
 def z_kernel(
-    where_ref, own, yext, sent_a, sent_b, got_a, got_b, t_low, t_high, w_low, w_own,
-    smooth, plane, y_a, y_b, z_low, z_high, own_low, head_rows, tail_rows,
+    where_ref, own, yext_in, xext_in, sent_a, sent_b, got_a, got_b, t_low, t_high, w_low, w_own,
+    plane, y_a, y_b, z_low, z_high, yext, xext,
+    own_low, head_rows, tail_rows, some_low, some_high, ends,
 ):
+    yext[...] = yext_in[...]
+    xext[...] = xext_in[...]
+
     def choose(upper, lower):
         z_high[...] = upper[0][...]
         z_low[...] = lower[0][...]
         own_low[...] = lower[1][...]
 
     by_parity(lax.rem(where_ref[2], 2) == 0, (got_a, sent_a), (got_b, sent_b), choose)
-    for g in range(8):
-        part = slice(4 * g, 4 * g + 4)
-        start = 112 - 16 * g
-        first = dot(z_low[...], t_low[start : start + 128])
-        last = dot(z_high[...], t_high[start : start + 128])
-        smooth[part, :, 0:128] = own[part, :, 0:128] + first.reshape(4, 32, 128)
-        smooth[part, :, 128:256] = own[part, :, 128:256] + last.reshape(4, 32, 128)
+    group = lanes((8, 128)) // 16
+    for half in range(2):
+        for x in range(32):
+            start = 32 * (x % 4) + 24 * half
+            at = 256 * half + 8 * x
+            inside = group == x // 4
+            for some, ref in ((some_low, z_low), (some_high, z_high)):
+                some[at : at + 8, :] = jnp.where(inside, ref[start : start + 8, :], 0.0)
+    first = dot(some_low[...], t_low[...])
+    last = dot(some_high[...], t_high[...])
+    for half in range(2):
+        part = slice(256 * half, 256 * half + 256)
+        here = slice(24 * half, 24 * half + 8)
+        ends[half, :, :, 0:128] = own[:, here, 0:128] + first[part].reshape(32, 8, 128)
+        ends[half, :, :, 128:256] = own[:, here, 128:256] + last[part].reshape(32, 8, 128)
     turned = dot_lanes(w_low[...], z_low[...]) + dot_lanes(w_own[...], own_low[...])
     lane = lanes((8, 128))
     for b in range(4):
@@ -286,18 +291,26 @@
 
     def store(upper, lower):
         for j in range(7):
-            upper[j] = smooth[:, 25 + j, :]
-        for e in range(4):
-            upper[7 + e] = yext[e]
-        upper[11] = plane[...]
+            upper[j] = ends[1, :, 1 + j, :]
+        upper[7] = plane[...]
         for j in range(6):
-            lower[j] = smooth[:, j, :]
-        lower[11] = plane[...]
+            lower[j] = ends[0, :, j, :]
+        lower[6] = plane[...]
+        lower[7] = plane[...]
 
     by_parity(lax.rem(where_ref[1], 2) == 0, y_a, y_b, store)
 
 
-def own_rows_kernel(smooth, my, out, out_face):
+def own_rows_kernel(own, z_low, z_high, t_low, t_high, my, out, out_face, some, smooth):
+    group = lanes((128, 128)) // 16
+    for half, (ref, band_rows) in enumerate(((z_low, t_low), (z_high, t_high))):
+        for g in range(8):
+            some[128 * g : 128 * g + 128, :] = jnp.where(group == g, ref[...], 0.0)
+        here = slice(128 * half, 128 * half + 128)
+        for c in range(4):
+            part = dot(some[256 * c : 256 * c + 256, :], band_rows[...])
+            at = slice(8 * c, 8 * c + 8)
+            smooth[at, :, here] = own[at, :, here] + part.reshape(8, 32, 128)
     for x in range(32):
         both = dot(my[...], smooth[x])
         out[x] = both[0:32]
@@ -305,52 +318,69 @@
 
 
 def y_kernel(
-    where_ref, own, own_face, plane, xext, got_a, got_b, my, v_own, v_low, v_high,
-    edges, out_face, out_plane, face_ext, halo, x_a, x_b, plane_low, plane_high,
+    where_ref, own, own_face, plane, got_a, got_b, face_ext, _, my, v,
+    edges, out_face, out_plane, halo, x_a, x_b, plane_low, plane_high,
 ):
     def choose(upper, lower):
         for j in range(7):
             halo[:, j, :] = lower[j]
         for j in range(6):
             halo[:, 8 + j, :] = upper[j]
-        for e in range(4):
-            face_ext[e] = lower[7 + e]
-        plane_low[...] = lower[11]
-        plane_high[...] = upper[11]
+        plane_low[...] = lower[7]
+        plane_high[...] = upper[7]
 
     halo[:, 0:8, :] = jnp.zeros((32, 8, 256), F32)
     halo[:, 8:16, :] = jnp.zeros((32, 8, 256), F32)
     by_parity(lax.rem(where_ref[1], 2) == 0, got_a, got_b, choose)
-    for x in range(32):
-        if x < 8 or x >= 24:
-            both = dot(my[...], halo[x])
-            edges[x if x < 8 else x - 16] = own[x] + both[0:32]
-            out_face[x : x + 1, :] = own_face[x : x + 1, :] + both[32:33]
-        else:
-            both = dot(my[32:40, :], halo[x])
-            out_face[x : x + 1, :] = own_face[x : x + 1, :] + both[0:1]
-    total = dot(plane[...], v_own[...])
-    total += dot(plane_low[...], v_low[...])
-    total += dot(plane_high[...], v_high[...])
-    out_plane[...] = total
+    out_face[8:24, :] = own_face[8:24, :]
+    for i in range(16):
+        x = i if i < 8 else i + 16
+        both = dot(my[...], halo[x])
+        edges[i] = own[x] + both[0:32]
+        out_face[x : x + 1, :] = own_face[x : x + 1, :] + both[32:33]
+    mine, low, high = plane[...], plane_low[...], plane_high[...]
+    lane = lanes((32, 256))
+    total = jnp.zeros((32, 256), F32)
+    for c in range(1, 5):
+        inside = (lane > 40 * c) & (lane <= 40 * c + 32)
+        total = jnp.where(inside, pltpu.roll(mine, 8 * c + 1, 1), total)
+        total = jnp.where(lane == 40 * c, pltpu.roll(low, (8 * c - 31) % 256, 1), total)
+    wide = jnp.where(
+        lane < 7,
+        pltpu.roll(low, 256 - 25, 1),
+        jnp.where(lane < 39, pltpu.roll(mine, 7, 1), jnp.where(lane < 45, pltpu.roll(high, 39, 1), 0.0)),
+    )
+    smoothed = dot(wide[:, 0:128], v[...])
+    out_plane[:, 0:128] = jnp.where(lanes((32, 128)) < 40, smoothed, total[:, 0:128])
+    out_plane[:, 128:256] = total[:, 128:256]
 
     def store(upper, lower):
         for j in range(7):
             upper[j] = edges[9 + j]
+        upper[7] = jnp.zeros((32, 256), F32)
+        upper[7, 0:8, :] = out_face[24:32, :]
         for e in range(4):
-            upper[7 + e] = xext[e]
-        upper[11] = jnp.zeros((32, 256), F32)
-        upper[11, 0:8, :] = out_face[24:32, :]
-        for e in range(4):
-            upper[11, 8 + e : 9 + e, :] = face_ext[e, 31:32, :]
-        upper[11, 16:24, :] = out_plane[24:32, :]
+            corner = face_ext[e, 31:32, :]
+            upper[7, 8 + e : 9 + e, :] = jnp.where(where_ref[1] == 0, 0.0, corner)
+        upper[7, 16:24, :] = out_plane[24:32, :]
         for j in range(6):
             lower[j] = edges[j]
-        lower[11] = jnp.zeros((32, 256), F32)
-        lower[11, 0:8, :] = out_face[0:8, :]
-        lower[11, 16:24, :] = out_plane[0:8, :]
+        lower[6] = jnp.zeros((32, 256), F32)
+        lower[7] = jnp.zeros((32, 256), F32)
+        lower[7, 0:8, :] = out_face[0:8, :]
+        lower[7, 16:24, :] = out_plane[0:8, :]
 
     by_parity(lax.rem(where_ref[0], 2) == 0, x_a, x_b, store)
+
+
+def fill_side(at, side, face_ext):
+    for e in range(4):
+        side[e, 0:32, :] = face_ext[e]
+        side[e, 32:40, :] = jnp.zeros((8, 256), F32)
+
+    @pl.when(at[1] == 0)
+    def _():
+        side[...] = jnp.zeros_like(side)
 
 
 def faces(extents, at, mx, face_all, plane_all, side, face_e, face_a, column, inv_x, inv_yz):
@@ -424,7 +454,7 @@
 
 def middle_kernel(
     extents, where_ref, strain, free, kappa, own, edges, halo, face, plane, face_ext, my,
-    force, kappa_new, part,
+    force, kappa_new, part, face_out,
     ext, face_all, plane_all, side, before, face_e, face_a, column, inv_x, inv_yz,
     force_v, kappa_v, sems,
 ):
@@ -435,14 +465,16 @@
         elif x >= 24:
             ext[x] = edges[x - 16]
         else:
-            ext[x] = own[x] + dot(my[:, 32:48][0:32], halo[x])
-    for ref, value in ((face_all, face), (plane_all, plane)):
+            both = dot(my[:, 32:48], halo[x])
+            ext[x] = own[x] + both[0:32]
+            face_out[x : x + 1, :] = face[x : x + 1, :] + both[32:33]
+    face_out[0:8, :] = face[0:8, :]
+    face_out[24:32, :] = face[24:32, :]
+    for ref, value in ((face_all, face_out), (plane_all, plane)):
         ref[0:8, :] = jnp.zeros((8, 256), F32)
         ref[8:40, :] = value[...]
         ref[40:48, :] = jnp.zeros((8, 256), F32)
-    for e in range(4):
-        side[e, 0:32, :] = face_ext[e]
-        side[e, 32:40, :] = jnp.zeros((8, 256), F32)
+    fill_side(at, side, face_ext)
     faces(
         extents, at, my.at[:, 48:96], face_all, plane_all, side,
         face_e, face_a, column, inv_x, inv_yz,
@@ -485,7 +517,7 @@
 
 
 def outer_kernel(
-    extents, where_ref, strain, free, kappa, part, face, plane, face_ext, got_a, got_b, my,
+    extents, where_ref, strain, free, kappa, part, face, plane, face_ext, got_a, got_b, got_ext, my,
     force_in, kappa_in,
     force, kappa_new,
     low, high, face_all, plane_all, side, before, face_e, face_a, column, inv_x, inv_yz,
@@ -498,18 +530,32 @@
             low[j] = lower[j]
         for j in range(6):
             high[j] = upper[j]
-        face_all[0:8, :] = lower[11, 0:8, :]
-        face_all[40:48, :] = upper[11, 0:8, :]
-        plane_all[0:8, :] = lower[11, 16:24, :]
-        plane_all[40:48, :] = upper[11, 16:24, :]
+        face_all[0:8, :] = lower[7, 0:8, :]
+        face_all[40:48, :] = upper[7, 0:8, :]
+        plane_all[0:8, :] = lower[7, 16:24, :]
+        plane_all[40:48, :] = upper[7, 16:24, :]
         for e in range(4):
-            side[e, 32:33, :] = lower[11, 8 + e : 9 + e, :]
-            before[e] = lower[7 + e]
-
-    for e in range(4):
-        side[e, 0:32, :] = face_ext[e]
-        side[e, 32:40, :] = jnp.zeros((8, 256), F32)
+            side[e, 32:33, :] = lower[7, 8 + e : 9 + e, :]
+
+    fill_side(at, side, face_ext)
     by_parity(lax.rem(at[0], 2) == 0, got_a, got_b, choose)
+    before[...] = got_ext[...]
+
+    @pl.when(at[0] == 0)
+    def _():
+        low[...] = jnp.zeros_like(low)
+        before[...] = jnp.zeros_like(before)
+        face_all[0:8, :] = jnp.zeros((8, 256), F32)
+        plane_all[0:8, :] = jnp.zeros((8, 256), F32)
+        for e in range(4):
+            side[e, 32:33, :] = jnp.zeros((1, 256), F32)
+
+    @pl.when(at[0] == extents[0] // 32 - 1)
+    def _():
+        high[...] = jnp.zeros_like(high)
+        face_all[40:48, :] = jnp.zeros((8, 256), F32)
+        plane_all[40:48, :] = jnp.zeros((8, 256), F32)
+
     face_all[8:40, :] = face[...]
     plane_all[8:40, :] = plane[...]
     faces(
@@ -551,16 +597,23 @@
         copy.wait()
 
 
-def swap(first, second, axis):
+def swap(first, second, axis, around=False):
     count = lax.axis_size(axis)
 
     def route(start):
         out = []
         for i in range(start, count - 1, 2):
             out += [(i, i + 1), (i + 1, i)]
+        if start and around:
+            out += [(count - 1, 0), (0, count - 1)]
         return out
 
     return lax.ppermute(first, axis, route(0)), lax.ppermute(second, axis, route(1))
+
+
+def to_next(block, axis):
+    count = lax.axis_size(axis)
+    return lax.ppermute(block, axis, [(i, (i + 1) % count) for i in range(count)])
 
 
 def shape_of(*dims):
@@ -607,70 +660,79 @@
     rows_three[:, 32:48] = rows_halo
     rows_three[:, 48:96] = rows_all
 
-    strain, plastic, alpha, kappa, z_a, z_b = call(
+    whole_in = [
+        pltpu.with_memory_space_constraint(v, pltpu.HBM)
+        for v in (strain_in, plastic_in, alpha_in, kappa_in, flags)
+    ]
+    ends, eight = shape_of(4, 32, 256), shape_of(8, 32, 256)
+    square = shape_of(128, 128)
+    strain, plastic, alpha, kappa, turned, z_a, z_b = call(
         pack_kernel,
         "pack",
-        [SM, HBM, HBM, HBM, HBM, VM],
-        [shape_of(3, 32, 32, 256), BLOCK, BLOCK, BLOCK, shape_of(128, 128), shape_of(128, 128)],
-        scratch=[vmem(128, 128)] * 6 + [pltpu.SemaphoreType.DMA((CHUNKS, 4))],
-    )(where, strain_in, plastic_in, alpha_in, kappa_in, flags)
+        [SM] + [HBM] * 5,
+        [shape_of(3, 32, 32, 256), BLOCK, BLOCK, BLOCK, shape_of(32, 32), square, square],
+        scratch=[pltpu.VMEM((32, 32), jnp.int32)] + [vmem(128, 128)] * 6
+        + [pltpu.SemaphoreType.DMA((CHUNKS + 1, 4))],
+    )(where, *whole_in)
     got_a, got_b = swap(z_a, z_b, "gz")
     own, free, yext, xext = call(
-        inner_kernel,
-        "inner",
-        [VM] * 6,
-        [BLOCK, BLOCK, shape_of(4, 32, 256), shape_of(4, 32, 256)],
-        scratch=[vmem(32, 32), vmem(32, 32, 256)],
-    )(strain, plastic, alpha, kappa, flags, z_band(256))
-
-    smooth, plane, y_a, y_b = call(
+        inner_kernel, "inner", [VM] * 6, [BLOCK, BLOCK, ends, ends], scratch=[vmem(32, 32, 256)]
+    )(strain, plastic, alpha, kappa, turned, z_band(256))
+    t_low, t_high = z_low_rows(), z_high_rows()
+    plane, y_a, y_b, z_low, z_high, yext, xext = call(
         z_kernel,
         "along_z",
-        [SM] + [VM] * 10,
-        [BLOCK, FACE, shape_of(12, 32, 256), shape_of(12, 32, 256)],
-        scratch=[vmem(128, 128)] * 3 + [vmem(32, 128)] * 2,
+        [SM] + [VM] * 11,
+        [FACE, eight, eight, square, square, ends, ends],
+        scratch=[vmem(128, 128)] + [vmem(32, 128)] * 2 + [vmem(512, 128)] * 2
+        + [vmem(2, 32, 8, 256)],
     )(
-        where, own, yext, z_a, z_b, got_a, got_b,
-        z_low_rows(), z_high_rows(), plane_from_low(), plane_from_own(),
+        where, own, yext, xext, z_a, z_b, got_a, got_b,
+        t_low, t_high, plane_from_low(), plane_from_own(),
     )
     got_a, got_b = swap(y_a, y_b, "gy")
-    own, own_face = call(own_rows_kernel, "own_rows", [VM] * 2, [BLOCK, FACE])(smooth, rows_own)
-
-    edges, face, plane, face_ext, halo, x_a, x_b = call(
+    face_ext = to_next(yext, "gy")
+    got_ext = to_next(xext, "gx")
+    own, own_face = call(
+        own_rows_kernel,
+        "own_rows",
+        [VM] * 6,
+        [BLOCK, FACE],
+        scratch=[vmem(1024, 128), vmem(32, 32, 256)],
+    )(own, z_low, z_high, t_low, t_high, rows_own)
+
+    edges, face, plane, halo, x_a, x_b = call(
         y_kernel,
         "along_y",
-        [SM] + [VM] * 10,
-        [
-            shape_of(16, 32, 256), FACE, FACE, shape_of(4, 32, 256), shape_of(32, 16, 256),
-            shape_of(12, 32, 256), shape_of(12, 32, 256),
-        ],
+        [SM] + [VM] * 9,
+        [shape_of(16, 32, 256), FACE, FACE, shape_of(32, 16, 256), eight, eight],
         scratch=[vmem(32, 256), vmem(32, 256)],
-    )(where, own, own_face, plane, xext, got_a, got_b, rows_halo, *plane_y_matrices())
-    got_a, got_b = swap(x_a, x_b, "gx")
+    )(where, own, own_face, plane, got_a, got_b, face_ext, got_ext, rows_halo, plane_y_matrix())
+    got_a, got_b = swap(x_a, x_b, "gx", around=True)
 
     shared = [
         vmem(48, 256), vmem(48, 256), vmem(4, 40, 256), vmem(4, 32, 256),
         vmem(32, 256), vmem(32, 256), vmem(32, 128), vmem(40, 256), vmem(32, 256),
         vmem(16, 32, 256), vmem(16, 32, 256), pltpu.SemaphoreType.DMA((2, 2)),
     ]
-    force, kappa_new, part = call(
+    force, kappa_new, part, face = call(
         functools.partial(middle_kernel, extents),
         "middle",
         [SM] + [VM] * 10,
-        [BLOCK, BLOCK, shape_of(18, 32, 256)],
-        out_specs=[HBM, HBM, VM],
+        [BLOCK, BLOCK, shape_of(18, 32, 256), FACE],
+        out_specs=[HBM, HBM, VM, VM],
         scratch=[vmem(32, 32, 256)] + shared,
     )(where, strain, free, kappa, own, edges, halo, face, plane, face_ext, rows_three)
     force, kappa_new = call(
         functools.partial(outer_kernel, extents),
         "outer",
-        [SM] + [VM] * 10 + [HBM, HBM],
+        [SM] + [VM] * 11 + [HBM, HBM],
         [BLOCK, BLOCK],
         out_specs=[HBM, HBM],
         scratch=[vmem(7, 32, 256), vmem(6, 32, 256)] + shared,
-        input_output_aliases={11: 0, 12: 1},
+        input_output_aliases={12: 0, 13: 1},
     )(
-        where, strain, free, kappa, part, face, plane, face_ext, got_a, got_b, rows_three,
+        where, strain, free, kappa, part, face, plane, face_ext, got_a, got_b, got_ext, rows_three,
         force, kappa_new,
     )
     return (force, kappa_new)

time: 50.2 us -> 45.5 us (0.906)
  the two profiles are of different devices: /device:TPU:120 before, /device:TPU:16 now
where the time goes in v3:
time: 45.5 us; the launch traced here: 45.3 us
  Pallas kernels  19.4 us (43%)
  starting transfers between devices  13.7 us (30%)
  waiting for transfers between devices  11.2 us (25%)
  between operations  0.83 us (2%)
    ppermute x3, starting transfers between devices, swap(): lax.ppermute(second, axis, route(1))  7.26 us
    ppermute x2, waiting for transfers between devices, to_next(): lax.ppermute(block, axis, [(i, (i + 1) % count) for i in range(count)])  6.11 us
    pallas_call x1, Pallas kernels, body(): call(functools.partial(middle_kernel, extents), 'middle', [SM] + [VM] * 1...  4.84 us
    ppermute x2, starting transfers between devices, to_next(): lax.ppermute(block, axis, [(i, (i + 1) % count) for i in range(count)])  4.73 us
    ppermute x3, waiting for transfers between devices, swap(): lax.ppermute(second, axis, route(1))  4.45 us
    pallas_call x1, Pallas kernels, body(): call(pack_kernel, 'pack', [SM] + [HBM] * 5, [shape_of(3, 32, 32, 256), BL...  3.92 us
    pallas_call x1, Pallas kernels, body(): call(functools.partial(outer_kernel, extents), 'outer', [SM] + [VM] * 11...  2.77 us
    pallas_call x1, Pallas kernels, body(): call(inner_kernel, 'inner', [VM] * 6, [BLOCK, BLOCK, ends, ends], scratch...  2.73 us
  transfers between devices with their start and end apart: 8, of which 4 were waited for; matrix products, arithmetic and copies ran while one was open for 0% of the time, Pallas kernels for 21%

profile of v3, /device:TPU:16, one launch (start us, length us, event | category | flops | bytes accessed | tf_op | source)
XLA Modules:
  0.0 45.3 jit_solution(18132039589798715130)
XLA Ops:
  0.6 0.1 pad_add_fusion.where_ref
  0.7 0.0 copy-start
  0.7 3.9 %pack.1 = (f32[3,32,32,256]{3,2,1,0:T(8,128)S(1)}, f32[32,32,256]{2,1,0:T(8,128)S(1)}, f32[32,32,256]{2,1,0:T(8,128)S(1)}, f32[32,32,256]{2,1,0:T(8,128)S(1)}, f...) custom-call(s32[3]{0:T(128)S(1)} %pad_add_fusion.where_ref, f32[3,32,32,256]{3,2,1,0:T(8,128)} %strain_in.1, ...), custom_call_target="tpu_custom_call" | custom-call | tf_op jit(solution)/shard_map/pack/pallas_call | solution.py:669
  4.6 1.6 %collective-permute-start = (f32[128,128]{1,0:T(8,128)S(1)}, f32[128,128]{1,0:T(8,128)S(1)}, u32[]{:S(2)}, u32[]{:S(2)}) collective-permute-start(f32[128,128]{1,0:T(8,128)S(1)} %get-tuple-element.41.sent_a), channel_id=1, source_target_pairs={{0,1},{1,0},{2,3},{3,2},{4,5},{5,4},{6,7},{7,6},{8,9},{9,8},{10,11... | collective-permute-start | bytes 196616 | tf_op jit(solution)/shard_map/ppermute | solution.py:611
  6.2 3.8 %collective-permute-start.1 = (f32[128,128]{1,0:T(8,128)S(1)}, f32[128,128]{1,0:T(8,128)S(1)}, u32[]{:S(2)}, u32[]{:S(2)}) collective-permute-start(f32[128,128]{1,0:T(8,128)S(1)} %get-tuple-element.42.sent_b), channel_id=1, source_target_pairs={{1,2},{2,1},{3,4},{4,3},{5,6},{6,5},{9,10},{10,9},{11,12},{12,11},... | collective-permute-start | bytes 196616 | tf_op jit(solution)/shard_map/ppermute | solution.py:611
  10.0 0.0 copy-done
  10.0 0.0 copy-start.1
  10.0 0.0 copy-start.2
  10.0 0.0 copy-start.6
  10.0 0.0 copy-start.7
  10.1 0.0 copy-start.8
  10.1 0.0 copy-start.4
  10.1 0.0 copy-start.5
  10.1 2.7 %inner.1 = (f32[32,32,256]{2,1,0:T(8,128)S(1)}, f32[32,32,256]{2,1,0:T(8,128)S(1)}, f32[4,32,256]{2,1,0:T(8,128)S(1)}, f32[4,32,256]{2,1,0:T(8,128)S(1)}) custom-call(f32[3,32,32,256]{3,2,1,0:T(8,128)S(1)} %get-tuple-element.32.strain, f32[32,32,256]{2,1,0:T(8,128)S(1)} %get-tuple-element.33.plastic, f32[32,32,256]{2,1,0:T(8,128)S(1)} %get-tuple-element.34.alpha, ...), custom_call_target="tpu_custom_call" | custom-call | tf_op jit(solution)/shard_map/inner/pallas_call | solution.py:678
  12.8 0.0 copy-start.3
  12.8 0.0 collective-permute-done.got_a
  12.8 3.1 %collective-permute-done.1.got_b = f32[128,128]{1,0:T(8,128)S(1)} collective-permute-done((f32[128,128]{1,0:T(8,128)S(1)}, f32[128,128]{1,0:T(8,128)S(1)}, u32[]{:S(2)}, u32[]{:S(2)}) %collective-permute-start.1) | collective-permute-done | bytes 65568 | tf_op jit(solution)/shard_map/ppermute | solution.py:611
  16.0 0.0 copy-done.1
  16.0 0.0 copy-done.2
  16.0 0.0 copy-done.6
  16.0 0.0 copy-done.7
  16.0 1.6 %along_z.1 = (f32[32,256]{1,0:T(8,128)S(1)}, f32[8,32,256]{2,1,0:T(8,128)S(1)}, f32[8,32,256]{2,1,0:T(8,128)S(1)}, f32[128,128]{1,0:T(8,128)S(1)}, f32[128,128]{...) custom-call(s32[3]{0:T(128)S(1)} %pad_add_fusion.where_ref, ...), custom_call_target="tpu_custom_call" | custom-call | tf_op jit(solution)/shard_map/along_z/pallas_call | solution.py:682
  17.6 0.1 collective-permute-start.2
  17.7 0.7 %collective-permute-start.3 = (f32[8,32,256]{2,1,0:T(8,128)S(1)}, f32[8,32,256]{2,1,0:T(8,128)S(1)}, u32[]{:S(2)}, u32[]{:S(2)}) collective-permute-start(f32[8,32,256]{2,1,0:T(8,128)S(1)} %get-tuple-element.49), channel_id=1, source_target_pairs={{8,16},{16,8},{9,17},{17,9},{10,18},{18,10},{11,19},{19,11},{12,20... | collective-permute-start | bytes 786440 | tf_op jit(solution)/shard_map/ppermute | solution.py:611
  18.4 2.7 %collective-permute-start.4 = (f32[4,32,256]{2,1,0:T(8,128)S(1)}, f32[4,32,256]{2,1,0:T(8,128)S(1)}, u32[]{:S(2)}, u32[]{:S(2)}) collective-permute-start(f32[4,32,256]{2,1,0:T(8,128)S(1)} %get-tuple-element.50), channel_id=1, source_target_pairs={{0,8},{8,16},{16,24},{24,0},{1,9},{9,17},{17,25},{25,1},{2,10},{10... | collective-permute-start | bytes 393224 | tf_op jit(solution)/shard_map/ppermute | solution.py:616
  21.1 2.0 %collective-permute-start.5 = (f32[4,32,256]{2,1,0:T(8,128)S(1)}, f32[4,32,256]{2,1,0:T(8,128)S(1)}, u32[]{:S(2)}, u32[]{:S(2)}) collective-permute-start(f32[4,32,256]{2,1,0:T(8,128)S(1)} %get-tuple-element.51), channel_id=1, source_target_pairs={{0,32},{32,64},{64,96},{96,128},{128,160},{160,192},{192,224},{224... | collective-permute-start | bytes 393224 | tf_op jit(solution)/shard_map/ppermute | solution.py:616
  23.1 0.0 copy-done.8
  23.1 2.1 %own_rows.1 = (f32[32,32,256]{2,1,0:T(8,128)S(1)}, f32[32,256]{1,0:T(8,128)S(1)}) custom-call(f32[32,32,256]{2,1,0:T(8,128)S(1)} %get-tuple-element.38.own, f32[128,128]{1,0:T(8,128)S(1)} %get-tuple-element.43.z_low, f32[128,128]{1,0:T(8,128)S(1)} %get-tuple-element.44.z_high, f32[128,128]{1,0:T(8,128)S(1)} %copy-done.2, f32[128,128]{1,0:T(8,128)S(1)} %copy-done.1, ...), custom_call_target="tpu_custom_call" | custom-call | tf_op jit(solution)/shard_map/own_rows/pallas_call | solution.py:696
  25.2 0.0 collective-permute-done.4.face_ext
  25.2 6.1 %collective-permute-done.5._.got_ext = f32[4,32,256]{2,1,0:T(8,128)S(1)} collective-permute-done((f32[4,32,256]{2,1,0:T(8,128)S(1)}, f32[4,32,256]{2,1,0:T(8,128)S(1)}, u32[]{:S(2)}, u32[]{:S(2)}) %collective-permute-start.5) | collective-permute-done | bytes 131104 | tf_op jit(solution)/shard_map/ppermute | solution.py:616
  31.3 0.0 collective-permute-done.2.got_a
  31.3 0.0 collective-permute-done.3.got_b
  31.3 0.0 copy-done.4
  31.3 0.0 copy-done.5
  31.4 1.5 %along_y.1 = (f32[16,32,256]{2,1,0:T(8,128)S(1)}, f32[32,256]{1,0:T(8,128)S(1)}, f32[32,256]{1,0:T(8,128)S(1)}, f32[32,16,256]{2,1,0:T(8,128)S(1)}, f32[8,32,256...) custom-call(s32[3]{0:T(128)S(1)} %pad_add_fusion.where_ref, f32[32,32,256]{2,1,0:T(8,128)S(1)} %get-tuple-element.45.own, ...), custom_call_target="tpu_custom_call" | custom-call | tf_op jit(solution)/shard_map/along_y/pallas_call | solution.py:704
  32.8 0.1 collective-permute-start.6
  33.0 2.8 %collective-permute-start.7 = (f32[8,32,256]{2,1,0:T(8,128)S(1)}, f32[8,32,256]{2,1,0:T(8,128)S(1)}, u32[]{:S(2)}, u32[]{:S(2)}) collective-permute-start(f32[8,32,256]{2,1,0:T(8,128)S(1)} %get-tuple-element.59), channel_id=1, source_target_pairs={{32,64},{64,32},{96,128},{128,96},{160,192},{192,160},{224,0},{0,2... | collective-permute-start | bytes 786440 | tf_op jit(solution)/shard_map/ppermute | solution.py:611
  35.8 0.0 copy-done.3
  35.8 4.8 %middle.1 = (f32[32,32,256]{2,1,0:T(8,128)}, f32[32,32,256]{2,1,0:T(8,128)}, f32[18,32,256]{2,1,0:T(8,128)S(1)}, f32[32,256]{1,0:T(8,128)S(1)}) custom-call(s32[3]{0:T(128)S(1)} %pad_add_fusion.where_ref, f32[3,32,32,256]{3,2,1,0:T(8,128)S(1)} %get-tuple-element.32.strain, f32[32,32,256]{2,1,0:T(8,128)S(1)} %get-tuple-element.37.free, ...), custom_call_target="tpu_custom_call" | custom-call | tf_op jit(solution)/shard_map/middle/pallas_call | solution.py:718
  40.6 0.7 %collective-permute-done.6.got_a = f32[8,32,256]{2,1,0:T(8,128)S(1)} collective-permute-done((f32[8,32,256]{2,1,0:T(8,128)S(1)}, f32[8,32,256]{2,1,0:T(8,128)S(1)}, u32[]{:S(2)}, u32[]{:S(2)}) %collective-permute-start.6) | collective-permute-done | bytes 262176 | tf_op jit(solution)/shard_map/ppermute | solution.py:611
  41.3 1.3 %collective-permute-done.7.got_b = f32[8,32,256]{2,1,0:T(8,128)S(1)} collective-permute-done((f32[8,32,256]{2,1,0:T(8,128)S(1)}, f32[8,32,256]{2,1,0:T(8,128)S(1)}, u32[]{:S(2)}, u32[]{:S(2)}) %collective-permute-start.7) | collective-permute-done | bytes 262176 | tf_op jit(solution)/shard_map/ppermute | solution.py:611
  42.6 2.8 %outer.1 = (f32[32,32,256]{2,1,0:T(8,128)}, f32[32,32,256]{2,1,0:T(8,128)}) custom-call(s32[3]{0:T(128)S(1)} %pad_add_fusion.where_ref, f32[3,32,32,256]{3,2,1,0:T(8,128)S(1)} %get-tuple-element.32.strain, f32[32,32,256]{2,1,0:T(8,128)S(1)} %get-tuple-element.37.free, ...), custom_call_target="tpu_custom_call", output_to_operand_aliasing={{0}: (12, {}), {1}: (13, {})} | custom-call | tf_op jit(solution)/shard_map/outer/pallas_call | solution.py:726
Async XLA Ops:
  0.7 9.3 %copy-start = (f32[256,256]{1,0:T(8,128)S(1)}, f32[256,256]{1,0:T(8,128)}, u32[]{:S(2)}) copy-start(f32[256,256]{1,0:T(8,128)} %constant.30.clone.bz) | copy-start | bytes 786436
  4.6 8.2 %collective-permute-start = (f32[128,128]{1,0:T(8,128)S(1)}, f32[128,128]{1,0:T(8,128)S(1)}, u32[]{:S(2)}, u32[]{:S(2)}) collective-permute-start(f32[128,128]{1,0:T(8,128)S(1)} %get-tuple-element.41.sent_a), channel_id=1, source_target_pairs={{0,1},{1,0},{2,3},{3,2},{4,5},{5,4},{6,7},{7,6},{8,9},{9,8},{10,11... | collective-permute-start | bytes 196616 | tf_op jit(solution)/shard_map/ppermute | solution.py:611
  6.2 9.8 %collective-permute-start.1 = (f32[128,128]{1,0:T(8,128)S(1)}, f32[128,128]{1,0:T(8,128)S(1)}, u32[]{:S(2)}, u32[]{:S(2)}) collective-permute-start(f32[128,128]{1,0:T(8,128)S(1)} %get-tuple-element.42.sent_b), channel_id=1, source_target_pairs={{1,2},{2,1},{3,4},{4,3},{5,6},{6,5},{9,10},{10,9},{11,12},{12,11},... | collective-permute-start | bytes 196616 | tf_op jit(solution)/shard_map/ppermute | solution.py:611
  10.0 6.0 %copy-start.1 = (f32[128,128]{1,0:T(8,128)S(1)}, f32[128,128]{1,0:T(8,128)}, u32[]{:S(2)}) copy-start(f32[128,128]{1,0:T(8,128)} %constant.32.clone.t_high) | copy-start | bytes 196612
  10.0 6.0 %copy-start.2 = (f32[128,128]{1,0:T(8,128)S(1)}, f32[128,128]{1,0:T(8,128)}, u32[]{:S(2)}) copy-start(f32[128,128]{1,0:T(8,128)} %constant.31.clone.t_low) | copy-start | bytes 196612
  10.0 6.0 %copy-start.6 = (f32[40,128]{1,0:T(8,128)S(1)}, f32[40,128]{1,0:T(8,128)}, u32[]{:S(2)}) copy-start(f32[40,128]{1,0:T(8,128)} %constant.34.clone.w_own) | copy-start | bytes 61444
  10.0 6.0 %copy-start.7 = (f32[40,128]{1,0:T(8,128)S(1)}, f32[40,128]{1,0:T(8,128)}, u32[]{:S(2)}) copy-start(f32[40,128]{1,0:T(8,128)} %constant.33.clone.w_low) | copy-start | bytes 61444
  10.1 13.0 %copy-start.8 = (f32[40,32]{1,0:T(8,128)S(1)}, f32[40,32]{1,0:T(8,128)}, u32[]{:S(2)}) copy-start(f32[40,32]{1,0:T(8,128)} %constant.35.clone.my) | copy-start | bytes 15364
  10.1 21.3 %copy-start.4 = (f32[128,128]{1,0:T(8,128)S(1)}, f32[128,128]{1,0:T(8,128)}, u32[]{:S(2)}) copy-start(f32[128,128]{1,0:T(8,128)} %constant.37.clone.v) | copy-start | bytes 196612
  10.1 21.3 %copy-start.5 = (f32[40,16]{1,0:T(8,128)S(1)}, f32[40,16]{1,0:T(8,128)}, u32[]{:S(2)}) copy-start(f32[40,16]{1,0:T(8,128)} %constant.36.clone.my) | copy-start | bytes 7684
  12.8 22.9 %copy-start.3 = (f32[40,128]{1,0:T(8,128)S(1)}, f32[40,128]{1,0:T(8,128)}, u32[]{:S(2)}) copy-start(f32[40,128]{1,0:T(8,128)} %constant.38.clone.my) | copy-start | bytes 61444
  17.6 13.8 %collective-permute-start.2 = (f32[8,32,256]{2,1,0:T(8,128)S(1)}, f32[8,32,256]{2,1,0:T(8,128)S(1)}, u32[]{:S(2)}, u32[]{:S(2)}) collective-permute-start(f32[8,32,256]{2,1,0:T(8,128)S(1)} %get-tuple-element.48), channel_id=1, source_target_pairs={{0,8},{8,0},{16,24},{24,16},{1,9},{9,1},{17,25},{25,17},{2,10},{10... | collective-permute-start | bytes 786440 | tf_op jit(solution)/shard_map/ppermute | solution.py:611
  17.7 13.7 %collective-permute-start.3 = (f32[8,32,256]{2,1,0:T(8,128)S(1)}, f32[8,32,256]{2,1,0:T(8,128)S(1)}, u32[]{:S(2)}, u32[]{:S(2)}) collective-permute-start(f32[8,32,256]{2,1,0:T(8,128)S(1)} %get-tuple-element.49), channel_id=1, source_target_pairs={{8,16},{16,8},{9,17},{17,9},{10,18},{18,10},{11,19},{19,11},{12,20... | collective-permute-start | bytes 786440 | tf_op jit(solution)/shard_map/ppermute | solution.py:611
  18.4 6.9 %collective-permute-start.4 = (f32[4,32,256]{2,1,0:T(8,128)S(1)}, f32[4,32,256]{2,1,0:T(8,128)S(1)}, u32[]{:S(2)}, u32[]{:S(2)}) collective-permute-start(f32[4,32,256]{2,1,0:T(8,128)S(1)} %get-tuple-element.50), channel_id=1, source_target_pairs={{0,8},{8,16},{16,24},{24,0},{1,9},{9,17},{17,25},{25,1},{2,10},{10... | collective-permute-start | bytes 393224 | tf_op jit(solution)/shard_map/ppermute | solution.py:616
  21.1 10.3 %collective-permute-start.5 = (f32[4,32,256]{2,1,0:T(8,128)S(1)}, f32[4,32,256]{2,1,0:T(8,128)S(1)}, u32[]{:S(2)}, u32[]{:S(2)}) collective-permute-start(f32[4,32,256]{2,1,0:T(8,128)S(1)} %get-tuple-element.51), channel_id=1, source_target_pairs={{0,32},{32,64},{64,96},{96,128},{128,160},{160,192},{192,224},{224... | collective-permute-start | bytes 393224 | tf_op jit(solution)/shard_map/ppermute | solution.py:616
  32.8 8.4 %collective-permute-start.6 = (f32[8,32,256]{2,1,0:T(8,128)S(1)}, f32[8,32,256]{2,1,0:T(8,128)S(1)}, u32[]{:S(2)}, u32[]{:S(2)}) collective-permute-start(f32[8,32,256]{2,1,0:T(8,128)S(1)} %get-tuple-element.58), channel_id=1, source_target_pairs={{0,32},{32,0},{64,96},{96,64},{128,160},{160,128},{192,224},{224,1... | collective-permute-start | bytes 786440 | tf_op jit(solution)/shard_map/ppermute | solution.py:611
  33.0 9.6 %collective-permute-start.7 = (f32[8,32,256]{2,1,0:T(8,128)S(1)}, f32[8,32,256]{2,1,0:T(8,128)S(1)}, u32[]{:S(2)}, u32[]{:S(2)}) collective-permute-start(f32[8,32,256]{2,1,0:T(8,128)S(1)} %get-tuple-element.59), channel_id=1, source_target_pairs={{32,64},{64,32},{96,128},{128,96},{160,192},{192,160},{224,0},{0,2... | collective-permute-start | bytes 786440 | tf_op jit(solution)/shard_map/ppermute | solution.py:611

commit v4 on v3

--- a/solution.py
+++ b/solution.py
@@ -147,7 +147,7 @@
 
 def pack_kernel(
     where_ref, strain_in, plastic_in, alpha_in, kappa_in, flags,
-    strain, plastic, alpha, kappa, turned, z_a, z_b,
+    strain, plastic, alpha, kappa, turned, z_a, z_b, yext, xext,
     flags_v, up_trial, up_alpha, up_drive, low_trial, low_alpha, low_drive, sems,
 ):
     flags_copy = pltpu.make_async_copy(flags, flags_v, sems.at[CHUNKS, 0])
@@ -208,6 +208,17 @@
             place(low_alpha, tile(alpha, 0), 0)
             place(low_drive, field_of(s0, s1, s2), 0)
 
+    trial = strain[0, 31] - plastic[31]
+    here = (rows((32, 256)) == 31).astype(F32)
+    flag_x = jnp.dot(turned[...], here, preferred_element_type=F32)
+    xext[0] = trial - newton_plastic(trial, alpha[31]) * flag_x
+    trial = strain[0, :, 31, :] - plastic[:, 31, :]
+    flag_y = jnp.broadcast_to(flags_v[:, 31:32].astype(F32), (32, 256))
+    yext[0] = trial - newton_plastic(trial, alpha[:, 31, :]) * flag_y
+    for e, ref in enumerate((strain.at[1], strain.at[2], kappa)):
+        xext[1 + e] = ref[31]
+        yext[1 + e] = ref[:, 31, :]
+
     increment = newton_plastic(up_trial[...], up_alpha[...]) * flag
     free = pltpu.roll(up_trial[...] - increment, 1, 1)
     up_drive[...] = jnp.where(
@@ -225,7 +236,7 @@
     by_parity(lax.rem(where_ref[2], 2) == 0, z_a, z_b, store)
 
 
-def inner_kernel(strain, plastic, alpha, kappa, turned, bz, smooth, free, yext, xext, field):
+def inner_kernel(strain, plastic, alpha, turned, bz, smooth, free, field):
     @pl.loop(0, 8)
     def _(g):
         for i in range(4):
@@ -241,18 +252,13 @@
     for g in range(4):
         part = field[8 * g : 8 * g + 8].reshape(256, 256)
         smooth[8 * g : 8 * g + 8] = dot(part, bz[...]).reshape(8, 32, 256)
-    for e, ref in enumerate((free, strain.at[1], strain.at[2], kappa)):
-        xext[e] = ref[31]
-        for x in range(32):
-            yext[e, x : x + 1, :] = ref[x, 31:32, :]
 
 
 def z_kernel(
-    where_ref, own, yext_in, xext_in, sent_a, sent_b, got_a, got_b, t_low, t_high, w_low, w_own,
-    plane, y_a, y_b, z_low, z_high, yext, xext,
+    counts, where_ref, own, xext_in, sent_a, sent_b, got_a, got_b, _, t_low, t_high, w_low, w_own,
+    plane, y_a, y_b, z_low, z_high, xext,
     own_low, head_rows, tail_rows, some_low, some_high, ends,
 ):
-    yext[...] = yext_in[...]
     xext[...] = xext_in[...]
 
     def choose(upper, lower):
@@ -261,6 +267,15 @@
         own_low[...] = lower[1][...]
 
     by_parity(lax.rem(where_ref[2], 2) == 0, (got_a, sent_a), (got_b, sent_b), choose)
+
+    @pl.when(where_ref[2] == 0)
+    def _():
+        z_low[...] = jnp.zeros_like(z_low)
+
+    @pl.when(where_ref[2] == counts[2] - 1)
+    def _():
+        z_high[...] = jnp.zeros_like(z_high)
+
     group = lanes((8, 128)) // 16
     for half in range(2):
         for x in range(32):
@@ -318,8 +333,8 @@
 
 
 def y_kernel(
-    where_ref, own, own_face, plane, got_a, got_b, face_ext, _, my, v,
-    edges, out_face, out_plane, halo, x_a, x_b, plane_low, plane_high,
+    counts, where_ref, own, own_face, plane, got_a, got_b, face_ext, ext_a, ext_b, my, v,
+    edges, out_face, out_plane, halo, x_a, x_b, got_ext, plane_low, plane_high,
 ):
     def choose(upper, lower):
         for j in range(7):
@@ -329,9 +344,21 @@
         plane_low[...] = lower[7]
         plane_high[...] = upper[7]
 
-    halo[:, 0:8, :] = jnp.zeros((32, 8, 256), F32)
-    halo[:, 8:16, :] = jnp.zeros((32, 8, 256), F32)
+    halo[:, 7, :] = jnp.zeros((32, 256), F32)
+    halo[:, 14, :] = jnp.zeros((32, 256), F32)
+    halo[:, 15, :] = jnp.zeros((32, 256), F32)
     by_parity(lax.rem(where_ref[1], 2) == 0, got_a, got_b, choose)
+
+    @pl.when(where_ref[1] == 0)
+    def _():
+        halo[:, 0:8, :] = jnp.zeros((32, 8, 256), F32)
+        plane_low[...] = jnp.zeros_like(plane_low)
+
+    @pl.when(where_ref[1] == counts[1] - 1)
+    def _():
+        halo[:, 8:16, :] = jnp.zeros((32, 8, 256), F32)
+        plane_high[...] = jnp.zeros_like(plane_high)
+
     out_face[8:24, :] = own_face[8:24, :]
     for i in range(16):
         x = i if i < 8 else i + 16
@@ -371,6 +398,11 @@
         lower[7, 16:24, :] = out_plane[0:8, :]
 
     by_parity(lax.rem(where_ref[0], 2) == 0, x_a, x_b, store)
+
+    def keep(_, lower):
+        got_ext[...] = lower[...]
+
+    by_parity(lax.rem(where_ref[0], 2) == 0, ext_a, ext_b, keep)
 
 
 def fill_side(at, side, face_ext):
@@ -597,18 +629,26 @@
         copy.wait()
 
 
-def swap(first, second, axis, around=False):
-    count = lax.axis_size(axis)
+AXES = ("gx", "gy", "gz")
+
+
+def swap(first, second, axis):
+    sizes = [lax.axis_size(a) for a in AXES]
+    at = AXES.index(axis)
+    other = 2 if at == 1 else 1
 
     def route(start):
         out = []
-        for i in range(start, count - 1, 2):
-            out += [(i, i + 1), (i + 1, i)]
-        if start and around:
-            out += [(count - 1, 0), (0, count - 1)]
+        for place in np.ndindex(*sizes):
+            there = list(place)
+            if place[at] >= start and place[at] - start < (sizes[at] - start) // 2 * 2:
+                there[at] += 1 if (place[at] - start) % 2 == 0 else -1
+            else:
+                there[other] ^= 1
+            out.append(tuple(int(np.ravel_multi_index(p, sizes)) for p in (place, tuple(there))))
         return out
 
-    return lax.ppermute(first, axis, route(0)), lax.ppermute(second, axis, route(1))
+    return lax.ppermute(first, AXES, route(0)), lax.ppermute(second, AXES, route(1))
 
 
 def to_next(block, axis):
@@ -646,11 +686,10 @@
 
 
 def body(strain_in, plastic_in, alpha_in, kappa_in, flags):
-    where = jnp.stack([lax.axis_index(a) for a in ("gx", "gy", "gz")]).astype(jnp.int32)
+    where = jnp.stack([lax.axis_index(a) for a in AXES]).astype(jnp.int32)
     flags = flags.reshape(32, 32)
-    extents = (
-        32 * lax.axis_size("gx"), 32 * lax.axis_size("gy"), 256 * lax.axis_size("gz"),
-    )
+    counts = tuple(lax.axis_size(a) for a in AXES)
+    extents = (32 * counts[0], 32 * counts[1], 256 * counts[2])
     rows_all = rows_matrix()
     rows_own = np.ascontiguousarray(rows_all[:, 8:40])
     rows_halo = np.concatenate(
@@ -666,33 +705,36 @@
     ]
     ends, eight = shape_of(4, 32, 256), shape_of(8, 32, 256)
     square = shape_of(128, 128)
-    strain, plastic, alpha, kappa, turned, z_a, z_b = call(
+    strain, plastic, alpha, kappa, turned, z_a, z_b, yext, xext = call(
         pack_kernel,
         "pack",
         [SM] + [HBM] * 5,
-        [shape_of(3, 32, 32, 256), BLOCK, BLOCK, BLOCK, shape_of(32, 32), square, square],
+        [
+            shape_of(3, 32, 32, 256), BLOCK, BLOCK, BLOCK, shape_of(32, 32), square, square,
+            ends, ends,
+        ],
         scratch=[pltpu.VMEM((32, 32), jnp.int32)] + [vmem(128, 128)] * 6
         + [pltpu.SemaphoreType.DMA((CHUNKS + 1, 4))],
     )(where, *whole_in)
     got_a, got_b = swap(z_a, z_b, "gz")
-    own, free, yext, xext = call(
-        inner_kernel, "inner", [VM] * 6, [BLOCK, BLOCK, ends, ends], scratch=[vmem(32, 32, 256)]
-    )(strain, plastic, alpha, kappa, turned, z_band(256))
+    face_ext = to_next(yext, "gy")
+    own, free = call(
+        inner_kernel, "inner", [VM] * 5, [BLOCK, BLOCK], scratch=[vmem(32, 32, 256)]
+    )(strain, plastic, alpha, turned, z_band(256))
     t_low, t_high = z_low_rows(), z_high_rows()
-    plane, y_a, y_b, z_low, z_high, yext, xext = call(
-        z_kernel,
+    plane, y_a, y_b, z_low, z_high, xext = call(
+        functools.partial(z_kernel, counts),
         "along_z",
         [SM] + [VM] * 11,
-        [FACE, eight, eight, square, square, ends, ends],
+        [FACE, eight, eight, square, square, ends],
         scratch=[vmem(128, 128)] + [vmem(32, 128)] * 2 + [vmem(512, 128)] * 2
         + [vmem(2, 32, 8, 256)],
     )(
-        where, own, yext, xext, z_a, z_b, got_a, got_b,
+        where, own, xext, z_a, z_b, got_a, got_b, face_ext,
         t_low, t_high, plane_from_low(), plane_from_own(),
     )
     got_a, got_b = swap(y_a, y_b, "gy")
-    face_ext = to_next(yext, "gy")
-    got_ext = to_next(xext, "gx")
+    ext_a, ext_b = swap(xext, xext, "gx")
     own, own_face = call(
         own_rows_kernel,
         "own_rows",
@@ -701,14 +743,14 @@
         scratch=[vmem(1024, 128), vmem(32, 32, 256)],
     )(own, z_low, z_high, t_low, t_high, rows_own)
 
-    edges, face, plane, halo, x_a, x_b = call(
-        y_kernel,
+    edges, face, plane, halo, x_a, x_b, got_ext = call(
+        functools.partial(y_kernel, counts),
         "along_y",
-        [SM] + [VM] * 9,
-        [shape_of(16, 32, 256), FACE, FACE, shape_of(32, 16, 256), eight, eight],
+        [SM] + [VM] * 10,
+        [shape_of(16, 32, 256), FACE, FACE, shape_of(32, 16, 256), eight, eight, ends],
         scratch=[vmem(32, 256), vmem(32, 256)],
-    )(where, own, own_face, plane, got_a, got_b, face_ext, got_ext, rows_halo, plane_y_matrix())
-    got_a, got_b = swap(x_a, x_b, "gx", around=True)
+    )(where, own, own_face, plane, got_a, got_b, face_ext, ext_a, ext_b, rows_halo, plane_y_matrix())
+    got_a, got_b = swap(x_a, x_b, "gx")
 
     shared = [
         vmem(48, 256), vmem(48, 256), vmem(4, 40, 256), vmem(4, 32, 256),

time: 45.5 us -> 40.6 us (0.89)
  the two profiles are of different devices: /device:TPU:16 before, /device:TPU:48 now
where the time goes in v4:
time: 40.6 us; the launch traced here: 40.5 us
  Pallas kernels  19.8 us (49%)
  starting transfers between devices  10.9 us (27%)
  waiting for transfers between devices  8.73 us (22%)
  between operations  0.95 us (2%)
    ppermute x4, starting transfers between devices, swap(): lax.ppermute(second, AXES, route(1))  8.7 us
    ppermute x4, waiting for transfers between devices, swap(): lax.ppermute(second, AXES, route(1))  7.26 us
    pallas_call x1, Pallas kernels, body(): call(functools.partial(middle_kernel, extents), 'middle', [SM] + [VM] * 1...  4.89 us
    pallas_call x1, Pallas kernels, body(): call(pack_kernel, 'pack', [SM] + [HBM] * 5, [shape_of(3, 32, 32, 256), BL...  4.19 us
    pallas_call x1, Pallas kernels, body(): call(functools.partial(outer_kernel, extents), 'outer', [SM] + [VM] * 11...  2.76 us
    pallas_call x1, Pallas kernels, body(): call(inner_kernel, 'inner', [VM] * 5, [BLOCK, BLOCK], scratch=[vmem(32, 3...  2.73 us
    pallas_call x1, Pallas kernels, body(): call(own_rows_kernel, 'own_rows', [VM] * 6, [BLOCK, FACE], scratch=[vmem(...  2.13 us
    ppermute x4, starting transfers between devices, swap(): lax.ppermute(first, AXES, route(0))  2.08 us
  transfers between devices with their start and end apart: 9, of which 4 were waited for; matrix products, arithmetic and copies ran while one was open for 0% of the time, Pallas kernels for 24%

profile of v4, /device:TPU:48, one launch (start us, length us, event | category | flops | bytes accessed | tf_op | source)
XLA Modules:
  0.0 40.5 jit_solution(13328487449498643690)
XLA Ops:
  0.6 0.1 pad_add_fusion.where_ref
  0.7 0.0 copy-start.2
  0.7 4.2 %pack.1 = (f32[3,32,32,256]{3,2,1,0:T(8,128)S(1)}, f32[32,32,256]{2,1,0:T(8,128)S(1)}, f32[32,32,256]{2,1,0:T(8,128)S(1)}, f32[32,32,256]{2,1,0:T(8,128)S(1)}, f...) custom-call(s32[3]{0:T(128)S(1)} %pad_add_fusion.where_ref, ...), custom_call_target="tpu_custom_call" | custom-call | tf_op jit(solution)/shard_map/pack/pallas_call | solution.py:708
  4.9 0.0 copy-start
  4.9 0.0 copy-start.1
  4.9 0.0 copy-start.6
  4.9 0.0 copy-start.7
  5.0 0.1 collective-permute-start.2
  5.0 1.6 %collective-permute-start = (f32[128,128]{1,0:T(8,128)S(1)}, f32[128,128]{1,0:T(8,128)S(1)}, u32[]{:S(2)}, u32[]{:S(2)}) collective-permute-start(f32[128,128]{1,0:T(8,128)S(1)} %get-tuple-element.40.sent_a), channel_id=1, source_target_pairs={{0,1},{1,0},{2,3},{3,2},{4,5},{5,4},{6,7},{7,6},{8,9},{9,8},{10,11... | collective-permute-start | bytes 196616 | tf_op jit(solution)/shard_map/ppermute | solution.py:651
  6.6 1.9 %collective-permute-start.1 = (f32[128,128]{1,0:T(8,128)S(1)}, f32[128,128]{1,0:T(8,128)S(1)}, u32[]{:S(2)}, u32[]{:S(2)}) collective-permute-start(f32[128,128]{1,0:T(8,128)S(1)} %get-tuple-element.41.sent_b), channel_id=1, source_target_pairs={{0,8},{1,2},{2,1},{3,4},{4,3},{5,6},{6,5},{7,15},{8,0},{9,10},{10,... | collective-permute-start | bytes 196616 | tf_op jit(solution)/shard_map/ppermute | solution.py:651
  8.5 0.0 copy-done.2
  8.5 0.0 copy-start.8
  8.5 0.0 copy-start.4
  8.5 0.0 copy-start.5
  8.5 2.7 %inner.1 = (f32[32,32,256]{2,1,0:T(8,128)S(1)}, f32[32,32,256]{2,1,0:T(8,128)S(1)}) custom-call(f32[3,32,32,256]{3,2,1,0:T(8,128)S(1)} %get-tuple-element.32.strain, f32[32,32,256]{2,1,0:T(8,128)S(1)} %get-tuple-element.33.plastic, f32[32,32,256]{2,1,0:T(8,128)S(1)} %get-tuple-element.34.alpha, f32[32,32]{1,0:T(8,128)S(1)} %get-tuple-element.35.turned, ...), custom_call_target="tpu_custom_call" | custom-call | tf_op jit(solution)/shard_map/inner/pallas_call | solution.py:721
  11.2 0.0 copy-start.3
  11.3 0.0 collective-permute-done.got_a
  11.3 4.0 %collective-permute-done.1.got_b = f32[128,128]{1,0:T(8,128)S(1)} collective-permute-done((f32[128,128]{1,0:T(8,128)S(1)}, f32[128,128]{1,0:T(8,128)S(1)}, u32[]{:S(2)}, u32[]{:S(2)}) %collective-permute-start.1) | collective-permute-done | bytes 65568 | tf_op jit(solution)/shard_map/ppermute | solution.py:651
  15.2 0.0 collective-permute-done.2._.face_ext
  15.2 0.0 copy-done
  15.2 0.0 copy-done.1
  15.2 0.0 copy-done.6
  15.3 0.0 copy-done.7
  15.3 1.6 %along_z.1 = (f32[32,256]{1,0:T(8,128)S(1)}, f32[8,32,256]{2,1,0:T(8,128)S(1)}, f32[8,32,256]{2,1,0:T(8,128)S(1)}, f32[128,128]{1,0:T(8,128)S(1)}, f32[128,128]{1,0:T(8,128)S(1)}, /*index=5*/f32[4,32,256]{2,1,0:T(8,128)S(1)}) custom-call(s32[3]{0:T(128)S(1)} %pad_add_fusion.where_ref, f32[32,32,256]{2,1,0:T(8,128)S(1)} %get-tuple-element.38.own, ...), custom_call_target="tpu_custom_call" | custom-call | tf_op jit(solution)/shard_map/along_z/pallas_call | solution.py:725
  16.8 0.1 collective-permute-start.3
  17.0 0.1 collective-permute-start.4
  17.0 2.0 %collective-permute-start.6 = (f32[4,32,256]{2,1,0:T(8,128)S(1)}, f32[4,32,256]{2,1,0:T(8,128)S(1)}, u32[]{:S(2)}, u32[]{:S(2)}) collective-permute-start(f32[4,32,256]{2,1,0:T(8,128)S(1)} %get-tuple-element.50), channel_id=1, source_target_pairs={{0,8},{1,9},{2,10},{3,11},{4,12},{5,13},{6,14},{7,15},{8,0},{9,1},... | collective-permute-start | bytes 393224 | tf_op jit(solution)/shard_map/ppermute | solution.py:651
  19.0 0.0 collective-permute-start.5
  19.0 0.0 copy-done.8
  19.0 2.1 %own_rows.1 = (f32[32,32,256]{2,1,0:T(8,128)S(1)}, f32[32,256]{1,0:T(8,128)S(1)}) custom-call(f32[32,32,256]{2,1,0:T(8,128)S(1)} %get-tuple-element.38.own, f32[128,128]{1,0:T(8,128)S(1)} %get-tuple-element.43.z_low, f32[128,128]{1,0:T(8,128)S(1)} %get-tuple-element.44.z_high, f32[128,128]{1,0:T(8,128)S(1)} %copy-done.1, f32[128,128]{1,0:T(8,128)S(1)} %copy-done, ...), custom_call_target="tpu_custom_call" | custom-call | tf_op jit(solution)/shard_map/own_rows/pallas_call | solution.py:738
  21.2 2.3 %collective-permute-done.6.ext_b = f32[4,32,256]{2,1,0:T(8,128)S(1)} collective-permute-done((f32[4,32,256]{2,1,0:T(8,128)S(1)}, f32[4,32,256]{2,1,0:T(8,128)S(1)}, u32[]{:S(2)}, u32[]{:S(2)}) %collective-permute-start.6) | collective-permute-done | bytes 131104 | tf_op jit(solution)/shard_map/ppermute | solution.py:651
  23.5 1.5 %collective-permute-done.5.ext_a = f32[4,32,256]{2,1,0:T(8,128)S(1)} collective-permute-done((f32[4,32,256]{2,1,0:T(8,128)S(1)}, f32[4,32,256]{2,1,0:T(8,128)S(1)}, u32[]{:S(2)}, u32[]{:S(2)}) %collective-permute-start.5) | collective-permute-done | bytes 131104 | tf_op jit(solution)/shard_map/ppermute | solution.py:651
  25.0 0.0 collective-permute-done.3.got_a
  25.0 0.0 collective-permute-done.4.got_b
  25.0 0.0 copy-done.4
  25.0 0.0 copy-done.5
  25.0 1.6 %along_y.1 = (f32[16,32,256]{2,1,0:T(8,128)S(1)}, f32[32,256]{1,0:T(8,128)S(1)}, f32[32,256]{1,0:T(8,128)S(1)}, f32[32,16,256]{2,1,0:T(8,128)S(1)}, f32[8,32,256...) custom-call(s32[3]{0:T(128)S(1)} %pad_add_fusion.where_ref, ...), custom_call_target="tpu_custom_call" | custom-call | tf_op jit(solution)/shard_map/along_y/pallas_call | solution.py:746
  26.6 0.4 collective-permute-start.7
  26.9 4.8 %collective-permute-start.8 = (f32[8,32,256]{2,1,0:T(8,128)S(1)}, f32[8,32,256]{2,1,0:T(8,128)S(1)}, u32[]{:S(2)}, u32[]{:S(2)}) collective-permute-start(f32[8,32,256]{2,1,0:T(8,128)S(1)} %get-tuple-element.58), channel_id=1, source_target_pairs={{0,8},{1,9},{2,10},{3,11},{4,12},{5,13},{6,14},{7,15},{8,0},{9,1},... | collective-permute-start | bytes 786440 | tf_op jit(solution)/shard_map/ppermute | solution.py:651
  31.7 0.0 copy-done.3
  31.7 4.9 %middle.1 = (f32[32,32,256]{2,1,0:T(8,128)}, f32[32,32,256]{2,1,0:T(8,128)}, f32[18,32,256]{2,1,0:T(8,128)S(1)}, f32[32,256]{1,0:T(8,128)S(1)}) custom-call(s32[3]{0:T(128)S(1)} %pad_add_fusion.where_ref, f32[3,32,32,256]{3,2,1,0:T(8,128)S(1)} %get-tuple-element.32.strain, f32[32,32,256]{2,1,0:T(8,128)S(1)} %get-tuple-element.36.free, ...), custom_call_target="tpu_custom_call" | custom-call | tf_op jit(solution)/shard_map/middle/pallas_call | solution.py:760
  36.6 0.0 collective-permute-done.7.got_a
  36.6 1.0 %collective-permute-done.8.got_b = f32[8,32,256]{2,1,0:T(8,128)S(1)} collective-permute-done((f32[8,32,256]{2,1,0:T(8,128)S(1)}, f32[8,32,256]{2,1,0:T(8,128)S(1)}, u32[]{:S(2)}, u32[]{:S(2)}) %collective-permute-start.8) | collective-permute-done | bytes 262176 | tf_op jit(solution)/shard_map/ppermute | solution.py:651
  37.6 2.8 %outer.1 = (f32[32,32,256]{2,1,0:T(8,128)}, f32[32,32,256]{2,1,0:T(8,128)}) custom-call(s32[3]{0:T(128)S(1)} %pad_add_fusion.where_ref, f32[3,32,32,256]{3,2,1,0:T(8,128)S(1)} %get-tuple-element.32.strain, f32[32,32,256]{2,1,0:T(8,128)S(1)} %get-tuple-element.36.free, ...), custom_call_target="tpu_custom_call", output_to_operand_aliasing={{0}: (12, {}), {1}: (13, {})} | custom-call | tf_op jit(solution)/shard_map/outer/pallas_call | solution.py:768
Async XLA Ops:
  0.7 7.8 %copy-start.2 = (f32[256,256]{1,0:T(8,128)S(1)}, f32[256,256]{1,0:T(8,128)}, u32[]{:S(2)}) copy-start(f32[256,256]{1,0:T(8,128)} %constant.30.clone.bz) | copy-start | bytes 786436
  4.9 10.3 %copy-start = (f32[128,128]{1,0:T(8,128)S(1)}, f32[128,128]{1,0:T(8,128)}, u32[]{:S(2)}) copy-start(f32[128,128]{1,0:T(8,128)} %constant.32.clone.t_high) | copy-start | bytes 196612
  4.9 10.3 %copy-start.1 = (f32[128,128]{1,0:T(8,128)S(1)}, f32[128,128]{1,0:T(8,128)}, u32[]{:S(2)}) copy-start(f32[128,128]{1,0:T(8,128)} %constant.31.clone.t_low) | copy-start | bytes 196612
  4.9 10.3 %copy-start.6 = (f32[40,128]{1,0:T(8,128)S(1)}, f32[40,128]{1,0:T(8,128)}, u32[]{:S(2)}) copy-start(f32[40,128]{1,0:T(8,128)} %constant.34.clone.w_own) | copy-start | bytes 61444
  4.9 10.3 %copy-start.7 = (f32[40,128]{1,0:T(8,128)S(1)}, f32[40,128]{1,0:T(8,128)}, u32[]{:S(2)}) copy-start(f32[40,128]{1,0:T(8,128)} %constant.33.clone.w_low) | copy-start | bytes 61444
  5.0 10.3 %collective-permute-start.2 = (f32[4,32,256]{2,1,0:T(8,128)S(1)}, f32[4,32,256]{2,1,0:T(8,128)S(1)}, u32[]{:S(2)}, u32[]{:S(2)}) collective-permute-start(f32[4,32,256]{2,1,0:T(8,128)S(1)} %get-tuple-element.42), channel_id=1, source_target_pairs={{0,8},{8,16},{16,24},{24,0},{1,9},{9,17},{17,25},{25,1},{2,10},{10... | collective-permute-start | bytes 393224 | tf_op jit(solution)/shard_map/ppermute | solution.py:656
  5.0 6.2 %collective-permute-start = (f32[128,128]{1,0:T(8,128)S(1)}, f32[128,128]{1,0:T(8,128)S(1)}, u32[]{:S(2)}, u32[]{:S(2)}) collective-permute-start(f32[128,128]{1,0:T(8,128)S(1)} %get-tuple-element.40.sent_a), channel_id=1, source_target_pairs={{0,1},{1,0},{2,3},{3,2},{4,5},{5,4},{6,7},{7,6},{8,9},{9,8},{10,11... | collective-permute-start | bytes 196616 | tf_op jit(solution)/shard_map/ppermute | solution.py:651
  6.6 8.6 %collective-permute-start.1 = (f32[128,128]{1,0:T(8,128)S(1)}, f32[128,128]{1,0:T(8,128)S(1)}, u32[]{:S(2)}, u32[]{:S(2)}) collective-permute-start(f32[128,128]{1,0:T(8,128)S(1)} %get-tuple-element.41.sent_b), channel_id=1, source_target_pairs={{0,8},{1,2},{2,1},{3,4},{4,3},{5,6},{6,5},{7,15},{8,0},{9,10},{10,... | collective-permute-start | bytes 196616 | tf_op jit(solution)/shard_map/ppermute | solution.py:651
  8.5 10.5 %copy-start.8 = (f32[40,32]{1,0:T(8,128)S(1)}, f32[40,32]{1,0:T(8,128)}, u32[]{:S(2)}) copy-start(f32[40,32]{1,0:T(8,128)} %constant.35.clone.my) | copy-start | bytes 15364
  8.5 16.5 %copy-start.4 = (f32[128,128]{1,0:T(8,128)S(1)}, f32[128,128]{1,0:T(8,128)}, u32[]{:S(2)}) copy-start(f32[128,128]{1,0:T(8,128)} %constant.37.clone.v) | copy-start | bytes 196612
  8.5 16.5 %copy-start.5 = (f32[40,16]{1,0:T(8,128)S(1)}, f32[40,16]{1,0:T(8,128)}, u32[]{:S(2)}) copy-start(f32[40,16]{1,0:T(8,128)} %constant.36.clone.my) | copy-start | bytes 7684
  11.2 20.5 %copy-start.3 = (f32[40,128]{1,0:T(8,128)S(1)}, f32[40,128]{1,0:T(8,128)}, u32[]{:S(2)}) copy-start(f32[40,128]{1,0:T(8,128)} %constant.38.clone.my) | copy-start | bytes 61444
  16.8 8.1 %collective-permute-start.3 = (f32[8,32,256]{2,1,0:T(8,128)S(1)}, f32[8,32,256]{2,1,0:T(8,128)S(1)}, u32[]{:S(2)}, u32[]{:S(2)}) collective-permute-start(f32[8,32,256]{2,1,0:T(8,128)S(1)} %get-tuple-element.48), channel_id=1, source_target_pairs={{0,8},{1,9},{2,10},{3,11},{4,12},{5,13},{6,14},{7,15},{8,0},{9,1},... | collective-permute-start | bytes 786440 | tf_op jit(solution)/shard_map/ppermute | solution.py:651
  17.0 8.0 %collective-permute-start.4 = (f32[8,32,256]{2,1,0:T(8,128)S(1)}, f32[8,32,256]{2,1,0:T(8,128)S(1)}, u32[]{:S(2)}, u32[]{:S(2)}) collective-permute-start(f32[8,32,256]{2,1,0:T(8,128)S(1)} %get-tuple-element.49), channel_id=1, source_target_pairs={{0,1},{1,0},{2,3},{3,2},{4,5},{5,4},{6,7},{7,6},{8,16},{9,17},{10,... | collective-permute-start | bytes 786440 | tf_op jit(solution)/shard_map/ppermute | solution.py:651
  17.0 6.5 %collective-permute-start.6 = (f32[4,32,256]{2,1,0:T(8,128)S(1)}, f32[4,32,256]{2,1,0:T(8,128)S(1)}, u32[]{:S(2)}, u32[]{:S(2)}) collective-permute-start(f32[4,32,256]{2,1,0:T(8,128)S(1)} %get-tuple-element.50), channel_id=1, source_target_pairs={{0,8},{1,9},{2,10},{3,11},{4,12},{5,13},{6,14},{7,15},{8,0},{9,1},... | collective-permute-start | bytes 393224 | tf_op jit(solution)/shard_map/ppermute | solution.py:651
  19.0 5.9 %collective-permute-start.5 = (f32[4,32,256]{2,1,0:T(8,128)S(1)}, f32[4,32,256]{2,1,0:T(8,128)S(1)}, u32[]{:S(2)}, u32[]{:S(2)}) collective-permute-start(f32[4,32,256]{2,1,0:T(8,128)S(1)} %get-tuple-element.50), channel_id=1, source_target_pairs={{0,32},{1,33},{2,34},{3,35},{4,36},{5,37},{6,38},{7,39},{8,40},{9,... | collective-permute-start | bytes 393224 | tf_op jit(solution)/shard_map/ppermute | solution.py:651
  26.6 10.0 %collective-permute-start.7 = (f32[8,32,256]{2,1,0:T(8,128)S(1)}, f32[8,32,256]{2,1,0:T(8,128)S(1)}, u32[]{:S(2)}, u32[]{:S(2)}) collective-permute-start(f32[8,32,256]{2,1,0:T(8,128)S(1)} %get-tuple-element.57), channel_id=1, source_target_pairs={{0,32},{1,33},{2,34},{3,35},{4,36},{5,37},{6,38},{7,39},{8,40},{9,... | collective-permute-start | bytes 786440 | tf_op jit(solution)/shard_map/ppermute | solution.py:651
  26.9 10.7 %collective-permute-start.8 = (f32[8,32,256]{2,1,0:T(8,128)S(1)}, f32[8,32,256]{2,1,0:T(8,128)S(1)}, u32[]{:S(2)}, u32[]{:S(2)}) collective-permute-start(f32[8,32,256]{2,1,0:T(8,128)S(1)} %get-tuple-element.58), channel_id=1, source_target_pairs={{0,8},{1,9},{2,10},{3,11},{4,12},{5,13},{6,14},{7,15},{8,0},{9,1},... | collective-permute-start | bytes 786440 | tf_op jit(solution)/shard_map/ppermute | solution.py:651

commit v5 on v4

--- a/solution.py
+++ b/solution.py
@@ -255,7 +255,7 @@
 
 
 def z_kernel(
-    counts, where_ref, own, xext_in, sent_a, sent_b, got_a, got_b, _, t_low, t_high, w_low, w_own,
+    counts, where_ref, own, xext_in, sent_a, sent_b, got_b, got_a, _, t_low, t_high, w_low, w_own,
     plane, y_a, y_b, z_low, z_high, xext,
     own_low, head_rows, tail_rows, some_low, some_high, ends,
 ):
@@ -333,7 +333,7 @@
 
 
 def y_kernel(
-    counts, where_ref, own, own_face, plane, got_a, got_b, face_ext, ext_a, ext_b, my, v,
+    counts, where_ref, own, own_face, plane, got_b, got_a, face_ext, ext_b, ext_a, my, v,
     edges, out_face, out_plane, halo, x_a, x_b, got_ext, plane_low, plane_high,
 ):
     def choose(upper, lower):
@@ -730,7 +730,7 @@
         scratch=[vmem(128, 128)] + [vmem(32, 128)] * 2 + [vmem(512, 128)] * 2
         + [vmem(2, 32, 8, 256)],
     )(
-        where, own, xext, z_a, z_b, got_a, got_b, face_ext,
+        where, own, xext, z_a, z_b, got_b, got_a, face_ext,
         t_low, t_high, plane_from_low(), plane_from_own(),
     )
     got_a, got_b = swap(y_a, y_b, "gy")
@@ -749,7 +749,7 @@
         [SM] + [VM] * 10,
         [shape_of(16, 32, 256), FACE, FACE, shape_of(32, 16, 256), eight, eight, ends],
         scratch=[vmem(32, 256), vmem(32, 256)],
-    )(where, own, own_face, plane, got_a, got_b, face_ext, ext_a, ext_b, rows_halo, plane_y_matrix())
+    )(where, own, own_face, plane, got_b, got_a, face_ext, ext_b, ext_a, rows_halo, plane_y_matrix())
     got_a, got_b = swap(x_a, x_b, "gx")
 
     shared = [

time: 40.6 us -> 40 us (0.985)
  the two profiles are of different devices: /device:TPU:48 before, /device:TPU:120 now
where the time goes in v5:
time: 40 us; the launch traced here: 39.4 us
  Pallas kernels  19.8 us (50%)
  starting transfers between devices  12.9 us (32%)
  waiting for transfers between devices  5.64 us (14%)
  between operations  0.96 us (2%)
    ppermute x4, starting transfers between devices, swap(): lax.ppermute(second, AXES, route(1))  11 us
    ppermute x4, waiting for transfers between devices, swap(): lax.ppermute(second, AXES, route(1))  5.63 us
    pallas_call x1, Pallas kernels, body(): call(functools.partial(middle_kernel, extents), 'middle', [SM] + [VM] * 1...  4.88 us
    pallas_call x1, Pallas kernels, body(): call(pack_kernel, 'pack', [SM] + [HBM] * 5, [shape_of(3, 32, 32, 256), BL...  4.19 us
    pallas_call x1, Pallas kernels, body(): call(functools.partial(outer_kernel, extents), 'outer', [SM] + [VM] * 11...  2.75 us
    pallas_call x1, Pallas kernels, body(): call(inner_kernel, 'inner', [VM] * 5, [BLOCK, BLOCK], scratch=[vmem(32, 3...  2.73 us
    pallas_call x1, Pallas kernels, body(): call(own_rows_kernel, 'own_rows', [VM] * 6, [BLOCK, FACE], scratch=[vmem(...  2.13 us
    ppermute x4, starting transfers between devices, swap(): lax.ppermute(first, AXES, route(0))  1.79 us
  transfers between devices with their start and end apart: 9, of which 3 were waited for; matrix products, arithmetic and copies ran while one was open for 0% of the time, Pallas kernels for 25%

profile of v5, /device:TPU:120, one launch (start us, length us, event | category | flops | bytes accessed | tf_op | source)
XLA Modules:
  0.0 39.4 jit_solution(16897608159182328057)
XLA Ops:
  0.6 0.1 pad_add_fusion.where_ref
  0.7 0.0 copy-start.2
  0.7 4.2 %pack.1 = (f32[3,32,32,256]{3,2,1,0:T(8,128)S(1)}, f32[32,32,256]{2,1,0:T(8,128)S(1)}, f32[32,32,256]{2,1,0:T(8,128)S(1)}, f32[32,32,256]{2,1,0:T(8,128)S(1)}, f...) custom-call(s32[3]{0:T(128)S(1)} %pad_add_fusion.where_ref, ...), custom_call_target="tpu_custom_call" | custom-call | tf_op jit(solution)/shard_map/pack/pallas_call | solution.py:708
  4.9 0.0 copy-start
  4.9 0.0 copy-start.1
  4.9 0.0 copy-start.6
  4.9 0.0 copy-start.7
  5.0 0.1 collective-permute-start.2
  5.0 1.6 %collective-permute-start.1 = (f32[128,128]{1,0:T(8,128)S(1)}, f32[128,128]{1,0:T(8,128)S(1)}, u32[]{:S(2)}, u32[]{:S(2)}) collective-permute-start(f32[128,128]{1,0:T(8,128)S(1)} %get-tuple-element.40.sent_a), channel_id=1, source_target_pairs={{0,1},{1,0},{2,3},{3,2},{4,5},{5,4},{6,7},{7,6},{8,9},{9,8},{10,11... | collective-permute-start | bytes 196616 | tf_op jit(solution)/shard_map/ppermute | solution.py:651
  6.6 2.8 %collective-permute-start = (f32[128,128]{1,0:T(8,128)S(1)}, f32[128,128]{1,0:T(8,128)S(1)}, u32[]{:S(2)}, u32[]{:S(2)}) collective-permute-start(f32[128,128]{1,0:T(8,128)S(1)} %get-tuple-element.41.sent_b), channel_id=1, source_target_pairs={{0,8},{1,2},{2,1},{3,4},{4,3},{5,6},{6,5},{7,15},{8,0},{9,10},{10,... | collective-permute-start | bytes 196616 | tf_op jit(solution)/shard_map/ppermute | solution.py:651
  9.4 0.0 copy-done.2
  9.4 0.0 copy-start.8
  9.4 0.0 copy-start.4
  9.4 0.0 copy-start.5
  9.4 2.7 %inner.1 = (f32[32,32,256]{2,1,0:T(8,128)S(1)}, f32[32,32,256]{2,1,0:T(8,128)S(1)}) custom-call(f32[3,32,32,256]{3,2,1,0:T(8,128)S(1)} %get-tuple-element.32.strain, f32[32,32,256]{2,1,0:T(8,128)S(1)} %get-tuple-element.33.plastic, f32[32,32,256]{2,1,0:T(8,128)S(1)} %get-tuple-element.34.alpha, f32[32,32]{1,0:T(8,128)S(1)} %get-tuple-element.35.turned, ...), custom_call_target="tpu_custom_call" | custom-call | tf_op jit(solution)/shard_map/inner/pallas_call | solution.py:721
  12.1 0.0 copy-start.3
  12.2 0.0 collective-permute-done.1.got_a
  12.2 2.6 %collective-permute-done.got_b = f32[128,128]{1,0:T(8,128)S(1)} collective-permute-done((f32[128,128]{1,0:T(8,128)S(1)}, f32[128,128]{1,0:T(8,128)S(1)}, u32[]{:S(2)}, u32[]{:S(2)}) %collective-permute-start) | collective-permute-done | bytes 65568 | tf_op jit(solution)/shard_map/ppermute | solution.py:651
  14.7 0.0 collective-permute-done.2._.face_ext
  14.7 0.0 copy-done
  14.7 0.0 copy-done.1
  14.7 0.0 copy-done.6
  14.7 0.0 copy-done.7
  14.8 1.6 %along_z.1 = (f32[32,256]{1,0:T(8,128)S(1)}, f32[8,32,256]{2,1,0:T(8,128)S(1)}, f32[8,32,256]{2,1,0:T(8,128)S(1)}, f32[128,128]{1,0:T(8,128)S(1)}, f32[128,128]{1,0:T(8,128)S(1)}, /*index=5*/f32[4,32,256]{2,1,0:T(8,128)S(1)}) custom-call(s32[3]{0:T(128)S(1)} %pad_add_fusion.where_ref, f32[32,32,256]{2,1,0:T(8,128)S(1)} %get-tuple-element.38.own, ...), custom_call_target="tpu_custom_call" | custom-call | tf_op jit(solution)/shard_map/along_z/pallas_call | solution.py:725
  16.3 1.0 %collective-permute-start.3 = (f32[8,32,256]{2,1,0:T(8,128)S(1)}, f32[8,32,256]{2,1,0:T(8,128)S(1)}, u32[]{:S(2)}, u32[]{:S(2)}) collective-permute-start(f32[8,32,256]{2,1,0:T(8,128)S(1)} %get-tuple-element.48), channel_id=1, source_target_pairs={{0,1},{1,0},{2,3},{3,2},{4,5},{5,4},{6,7},{7,6},{8,16},{9,17},{10,... | collective-permute-start | bytes 786440 | tf_op jit(solution)/shard_map/ppermute | solution.py:651
  17.3 0.0 collective-permute-start.4
  17.3 0.1 collective-permute-start.6
  17.4 4.0 %collective-permute-start.5 = (f32[4,32,256]{2,1,0:T(8,128)S(1)}, f32[4,32,256]{2,1,0:T(8,128)S(1)}, u32[]{:S(2)}, u32[]{:S(2)}) collective-permute-start(f32[4,32,256]{2,1,0:T(8,128)S(1)} %get-tuple-element.50), channel_id=1, source_target_pairs={{0,8},{1,9},{2,10},{3,11},{4,12},{5,13},{6,14},{7,15},{8,0},{9,1},... | collective-permute-start | bytes 393224 | tf_op jit(solution)/shard_map/ppermute | solution.py:651
  21.5 0.0 copy-done.8
  21.5 2.1 %own_rows.1 = (f32[32,32,256]{2,1,0:T(8,128)S(1)}, f32[32,256]{1,0:T(8,128)S(1)}) custom-call(f32[32,32,256]{2,1,0:T(8,128)S(1)} %get-tuple-element.38.own, f32[128,128]{1,0:T(8,128)S(1)} %get-tuple-element.43.z_low, f32[128,128]{1,0:T(8,128)S(1)} %get-tuple-element.44.z_high, f32[128,128]{1,0:T(8,128)S(1)} %copy-done.1, f32[128,128]{1,0:T(8,128)S(1)} %copy-done, ...), custom_call_target="tpu_custom_call" | custom-call | tf_op jit(solution)/shard_map/own_rows/pallas_call | solution.py:738
  23.6 0.0 collective-permute-done.6.ext_a
  23.6 1.7 %collective-permute-done.5.ext_b = f32[4,32,256]{2,1,0:T(8,128)S(1)} collective-permute-done((f32[4,32,256]{2,1,0:T(8,128)S(1)}, f32[4,32,256]{2,1,0:T(8,128)S(1)}, u32[]{:S(2)}, u32[]{:S(2)}) %collective-permute-start.5) | collective-permute-done | bytes 131104 | tf_op jit(solution)/shard_map/ppermute | solution.py:651
  25.4 0.0 collective-permute-done.3.got_b
  25.4 0.0 collective-permute-done.4.got_a
  25.4 0.0 copy-done.4
  25.4 0.0 copy-done.5
  25.4 1.6 %along_y.1 = (f32[16,32,256]{2,1,0:T(8,128)S(1)}, f32[32,256]{1,0:T(8,128)S(1)}, f32[32,256]{1,0:T(8,128)S(1)}, f32[32,16,256]{2,1,0:T(8,128)S(1)}, f32[8,32,256...) custom-call(s32[3]{0:T(128)S(1)} %pad_add_fusion.where_ref, ...), custom_call_target="tpu_custom_call" | custom-call | tf_op jit(solution)/shard_map/along_y/pallas_call | solution.py:746
  27.0 0.1 collective-permute-start.7
  27.1 3.2 %collective-permute-start.8 = (f32[8,32,256]{2,1,0:T(8,128)S(1)}, f32[8,32,256]{2,1,0:T(8,128)S(1)}, u32[]{:S(2)}, u32[]{:S(2)}) collective-permute-start(f32[8,32,256]{2,1,0:T(8,128)S(1)} %get-tuple-element.58), channel_id=1, source_target_pairs={{0,8},{1,9},{2,10},{3,11},{4,12},{5,13},{6,14},{7,15},{8,0},{9,1},... | collective-permute-start | bytes 786440 | tf_op jit(solution)/shard_map/ppermute | solution.py:651
  30.3 0.0 copy-done.3
  30.3 4.9 %middle.1 = (f32[32,32,256]{2,1,0:T(8,128)}, f32[32,32,256]{2,1,0:T(8,128)}, f32[18,32,256]{2,1,0:T(8,128)S(1)}, f32[32,256]{1,0:T(8,128)S(1)}) custom-call(s32[3]{0:T(128)S(1)} %pad_add_fusion.where_ref, f32[3,32,32,256]{3,2,1,0:T(8,128)S(1)} %get-tuple-element.32.strain, f32[32,32,256]{2,1,0:T(8,128)S(1)} %get-tuple-element.36.free, ...), custom_call_target="tpu_custom_call" | custom-call | tf_op jit(solution)/shard_map/middle/pallas_call | solution.py:760
  35.2 0.0 collective-permute-done.7.got_a
  35.2 1.3 %collective-permute-done.8.got_b = f32[8,32,256]{2,1,0:T(8,128)S(1)} collective-permute-done((f32[8,32,256]{2,1,0:T(8,128)S(1)}, f32[8,32,256]{2,1,0:T(8,128)S(1)}, u32[]{:S(2)}, u32[]{:S(2)}) %collective-permute-start.8) | collective-permute-done | bytes 262176 | tf_op jit(solution)/shard_map/ppermute | solution.py:651
  36.5 2.8 %outer.1 = (f32[32,32,256]{2,1,0:T(8,128)}, f32[32,32,256]{2,1,0:T(8,128)}) custom-call(s32[3]{0:T(128)S(1)} %pad_add_fusion.where_ref, f32[3,32,32,256]{3,2,1,0:T(8,128)S(1)} %get-tuple-element.32.strain, f32[32,32,256]{2,1,0:T(8,128)S(1)} %get-tuple-element.36.free, ...), custom_call_target="tpu_custom_call", output_to_operand_aliasing={{0}: (12, {}), {1}: (13, {})} | custom-call | tf_op jit(solution)/shard_map/outer/pallas_call | solution.py:768
Async XLA Ops:
  0.7 8.7 %copy-start.2 = (f32[256,256]{1,0:T(8,128)S(1)}, f32[256,256]{1,0:T(8,128)}, u32[]{:S(2)}) copy-start(f32[256,256]{1,0:T(8,128)} %constant.30.clone.bz) | copy-start | bytes 786436
  4.9 9.8 %copy-start = (f32[128,128]{1,0:T(8,128)S(1)}, f32[128,128]{1,0:T(8,128)}, u32[]{:S(2)}) copy-start(f32[128,128]{1,0:T(8,128)} %constant.32.clone.t_high) | copy-start | bytes 196612
  4.9 9.8 %copy-start.1 = (f32[128,128]{1,0:T(8,128)S(1)}, f32[128,128]{1,0:T(8,128)}, u32[]{:S(2)}) copy-start(f32[128,128]{1,0:T(8,128)} %constant.31.clone.t_low) | copy-start | bytes 196612
  4.9 9.8 %copy-start.6 = (f32[40,128]{1,0:T(8,128)S(1)}, f32[40,128]{1,0:T(8,128)}, u32[]{:S(2)}) copy-start(f32[40,128]{1,0:T(8,128)} %constant.34.clone.w_own) | copy-start | bytes 61444
  4.9 9.8 %copy-start.7 = (f32[40,128]{1,0:T(8,128)S(1)}, f32[40,128]{1,0:T(8,128)}, u32[]{:S(2)}) copy-start(f32[40,128]{1,0:T(8,128)} %constant.33.clone.w_low) | copy-start | bytes 61444
  5.0 9.8 %collective-permute-start.2 = (f32[4,32,256]{2,1,0:T(8,128)S(1)}, f32[4,32,256]{2,1,0:T(8,128)S(1)}, u32[]{:S(2)}, u32[]{:S(2)}) collective-permute-start(f32[4,32,256]{2,1,0:T(8,128)S(1)} %get-tuple-element.42), channel_id=1, source_target_pairs={{0,8},{8,16},{16,24},{24,0},{1,9},{9,17},{17,25},{25,1},{2,10},{10... | collective-permute-start | bytes 393224 | tf_op jit(solution)/shard_map/ppermute | solution.py:656
  5.0 7.1 %collective-permute-start.1 = (f32[128,128]{1,0:T(8,128)S(1)}, f32[128,128]{1,0:T(8,128)S(1)}, u32[]{:S(2)}, u32[]{:S(2)}) collective-permute-start(f32[128,128]{1,0:T(8,128)S(1)} %get-tuple-element.40.sent_a), channel_id=1, source_target_pairs={{0,1},{1,0},{2,3},{3,2},{4,5},{5,4},{6,7},{7,6},{8,9},{9,8},{10,11... | collective-permute-start | bytes 196616 | tf_op jit(solution)/shard_map/ppermute | solution.py:651
  6.6 8.1 %collective-permute-start = (f32[128,128]{1,0:T(8,128)S(1)}, f32[128,128]{1,0:T(8,128)S(1)}, u32[]{:S(2)}, u32[]{:S(2)}) collective-permute-start(f32[128,128]{1,0:T(8,128)S(1)} %get-tuple-element.41.sent_b), channel_id=1, source_target_pairs={{0,8},{1,2},{2,1},{3,4},{4,3},{5,6},{6,5},{7,15},{8,0},{9,10},{10,... | collective-permute-start | bytes 196616 | tf_op jit(solution)/shard_map/ppermute | solution.py:651
  9.4 12.1 %copy-start.8 = (f32[40,32]{1,0:T(8,128)S(1)}, f32[40,32]{1,0:T(8,128)}, u32[]{:S(2)}) copy-start(f32[40,32]{1,0:T(8,128)} %constant.35.clone.my) | copy-start | bytes 15364
  9.4 16.0 %copy-start.4 = (f32[128,128]{1,0:T(8,128)S(1)}, f32[128,128]{1,0:T(8,128)}, u32[]{:S(2)}) copy-start(f32[128,128]{1,0:T(8,128)} %constant.37.clone.v) | copy-start | bytes 196612
  9.4 16.0 %copy-start.5 = (f32[40,16]{1,0:T(8,128)S(1)}, f32[40,16]{1,0:T(8,128)}, u32[]{:S(2)}) copy-start(f32[40,16]{1,0:T(8,128)} %constant.36.clone.my) | copy-start | bytes 7684
  12.1 18.1 %copy-start.3 = (f32[40,128]{1,0:T(8,128)S(1)}, f32[40,128]{1,0:T(8,128)}, u32[]{:S(2)}) copy-start(f32[40,128]{1,0:T(8,128)} %constant.38.clone.my) | copy-start | bytes 61444
  16.3 9.0 %collective-permute-start.3 = (f32[8,32,256]{2,1,0:T(8,128)S(1)}, f32[8,32,256]{2,1,0:T(8,128)S(1)}, u32[]{:S(2)}, u32[]{:S(2)}) collective-permute-start(f32[8,32,256]{2,1,0:T(8,128)S(1)} %get-tuple-element.48), channel_id=1, source_target_pairs={{0,1},{1,0},{2,3},{3,2},{4,5},{5,4},{6,7},{7,6},{8,16},{9,17},{10,... | collective-permute-start | bytes 786440 | tf_op jit(solution)/shard_map/ppermute | solution.py:651
  17.3 8.0 %collective-permute-start.4 = (f32[8,32,256]{2,1,0:T(8,128)S(1)}, f32[8,32,256]{2,1,0:T(8,128)S(1)}, u32[]{:S(2)}, u32[]{:S(2)}) collective-permute-start(f32[8,32,256]{2,1,0:T(8,128)S(1)} %get-tuple-element.49), channel_id=1, source_target_pairs={{0,8},{1,9},{2,10},{3,11},{4,12},{5,13},{6,14},{7,15},{8,0},{9,1},... | collective-permute-start | bytes 786440 | tf_op jit(solution)/shard_map/ppermute | solution.py:651
  17.3 6.3 %collective-permute-start.6 = (f32[4,32,256]{2,1,0:T(8,128)S(1)}, f32[4,32,256]{2,1,0:T(8,128)S(1)}, u32[]{:S(2)}, u32[]{:S(2)}) collective-permute-start(f32[4,32,256]{2,1,0:T(8,128)S(1)} %get-tuple-element.50), channel_id=1, source_target_pairs={{0,32},{1,33},{2,34},{3,35},{4,36},{5,37},{6,38},{7,39},{8,40},{9,... | collective-permute-start | bytes 393224 | tf_op jit(solution)/shard_map/ppermute | solution.py:651
  17.4 7.9 %collective-permute-start.5 = (f32[4,32,256]{2,1,0:T(8,128)S(1)}, f32[4,32,256]{2,1,0:T(8,128)S(1)}, u32[]{:S(2)}, u32[]{:S(2)}) collective-permute-start(f32[4,32,256]{2,1,0:T(8,128)S(1)} %get-tuple-element.50), channel_id=1, source_target_pairs={{0,8},{1,9},{2,10},{3,11},{4,12},{5,13},{6,14},{7,15},{8,0},{9,1},... | collective-permute-start | bytes 393224 | tf_op jit(solution)/shard_map/ppermute | solution.py:651
  27.0 8.2 %collective-permute-start.7 = (f32[8,32,256]{2,1,0:T(8,128)S(1)}, f32[8,32,256]{2,1,0:T(8,128)S(1)}, u32[]{:S(2)}, u32[]{:S(2)}) collective-permute-start(f32[8,32,256]{2,1,0:T(8,128)S(1)} %get-tuple-element.57), channel_id=1, source_target_pairs={{0,32},{1,33},{2,34},{3,35},{4,36},{5,37},{6,38},{7,39},{8,40},{9,... | collective-permute-start | bytes 786440 | tf_op jit(solution)/shard_map/ppermute | solution.py:651
  27.1 9.4 %collective-permute-start.8 = (f32[8,32,256]{2,1,0:T(8,128)S(1)}, f32[8,32,256]{2,1,0:T(8,128)S(1)}, u32[]{:S(2)}, u32[]{:S(2)}) collective-permute-start(f32[8,32,256]{2,1,0:T(8,128)S(1)} %get-tuple-element.58), channel_id=1, source_target_pairs={{0,8},{1,9},{2,10},{3,11},{4,12},{5,13},{6,14},{7,15},{8,0},{9,1},... | collective-permute-start | bytes 786440 | tf_op jit(solution)/shard_map/ppermute | solution.py:651

commit v6 on v5

--- a/solution.py
+++ b/solution.py
@@ -147,8 +147,8 @@
 
 def pack_kernel(
     where_ref, strain_in, plastic_in, alpha_in, kappa_in, flags,
-    strain, plastic, alpha, kappa, turned, z_a, z_b, yext, xext,
-    flags_v, up_trial, up_alpha, up_drive, low_trial, low_alpha, low_drive, sems,
+    strain, plastic, alpha, turned, z_b, z_a, yext,
+    kappa_high, kappa_low, flags_v, up_trial, up_alpha, up_drive, low_trial, low_alpha, low_drive, sems,
 ):
     flags_copy = pltpu.make_async_copy(flags, flags_v, sems.at[CHUNKS, 0])
     flags_copy.start()
@@ -158,14 +158,19 @@
         pairs = [(strain_in.at[:, part], strain.at[:, part])]
         pairs += [
             (src.at[part], dst.at[part])
-            for src, dst in ((plastic_in, plastic), (alpha_in, alpha), (kappa_in, kappa))
+            for src, dst in ((plastic_in, plastic), (alpha_in, alpha))
         ]
+        pairs.append((kappa_in.at[part, :, 128:256], kappa_high.at[part]))
         copies.append(
             [pltpu.make_async_copy(src, dst, sems.at[c, i]) for i, (src, dst) in enumerate(pairs)]
         )
     for group in copies:
         for copy in group:
             copy.start()
+    row_copy = pltpu.make_async_copy(
+        kappa_in.at[:, 24:32, 0:128], kappa_low, sems.at[CHUNKS, 1]
+    )
+    row_copy.start()
     flags_copy.wait()
     turned[...] = turned_flags(flags_v)
     flag = jnp.concatenate(
@@ -199,7 +204,8 @@
             place(up_alpha, tile(alpha, 1), 7)
             place(up_drive, field_of(s0, s1, s2), 7)
             mixed = up_drive[...]
-            for e, value in enumerate((s1, s2, tile(kappa, 1))):
+            edge = kappa_high[4 * g : 4 * g + 4].reshape(128, 128)
+            for e, value in enumerate((s1, s2, edge)):
                 moved = pltpu.roll(value, (9 + e + 16 * g) % 128, 1)
                 mixed = jnp.where(lane == 16 * g + 8 + e, moved, mixed)
             up_drive[...] = mixed
@@ -208,16 +214,14 @@
             place(low_alpha, tile(alpha, 0), 0)
             place(low_drive, field_of(s0, s1, s2), 0)
 
-    trial = strain[0, 31] - plastic[31]
-    here = (rows((32, 256)) == 31).astype(F32)
-    flag_x = jnp.dot(turned[...], here, preferred_element_type=F32)
-    xext[0] = trial - newton_plastic(trial, alpha[31]) * flag_x
     trial = strain[0, :, 31, :] - plastic[:, 31, :]
     flag_y = jnp.broadcast_to(flags_v[:, 31:32].astype(F32), (32, 256))
     yext[0] = trial - newton_plastic(trial, alpha[:, 31, :]) * flag_y
-    for e, ref in enumerate((strain.at[1], strain.at[2], kappa)):
-        xext[1 + e] = ref[31]
-        yext[1 + e] = ref[:, 31, :]
+    yext[1] = strain[1, :, 31, :]
+    yext[2] = strain[2, :, 31, :]
+    row_copy.wait()
+    yext[3, :, 0:128] = kappa_low[:, 7, :]
+    yext[3, :, 128:256] = kappa_high[:, 31, :]
 
     increment = newton_plastic(up_trial[...], up_alpha[...]) * flag
     free = pltpu.roll(up_trial[...] - increment, 1, 1)
@@ -236,7 +240,7 @@
     by_parity(lax.rem(where_ref[2], 2) == 0, z_a, z_b, store)
 
 
-def inner_kernel(strain, plastic, alpha, turned, bz, smooth, free, field):
+def inner_kernel(strain, plastic, alpha, kappa, turned, bz, smooth, free, xext, field):
     @pl.loop(0, 8)
     def _(g):
         for i in range(4):
@@ -252,10 +256,12 @@
     for g in range(4):
         part = field[8 * g : 8 * g + 8].reshape(256, 256)
         smooth[8 * g : 8 * g + 8] = dot(part, bz[...]).reshape(8, 32, 256)
+    for e, ref in enumerate((free, strain.at[1], strain.at[2], kappa)):
+        xext[e] = ref[31]
 
 
 def z_kernel(
-    counts, where_ref, own, xext_in, sent_a, sent_b, got_b, got_a, _, t_low, t_high, w_low, w_own,
+    counts, where_ref, own, xext_in, sent_b, sent_a, got_b, got_a, _, t_low, t_high, w_low, w_own,
     plane, y_a, y_b, z_low, z_high, xext,
     own_low, head_rows, tail_rows, some_low, some_high, ends,
 ):
@@ -635,7 +641,7 @@
 def swap(first, second, axis):
     sizes = [lax.axis_size(a) for a in AXES]
     at = AXES.index(axis)
-    other = 2 if at == 1 else 1
+    other = 0 if at == 1 else 1
 
     def route(start):
         out = []
@@ -685,7 +691,7 @@
     )
 
 
-def body(strain_in, plastic_in, alpha_in, kappa_in, flags):
+def body(strain_in, plastic_in, alpha_in, kappa, flags):
     where = jnp.stack([lax.axis_index(a) for a in AXES]).astype(jnp.int32)
     flags = flags.reshape(32, 32)
     counts = tuple(lax.axis_size(a) for a in AXES)
@@ -701,26 +707,26 @@
 
     whole_in = [
         pltpu.with_memory_space_constraint(v, pltpu.HBM)
-        for v in (strain_in, plastic_in, alpha_in, kappa_in, flags)
+        for v in (strain_in, plastic_in, alpha_in, kappa, flags)
     ]
     ends, eight = shape_of(4, 32, 256), shape_of(8, 32, 256)
     square = shape_of(128, 128)
-    strain, plastic, alpha, kappa, turned, z_a, z_b, yext, xext = call(
+    strain, plastic, alpha, turned, z_b, z_a, yext = call(
         pack_kernel,
         "pack",
         [SM] + [HBM] * 5,
         [
-            shape_of(3, 32, 32, 256), BLOCK, BLOCK, BLOCK, shape_of(32, 32), square, square,
-            ends, ends,
+            shape_of(3, 32, 32, 256), BLOCK, BLOCK, shape_of(32, 32), square, square, ends,
         ],
-        scratch=[pltpu.VMEM((32, 32), jnp.int32)] + [vmem(128, 128)] * 6
+        scratch=[vmem(32, 32, 128), vmem(32, 8, 128), pltpu.VMEM((32, 32), jnp.int32)]
+        + [vmem(128, 128)] * 6
         + [pltpu.SemaphoreType.DMA((CHUNKS + 1, 4))],
     )(where, *whole_in)
     got_a, got_b = swap(z_a, z_b, "gz")
     face_ext = to_next(yext, "gy")
-    own, free = call(
-        inner_kernel, "inner", [VM] * 5, [BLOCK, BLOCK], scratch=[vmem(32, 32, 256)]
-    )(strain, plastic, alpha, turned, z_band(256))
+    own, free, xext = call(
+        inner_kernel, "inner", [VM] * 6, [BLOCK, BLOCK, ends], scratch=[vmem(32, 32, 256)]
+    )(strain, plastic, alpha, kappa, turned, z_band(256))
     t_low, t_high = z_low_rows(), z_high_rows()
     plane, y_a, y_b, z_low, z_high, xext = call(
         functools.partial(z_kernel, counts),
@@ -730,7 +736,7 @@
         scratch=[vmem(128, 128)] + [vmem(32, 128)] * 2 + [vmem(512, 128)] * 2
         + [vmem(2, 32, 8, 256)],
     )(
-        where, own, xext, z_a, z_b, got_b, got_a, face_ext,
+        where, own, xext, z_b, z_a, got_b, got_a, face_ext,
         t_low, t_high, plane_from_low(), plane_from_own(),
     )
     got_a, got_b = swap(y_a, y_b, "gy")

time: 40 us -> 38 us (0.950); the launches traced: 39.4 us -> 37.9 us
  starting transfers between devices: 12.9 us -> 11.8 us
    ppermute x4, starting transfers between devices: 11 us -> 10.3 us  [swap(): lax.ppermute(second, AXES, route(1))]
    ppermute x4, starting transfers between devices: 1.79 us -> 1.36 us  [swap(): lax.ppermute(first, AXES, route(0))]
  transfers between devices with their start and end apart: 9 -> 9, of which waited for: 3 -> 3; matrix products, arithmetic and copies ran while one was open for 0% -> 0% of each run, Pallas kernels for 25% -> 26%
where the time goes in v6:
time: 38 us; the launch traced here: 37.9 us
  Pallas kernels  19.6 us (52%)
  starting transfers between devices  11.8 us (31%)
  waiting for transfers between devices  5.43 us (14%)
  between operations  0.98 us (3%)
    ppermute x4, starting transfers between devices, swap(): lax.ppermute(second, AXES, route(1))  10.3 us
    ppermute x4, waiting for transfers between devices, swap(): lax.ppermute(second, AXES, route(1))  5.41 us
    pallas_call x1, Pallas kernels, body(): call(functools.partial(middle_kernel, extents), 'middle', [SM] + [VM] * 1...  4.84 us
    pallas_call x1, Pallas kernels, body(): call(pack_kernel, 'pack', [SM] + [HBM] * 5, [shape_of(3, 32, 32, 256), BL...  4.06 us
    pallas_call x1, Pallas kernels, body(): call(functools.partial(outer_kernel, extents), 'outer', [SM] + [VM] * 11...  2.73 us
    pallas_call x1, Pallas kernels, body(): call(inner_kernel, 'inner', [VM] * 6, [BLOCK, BLOCK, ends], scratch=[vmem...  2.71 us
    pallas_call x1, Pallas kernels, body(): call(own_rows_kernel, 'own_rows', [VM] * 6, [BLOCK, FACE], scratch=[vmem(...  2.12 us
    pallas_call x1, Pallas kernels, body(): call(functools.partial(y_kernel, counts), 'along_y', [SM] + [VM] * 10, [s...  1.57 us
  transfers between devices with their start and end apart: 9, of which 3 were waited for; matrix products, arithmetic and copies ran while one was open for 0% of the time, Pallas kernels for 26%

profile of v6, /device:TPU:120, one launch (start us, length us, event | category | flops | bytes accessed | tf_op | source)
XLA Modules:
  0.0 37.9 jit_solution(5124861288996331910)
XLA Ops:
  0.6 0.1 pad_add_fusion.where_ref
  0.7 0.0 copy-start
  0.7 0.0 copy-start.1
  0.7 4.1 %pack.1 = (f32[3,32,32,256]{3,2,1,0:T(8,128)S(1)}, f32[32,32,256]{2,1,0:T(8,128)S(1)}, f32[32,32,256]{2,1,0:T(8,128)S(1)}, f32[32,32]{1,0:T(8,128)S(1)}, f32[128...) custom-call(s32[3]{0:T(128)S(1)} %pad_add_fusion.where_ref, f32[3,32,32,256]{3,2,1,0:T(8,128)} %strain_in.1, ...), custom_call_target="tpu_custom_call" | custom-call | tf_op jit(solution)/shard_map/pack/pallas_call | solution.py:714
  4.8 0.1 collective-permute-start.2
  4.9 3.5 %collective-permute-start = (f32[128,128]{1,0:T(8,128)S(1)}, f32[128,128]{1,0:T(8,128)S(1)}, u32[]{:S(2)}, u32[]{:S(2)}) collective-permute-start(f32[128,128]{1,0:T(8,128)S(1)} %get-tuple-element.38.sent_b), channel_id=1, source_target_pairs={{0,8},{1,2},{2,1},{3,4},{4,3},{5,6},{6,5},{7,15},{8,0},{9,10},{10,... | collective-permute-start | bytes 196616 | tf_op jit(solution)/shard_map/ppermute | solution.py:657
  8.4 0.0 collective-permute-start.1
  8.4 0.0 copy-done
  8.4 0.0 copy-done.1
  8.4 0.0 copy-start.2
  8.4 0.0 copy-start.3
  8.4 0.0 copy-start.7
  8.4 0.0 copy-start.8
  8.4 0.0 copy-start.9
  8.5 0.0 copy-start.5
  8.5 0.0 copy-start.6
  8.5 2.7 %inner.1 = (f32[32,32,256]{2,1,0:T(8,128)S(1)}, f32[32,32,256]{2,1,0:T(8,128)S(1)}, f32[4,32,256]{2,1,0:T(8,128)S(1)}) custom-call(f32[3,32,32,256]{3,2,1,0:T(8,128)S(1)} %get-tuple-element.31.strain, f32[32,32,256]{2,1,0:T(8,128)S(1)} %get-tuple-element.32.plastic, f32[32,32,256]{2,1,0:T(8,128)S(1)} %get-tuple-element.33.alpha, f32[32,32,256]{2,1,0:T(8,128)S(1)} %copy-done, ...), custom_call_target="tpu_custom_call" | custom-call | tf_op jit(solution)/shard_map/inner/pallas_call | solution.py:727
  11.2 0.0 copy-start.4
  11.2 2.1 %collective-permute-done.got_b = f32[128,128]{1,0:T(8,128)S(1)} collective-permute-done((f32[128,128]{1,0:T(8,128)S(1)}, f32[128,128]{1,0:T(8,128)S(1)}, u32[]{:S(2)}, u32[]{:S(2)}) %collective-permute-start) | collective-permute-done | bytes 65568 | tf_op jit(solution)/shard_map/ppermute | solution.py:657
  13.3 0.0 collective-permute-done.1.got_a
  13.3 0.0 collective-permute-done.2._.face_ext
  13.3 0.0 copy-done.2
  13.3 0.0 copy-done.3
  13.3 0.0 copy-done.7
  13.4 0.0 copy-done.8
  13.4 1.6 %along_z.1 = (f32[32,256]{1,0:T(8,128)S(1)}, f32[8,32,256]{2,1,0:T(8,128)S(1)}, f32[8,32,256]{2,1,0:T(8,128)S(1)}, f32[128,128]{1,0:T(8,128)S(1)}, f32[128,128]{1,0:T(8,128)S(1)}, /*index=5*/f32[4,32,256]{2,1,0:T(8,128)S(1)}) custom-call(s32[3]{0:T(128)S(1)} %pad_add_fusion.where_ref, f32[32,32,256]{2,1,0:T(8,128)S(1)} %get-tuple-element.36.own, ...), custom_call_target="tpu_custom_call" | custom-call | tf_op jit(solution)/shard_map/along_z/pallas_call | solution.py:731
  14.9 0.5 %collective-permute-start.3 = (f32[8,32,256]{2,1,0:T(8,128)S(1)}, f32[8,32,256]{2,1,0:T(8,128)S(1)}, u32[]{:S(2)}, u32[]{:S(2)}) collective-permute-start(f32[8,32,256]{2,1,0:T(8,128)S(1)} %get-tuple-element.46), channel_id=1, source_target_pairs={{0,32},{1,33},{2,34},{3,35},{4,36},{5,37},{6,38},{7,39},{8,16},{9,... | collective-permute-start | bytes 786440 | tf_op jit(solution)/shard_map/ppermute | solution.py:657
  15.4 0.0 collective-permute-start.4
  15.4 1.3 %collective-permute-start.6 = (f32[4,32,256]{2,1,0:T(8,128)S(1)}, f32[4,32,256]{2,1,0:T(8,128)S(1)}, u32[]{:S(2)}, u32[]{:S(2)}) collective-permute-start(f32[4,32,256]{2,1,0:T(8,128)S(1)} %get-tuple-element.48), channel_id=1, source_target_pairs={{0,32},{1,33},{2,34},{3,35},{4,36},{5,37},{6,38},{7,39},{8,40},{9,... | collective-permute-start | bytes 393224 | tf_op jit(solution)/shard_map/ppermute | solution.py:657
  16.7 3.1 %collective-permute-start.5 = (f32[4,32,256]{2,1,0:T(8,128)S(1)}, f32[4,32,256]{2,1,0:T(8,128)S(1)}, u32[]{:S(2)}, u32[]{:S(2)}) collective-permute-start(f32[4,32,256]{2,1,0:T(8,128)S(1)} %get-tuple-element.48), channel_id=1, source_target_pairs={{0,8},{1,9},{2,10},{3,11},{4,12},{5,13},{6,14},{7,15},{8,0},{9,1},... | collective-permute-start | bytes 393224 | tf_op jit(solution)/shard_map/ppermute | solution.py:657
  19.8 0.0 copy-done.9
  19.8 2.1 %own_rows.1 = (f32[32,32,256]{2,1,0:T(8,128)S(1)}, f32[32,256]{1,0:T(8,128)S(1)}) custom-call(f32[32,32,256]{2,1,0:T(8,128)S(1)} %get-tuple-element.36.own, f32[128,128]{1,0:T(8,128)S(1)} %get-tuple-element.41.z_low, f32[128,128]{1,0:T(8,128)S(1)} %get-tuple-element.42.z_high, f32[128,128]{1,0:T(8,128)S(1)} %copy-done.3, f32[128,128]{1,0:T(8,128)S(1)} %copy-done.2, ...), custom_call_target="tpu_custom_call" | custom-call | tf_op jit(solution)/shard_map/own_rows/pallas_call | solution.py:744
  21.9 0.0 collective-permute-done.6.ext_a
  22.0 1.5 %collective-permute-done.5.ext_b = f32[4,32,256]{2,1,0:T(8,128)S(1)} collective-permute-done((f32[4,32,256]{2,1,0:T(8,128)S(1)}, f32[4,32,256]{2,1,0:T(8,128)S(1)}, u32[]{:S(2)}, u32[]{:S(2)}) %collective-permute-start.5) | collective-permute-done | bytes 131104 | tf_op jit(solution)/shard_map/ppermute | solution.py:657
  23.5 0.0 collective-permute-done.3.got_b
  23.5 0.0 collective-permute-done.4.got_a
  23.5 0.0 copy-done.5
  23.5 0.0 copy-done.6
  23.5 1.6 %along_y.1 = (f32[16,32,256]{2,1,0:T(8,128)S(1)}, f32[32,256]{1,0:T(8,128)S(1)}, f32[32,256]{1,0:T(8,128)S(1)}, f32[32,16,256]{2,1,0:T(8,128)S(1)}, f32[8,32,256...) custom-call(s32[3]{0:T(128)S(1)} %pad_add_fusion.where_ref, ...), custom_call_target="tpu_custom_call" | custom-call | tf_op jit(solution)/shard_map/along_y/pallas_call | solution.py:752
  25.0 0.1 collective-permute-start.7
  25.1 3.2 %collective-permute-start.8 = (f32[8,32,256]{2,1,0:T(8,128)S(1)}, f32[8,32,256]{2,1,0:T(8,128)S(1)}, u32[]{:S(2)}, u32[]{:S(2)}) collective-permute-start(f32[8,32,256]{2,1,0:T(8,128)S(1)} %get-tuple-element.56), channel_id=1, source_target_pairs={{0,8},{1,9},{2,10},{3,11},{4,12},{5,13},{6,14},{7,15},{8,0},{9,1},... | collective-permute-start | bytes 786440 | tf_op jit(solution)/shard_map/ppermute | solution.py:657
  28.3 0.0 copy-done.4
  28.3 4.8 %middle.1 = (f32[32,32,256]{2,1,0:T(8,128)}, f32[32,32,256]{2,1,0:T(8,128)}, f32[18,32,256]{2,1,0:T(8,128)S(1)}, f32[32,256]{1,0:T(8,128)S(1)}) custom-call(s32[3]{0:T(128)S(1)} %pad_add_fusion.where_ref, f32[3,32,32,256]{3,2,1,0:T(8,128)S(1)} %get-tuple-element.31.strain, f32[32,32,256]{2,1,0:T(8,128)S(1)} %get-tuple-element.35.free, ...), custom_call_target="tpu_custom_call" | custom-call | tf_op jit(solution)/shard_map/middle/pallas_call | solution.py:766
  33.2 0.0 collective-permute-done.7.got_a
  33.2 1.8 %collective-permute-done.8.got_b = f32[8,32,256]{2,1,0:T(8,128)S(1)} collective-permute-done((f32[8,32,256]{2,1,0:T(8,128)S(1)}, f32[8,32,256]{2,1,0:T(8,128)S(1)}, u32[]{:S(2)}, u32[]{:S(2)}) %collective-permute-start.8) | collective-permute-done | bytes 262176 | tf_op jit(solution)/shard_map/ppermute | solution.py:657
  35.0 2.7 %outer.1 = (f32[32,32,256]{2,1,0:T(8,128)}, f32[32,32,256]{2,1,0:T(8,128)}) custom-call(s32[3]{0:T(128)S(1)} %pad_add_fusion.where_ref, f32[3,32,32,256]{3,2,1,0:T(8,128)S(1)} %get-tuple-element.31.strain, f32[32,32,256]{2,1,0:T(8,128)S(1)} %get-tuple-element.35.free, f32[32,32,256]{2,1,0:T(8,128)S(1)} %copy-done, ...), custom_call_target="tpu_custom_call", output_to_operand_aliasing={{0}: (12, {}), {1}: (13, {})} | custom-call | tf_op jit(solution)/shard_map/outer/pallas_call | solution.py:774
Async XLA Ops:
  0.7 7.7 %copy-start = (f32[32,32,256]{2,1,0:T(8,128)S(1)}, f32[32,32,256]{2,1,0:T(8,128)}, u32[]{:S(2)}) copy-start(f32[32,32,256]{2,1,0:T(8,128)} %kappa.5) | copy-start | bytes 3145732
  0.7 7.7 %copy-start.1 = (f32[256,256]{1,0:T(8,128)S(1)}, f32[256,256]{1,0:T(8,128)}, u32[]{:S(2)}) copy-start(f32[256,256]{1,0:T(8,128)} %constant.30.clone.bz) | copy-start | bytes 786436
  4.8 8.6 %collective-permute-start.2 = (f32[4,32,256]{2,1,0:T(8,128)S(1)}, f32[4,32,256]{2,1,0:T(8,128)S(1)}, u32[]{:S(2)}, u32[]{:S(2)}) collective-permute-start(f32[4,32,256]{2,1,0:T(8,128)S(1)} %get-tuple-element.40), channel_id=1, source_target_pairs={{0,8},{8,16},{16,24},{24,0},{1,9},{9,17},{17,25},{25,1},{2,10},{10... | collective-permute-start | bytes 393224 | tf_op jit(solution)/shard_map/ppermute | solution.py:662
  4.9 8.5 %collective-permute-start = (f32[128,128]{1,0:T(8,128)S(1)}, f32[128,128]{1,0:T(8,128)S(1)}, u32[]{:S(2)}, u32[]{:S(2)}) collective-permute-start(f32[128,128]{1,0:T(8,128)S(1)} %get-tuple-element.38.sent_b), channel_id=1, source_target_pairs={{0,8},{1,2},{2,1},{3,4},{4,3},{5,6},{6,5},{7,15},{8,0},{9,10},{10,... | collective-permute-start | bytes 196616 | tf_op jit(solution)/shard_map/ppermute | solution.py:657
  8.4 4.9 %collective-permute-start.1 = (f32[128,128]{1,0:T(8,128)S(1)}, f32[128,128]{1,0:T(8,128)S(1)}, u32[]{:S(2)}, u32[]{:S(2)}) collective-permute-start(f32[128,128]{1,0:T(8,128)S(1)} %get-tuple-element.39.sent_a), channel_id=1, source_target_pairs={{0,1},{1,0},{2,3},{3,2},{4,5},{5,4},{6,7},{7,6},{8,9},{9,8},{10,11... | collective-permute-start | bytes 196616 | tf_op jit(solution)/shard_map/ppermute | solution.py:657
  8.4 4.9 %copy-start.2 = (f32[128,128]{1,0:T(8,128)S(1)}, f32[128,128]{1,0:T(8,128)}, u32[]{:S(2)}) copy-start(f32[128,128]{1,0:T(8,128)} %constant.32.clone.t_high) | copy-start | bytes 196612
  8.4 4.9 %copy-start.3 = (f32[128,128]{1,0:T(8,128)S(1)}, f32[128,128]{1,0:T(8,128)}, u32[]{:S(2)}) copy-start(f32[128,128]{1,0:T(8,128)} %constant.31.clone.t_low) | copy-start | bytes 196612
  8.4 4.9 %copy-start.7 = (f32[40,128]{1,0:T(8,128)S(1)}, f32[40,128]{1,0:T(8,128)}, u32[]{:S(2)}) copy-start(f32[40,128]{1,0:T(8,128)} %constant.34.clone.w_own) | copy-start | bytes 61444
  8.4 4.9 %copy-start.8 = (f32[40,128]{1,0:T(8,128)S(1)}, f32[40,128]{1,0:T(8,128)}, u32[]{:S(2)}) copy-start(f32[40,128]{1,0:T(8,128)} %constant.33.clone.w_low) | copy-start | bytes 61444
  8.4 11.4 %copy-start.9 = (f32[40,32]{1,0:T(8,128)S(1)}, f32[40,32]{1,0:T(8,128)}, u32[]{:S(2)}) copy-start(f32[40,32]{1,0:T(8,128)} %constant.35.clone.my) | copy-start | bytes 15364
  8.5 15.0 %copy-start.5 = (f32[128,128]{1,0:T(8,128)S(1)}, f32[128,128]{1,0:T(8,128)}, u32[]{:S(2)}) copy-start(f32[128,128]{1,0:T(8,128)} %constant.37.clone.v) | copy-start | bytes 196612
  8.5 15.0 %copy-start.6 = (f32[40,16]{1,0:T(8,128)S(1)}, f32[40,16]{1,0:T(8,128)}, u32[]{:S(2)}) copy-start(f32[40,16]{1,0:T(8,128)} %constant.36.clone.my) | copy-start | bytes 7684
  11.2 17.1 %copy-start.4 = (f32[40,128]{1,0:T(8,128)S(1)}, f32[40,128]{1,0:T(8,128)}, u32[]{:S(2)}) copy-start(f32[40,128]{1,0:T(8,128)} %constant.38.clone.my) | copy-start | bytes 61444
  14.9 8.5 %collective-permute-start.3 = (f32[8,32,256]{2,1,0:T(8,128)S(1)}, f32[8,32,256]{2,1,0:T(8,128)S(1)}, u32[]{:S(2)}, u32[]{:S(2)}) collective-permute-start(f32[8,32,256]{2,1,0:T(8,128)S(1)} %get-tuple-element.46), channel_id=1, source_target_pairs={{0,32},{1,33},{2,34},{3,35},{4,36},{5,37},{6,38},{7,39},{8,16},{9,... | collective-permute-start | bytes 786440 | tf_op jit(solution)/shard_map/ppermute | solution.py:657
  15.4 8.0 %collective-permute-start.4 = (f32[8,32,256]{2,1,0:T(8,128)S(1)}, f32[8,32,256]{2,1,0:T(8,128)S(1)}, u32[]{:S(2)}, u32[]{:S(2)}) collective-permute-start(f32[8,32,256]{2,1,0:T(8,128)S(1)} %get-tuple-element.47), channel_id=1, source_target_pairs={{0,8},{1,9},{2,10},{3,11},{4,12},{5,13},{6,14},{7,15},{8,0},{9,1},... | collective-permute-start | bytes 786440 | tf_op jit(solution)/shard_map/ppermute | solution.py:657
  15.4 6.5 %collective-permute-start.6 = (f32[4,32,256]{2,1,0:T(8,128)S(1)}, f32[4,32,256]{2,1,0:T(8,128)S(1)}, u32[]{:S(2)}, u32[]{:S(2)}) collective-permute-start(f32[4,32,256]{2,1,0:T(8,128)S(1)} %get-tuple-element.48), channel_id=1, source_target_pairs={{0,32},{1,33},{2,34},{3,35},{4,36},{5,37},{6,38},{7,39},{8,40},{9,... | collective-permute-start | bytes 393224 | tf_op jit(solution)/shard_map/ppermute | solution.py:657
  16.7 6.8 %collective-permute-start.5 = (f32[4,32,256]{2,1,0:T(8,128)S(1)}, f32[4,32,256]{2,1,0:T(8,128)S(1)}, u32[]{:S(2)}, u32[]{:S(2)}) collective-permute-start(f32[4,32,256]{2,1,0:T(8,128)S(1)} %get-tuple-element.48), channel_id=1, source_target_pairs={{0,8},{1,9},{2,10},{3,11},{4,12},{5,13},{6,14},{7,15},{8,0},{9,1},... | collective-permute-start | bytes 393224 | tf_op jit(solution)/shard_map/ppermute | solution.py:657
  25.0 8.2 %collective-permute-start.7 = (f32[8,32,256]{2,1,0:T(8,128)S(1)}, f32[8,32,256]{2,1,0:T(8,128)S(1)}, u32[]{:S(2)}, u32[]{:S(2)}) collective-permute-start(f32[8,32,256]{2,1,0:T(8,128)S(1)} %get-tuple-element.55), channel_id=1, source_target_pairs={{0,32},{1,33},{2,34},{3,35},{4,36},{5,37},{6,38},{7,39},{8,40},{9,... | collective-permute-start | bytes 786440 | tf_op jit(solution)/shard_map/ppermute | solution.py:657
  25.1 9.9 %collective-permute-start.8 = (f32[8,32,256]{2,1,0:T(8,128)S(1)}, f32[8,32,256]{2,1,0:T(8,128)S(1)}, u32[]{:S(2)}, u32[]{:S(2)}) collective-permute-start(f32[8,32,256]{2,1,0:T(8,128)S(1)} %get-tuple-element.56), channel_id=1, source_target_pairs={{0,8},{1,9},{2,10},{3,11},{4,12},{5,13},{6,14},{7,15},{8,0},{9,1},... | collective-permute-start | bytes 786440 | tf_op jit(solution)/shard_map/ppermute | solution.py:657

commit v7 on v6

--- a/solution.py
+++ b/solution.py
@@ -30,19 +30,13 @@
     return np.array([[band(i - k) for k in range(width)] for i in range(width)], np.float32)
 
 
-def z_low_rows():
-    out = np.zeros((128, 128), np.float32)
+def z_halo_rows():
+    out = np.zeros((256, 256), np.float32)
     for r in range(128):
-        if r % 16 < 7:
-            out[r] = [band(k - (r % 16 - 7)) for k in range(128)]
-    return out
-
-
-def z_high_rows():
-    out = np.zeros((128, 128), np.float32)
-    for r in range(128):
-        if r % 16 < 6:
-            out[r] = [band(128 + r % 16 - k) for k in range(128)]
+        c = r % 16
+        for k in range(256):
+            out[r, k] = band(k - (c - 7)) if c < 7 else 0.0
+            out[128 + r, k] = band(256 + c - k) if c < 6 else 0.0
     return out
 
 
@@ -261,43 +255,40 @@
 
 
 def z_kernel(
-    counts, where_ref, own, xext_in, sent_b, sent_a, got_b, got_a, _, t_low, t_high, w_low, w_own,
-    plane, y_a, y_b, z_low, z_high, xext,
-    own_low, head_rows, tail_rows, some_low, some_high, ends,
+    counts, where_ref, own, xext_in, sent_b, sent_a, got_b, got_a, _, t, w,
+    plane, y_a, y_b, z_both, xext, turn, head_rows, tail_rows, some, ends,
 ):
     xext[...] = xext_in[...]
 
     def choose(upper, lower):
-        z_high[...] = upper[0][...]
-        z_low[...] = lower[0][...]
-        own_low[...] = lower[1][...]
+        z_both[:, 128:256] = upper[0][...]
+        z_both[:, 0:128] = lower[0][...]
+        turn[:, 0:128] = lower[0][...]
+        turn[:, 128:256] = lower[1][...]
 
     by_parity(lax.rem(where_ref[2], 2) == 0, (got_a, sent_a), (got_b, sent_b), choose)
 
     @pl.when(where_ref[2] == 0)
     def _():
-        z_low[...] = jnp.zeros_like(z_low)
+        z_both[:, 0:128] = jnp.zeros((128, 128), F32)
+        turn[:, 0:128] = jnp.zeros((128, 128), F32)
 
     @pl.when(where_ref[2] == counts[2] - 1)
     def _():
-        z_high[...] = jnp.zeros_like(z_high)
-
-    group = lanes((8, 128)) // 16
+        z_both[:, 128:256] = jnp.zeros((128, 128), F32)
+
+    group = lanes((8, 256)) % 128 // 16
     for half in range(2):
         for x in range(32):
             start = 32 * (x % 4) + 24 * half
             at = 256 * half + 8 * x
-            inside = group == x // 4
-            for some, ref in ((some_low, z_low), (some_high, z_high)):
-                some[at : at + 8, :] = jnp.where(inside, ref[start : start + 8, :], 0.0)
-    first = dot(some_low[...], t_low[...])
-    last = dot(some_high[...], t_high[...])
+            some[at : at + 8, :] = jnp.where(group == x // 4, z_both[start : start + 8, :], 0.0)
+    added = dot(some[...], t[...])
     for half in range(2):
-        part = slice(256 * half, 256 * half + 256)
         here = slice(24 * half, 24 * half + 8)
-        ends[half, :, :, 0:128] = own[:, here, 0:128] + first[part].reshape(32, 8, 128)
-        ends[half, :, :, 128:256] = own[:, here, 128:256] + last[part].reshape(32, 8, 128)
-    turned = dot_lanes(w_low[...], z_low[...]) + dot_lanes(w_own[...], own_low[...])
+        part = added[256 * half : 256 * half + 256]
+        ends[half] = own[:, here, :] + part.reshape(32, 8, 256)
+    turned = dot_lanes(w[...], turn[...])
     lane = lanes((8, 128))
     for b in range(4):
         head = jnp.zeros((8, 128), F32)
@@ -322,20 +313,35 @@
     by_parity(lax.rem(where_ref[1], 2) == 0, y_a, y_b, store)
 
 
-def own_rows_kernel(own, z_low, z_high, t_low, t_high, my, out, out_face, some, smooth):
-    group = lanes((128, 128)) // 16
-    for half, (ref, band_rows) in enumerate(((z_low, t_low), (z_high, t_high))):
-        for g in range(8):
-            some[128 * g : 128 * g + 128, :] = jnp.where(group == g, ref[...], 0.0)
-        here = slice(128 * half, 128 * half + 128)
-        for c in range(4):
-            part = dot(some[256 * c : 256 * c + 256, :], band_rows[...])
-            at = slice(8 * c, 8 * c + 8)
-            smooth[at, :, here] = own[at, :, here] + part.reshape(8, 32, 128)
+def own_rows_kernel(
+    extents, where_ref, own, z_both, t, my,
+    out, out_face, inv_x, inv_yz, inv_face, inv_plane, some, smooth,
+):
+    group = lanes((128, 256)) % 128 // 16
+    for g in range(8):
+        some[128 * g : 128 * g + 128, :] = jnp.where(group == g, z_both[...], 0.0)
+    for c in range(4):
+        part = dot(some[256 * c : 256 * c + 256, :], t[...])
+        at = slice(8 * c, 8 * c + 8)
+        smooth[at] = own[at] + part.reshape(8, 32, 256)
     for x in range(32):
         both = dot(my[...], smooth[x])
         out[x] = both[0:32]
         out_face[x : x + 1, :] = both[32:33]
+
+    nx, ny, nz = extents
+    ix, iy, iz = where_ref[0], where_ref[1], where_ref[2]
+    shape, small, line = (40, 256), (32, 256), (1, 256)
+    row, lane = rows(shape), lanes(shape)
+    invx = inverse_total(ix * 32 + jnp.where(row < 32, row, -1), nx)
+    inv_x[...] = invx
+    invz = inverse_total(iz * 256 + lanes(line), nz)
+    inv_yz[...] = inverse_total(iy * 32 + rows(small), ny) * invz
+    at_y = inverse_total(jnp.full(line, iy * 32 - 1, jnp.int32), ny)
+    inv_face[...] = invx * (at_y * invz)
+    at_z = inverse_total(jnp.full(line, iz * 256 - 1, jnp.int32), nz)
+    invy = inverse_total(iy * 32 - 1 + jnp.minimum(lanes(line), 32), ny)
+    inv_plane[...] = invx * (invy * at_z)
 
 
 def y_kernel(
@@ -369,8 +375,10 @@
     for i in range(16):
         x = i if i < 8 else i + 16
         both = dot(my[...], halo[x])
-        edges[i] = own[x] + both[0:32]
-        out_face[x : x + 1, :] = own_face[x : x + 1, :] + both[32:33]
+        edges[i, 0:8, :] = own[x, 0:8, :] + both[0:8]
+        edges[i, 8:24, :] = own[x, 8:24, :]
+        edges[i, 24:32, :] = own[x, 24:32, :] + both[8:16]
+        out_face[x : x + 1, :] = own_face[x : x + 1, :] + both[16:17]
     mine, low, high = plane[...], plane_low[...], plane_high[...]
     lane = lanes((32, 256))
     total = jnp.zeros((32, 256), F32)
@@ -421,16 +429,9 @@
         side[...] = jnp.zeros_like(side)
 
 
-def faces(extents, at, mx, face_all, plane_all, side, face_e, face_a, column, inv_x, inv_yz):
-    nx, ny, nz = extents
-    ix, iy, iz = at
+def faces(mx, face_all, plane_all, side, face_e, face_a, column, inv_face, inv_plane):
     shape = (40, 256)
     row, lane = rows(shape), lanes(shape)
-    invx = inverse_total(ix * 32 + jnp.where(row < 32, row, -1), nx)
-    inv_x[...] = invx
-    small = (32, 256)
-    invz = inverse_total(iz * 256 + lanes(small), nz)
-    inv_yz[...] = inverse_total(iy * 32 + rows(small), ny) * invz
 
     def previous(value):
         return jnp.where(row == 0, value[32:33, :], pltpu.roll(value, 1, 0))
@@ -441,8 +442,7 @@
         a2 = previous(t2) + t2
         return a0 + a1, a0 - a1, a2
 
-    at_y = inverse_total(jnp.full((1, 256), iy * 32 - 1, jnp.int32), ny)
-    kap = jnp.maximum(side[3], dot(mx[...], face_all[...]) * (invx * (at_y * invz[0:1, :])))
+    kap = jnp.maximum(side[3], dot(mx[...], face_all[...]) * inv_face[...])
     integ = integrity_of(kap)
     e, _, a2 = joined(integ * side[0], integ * side[1], integ * side[2])
     face_e[...] = e[0:32]
@@ -454,9 +454,7 @@
     def value(c):
         return pltpu.roll(own, (256 - 40 * c) % 256, 1)
 
-    at_z = inverse_total(jnp.full((1, 256), iz * 256 - 1, jnp.int32), nz)
-    invy = inverse_total(iy * 32 - 1 + jnp.minimum(lane, 32), ny)
-    kap = jnp.maximum(value(4), avg * (invx * (invy * at_z)))
+    kap = jnp.maximum(value(4), avg * inv_plane[...])
     integ = integrity_of(kap)
     e, f, a2 = joined(integ * value(1), integ * value(2), integ * value(3))
     parts = e + a2 + pltpu.roll(f + a2, 255, 1)
@@ -491,9 +489,10 @@
 
 
 def middle_kernel(
-    extents, where_ref, strain, free, kappa, own, edges, halo, face, plane, face_ext, my,
+    where_ref, strain, free, kappa, own, edges, halo, face, plane, face_ext,
+    inv_x, inv_yz, inv_face, inv_plane, my,
     force, kappa_new, part, face_out,
-    ext, face_all, plane_all, side, before, face_e, face_a, column, inv_x, inv_yz,
+    ext, face_all, plane_all, side, before, face_e, face_a, column,
     force_v, kappa_v, sems,
 ):
     at = (where_ref[0], where_ref[1], where_ref[2])
@@ -503,9 +502,11 @@
         elif x >= 24:
             ext[x] = edges[x - 16]
         else:
-            both = dot(my[:, 32:48], halo[x])
-            ext[x] = own[x] + both[0:32]
-            face_out[x : x + 1, :] = face[x : x + 1, :] + both[32:33]
+            both = dot(my[0:24, 0:16], halo[x])
+            ext[x, 0:8, :] = own[x, 0:8, :] + both[0:8]
+            ext[x, 8:24, :] = own[x, 8:24, :]
+            ext[x, 24:32, :] = own[x, 24:32, :] + both[8:16]
+            face_out[x : x + 1, :] = face[x : x + 1, :] + both[16:17]
     face_out[0:8, :] = face[0:8, :]
     face_out[24:32, :] = face[24:32, :]
     for ref, value in ((face_all, face_out), (plane_all, plane)):
@@ -514,8 +515,7 @@
         ref[40:48, :] = jnp.zeros((8, 256), F32)
     fill_side(at, side, face_ext)
     faces(
-        extents, at, my.at[:, 48:96], face_all, plane_all, side,
-        face_e, face_a, column, inv_x, inv_yz,
+        my.at[:, 48:96], face_all, plane_all, side, face_e, face_a, column, inv_face, inv_plane
     )
 
     def layer(x):
@@ -555,10 +555,11 @@
 
 
 def outer_kernel(
-    extents, where_ref, strain, free, kappa, part, face, plane, face_ext, got_a, got_b, got_ext, my,
+    counts, where_ref, strain, free, kappa, part, face, plane, face_ext, got_a, got_b, got_ext,
+    inv_x, inv_yz, inv_face, inv_plane, my,
     force_in, kappa_in,
     force, kappa_new,
-    low, high, face_all, plane_all, side, before, face_e, face_a, column, inv_x, inv_yz,
+    low, high, face_all, plane_all, side, before, face_e, face_a, column,
     force_v, kappa_v, sems,
 ):
     at = (where_ref[0], where_ref[1], where_ref[2])
@@ -588,7 +589,7 @@
         for e in range(4):
             side[e, 32:33, :] = jnp.zeros((1, 256), F32)
 
-    @pl.when(at[0] == extents[0] // 32 - 1)
+    @pl.when(at[0] == counts[0] - 1)
     def _():
         high[...] = jnp.zeros_like(high)
         face_all[40:48, :] = jnp.zeros((8, 256), F32)
@@ -597,8 +598,7 @@
     face_all[8:40, :] = face[...]
     plane_all[8:40, :] = plane[...]
     faces(
-        extents, at, my.at[:, 48:96], face_all, plane_all, side,
-        face_e, face_a, column, inv_x, inv_yz,
+        my.at[:, 48:96], face_all, plane_all, side, face_e, face_a, column, inv_face, inv_plane
     )
 
     def layer(x):
@@ -701,8 +701,9 @@
     rows_halo = np.concatenate(
         [rows_all[:, 1:8], np.zeros((40, 1), np.float32), rows_all[:, 40:48]], axis=1
     )
+    rows_halo = np.concatenate([rows_halo[0:8], rows_halo[24:40]], axis=0)
     rows_three = np.zeros((40, 128), np.float32)
-    rows_three[:, 32:48] = rows_halo
+    rows_three[0:24, 0:16] = rows_halo
     rows_three[:, 48:96] = rows_all
 
     whole_in = [
@@ -727,27 +728,24 @@
     own, free, xext = call(
         inner_kernel, "inner", [VM] * 6, [BLOCK, BLOCK, ends], scratch=[vmem(32, 32, 256)]
     )(strain, plastic, alpha, kappa, turned, z_band(256))
-    t_low, t_high = z_low_rows(), z_high_rows()
-    plane, y_a, y_b, z_low, z_high, xext = call(
+    t = z_halo_rows()
+    w = np.concatenate([plane_from_low(), plane_from_own()], axis=1)
+    plane, y_a, y_b, z_both, xext = call(
         functools.partial(z_kernel, counts),
         "along_z",
-        [SM] + [VM] * 11,
-        [FACE, eight, eight, square, square, ends],
-        scratch=[vmem(128, 128)] + [vmem(32, 128)] * 2 + [vmem(512, 128)] * 2
-        + [vmem(2, 32, 8, 256)],
-    )(
-        where, own, xext, z_b, z_a, got_b, got_a, face_ext,
-        t_low, t_high, plane_from_low(), plane_from_own(),
-    )
+        [SM] + [VM] * 9,
+        [FACE, eight, eight, shape_of(128, 256), ends],
+        scratch=[vmem(128, 256)] + [vmem(32, 128)] * 2 + [vmem(512, 256), vmem(2, 32, 8, 256)],
+    )(where, own, xext, z_b, z_a, got_b, got_a, face_ext, t, w)
     got_a, got_b = swap(y_a, y_b, "gy")
     ext_a, ext_b = swap(xext, xext, "gx")
-    own, own_face = call(
-        own_rows_kernel,
+    own, own_face, *inverse = call(
+        functools.partial(own_rows_kernel, extents),
         "own_rows",
-        [VM] * 6,
-        [BLOCK, FACE],
-        scratch=[vmem(1024, 128), vmem(32, 32, 256)],
-    )(own, z_low, z_high, t_low, t_high, rows_own)
+        [SM] + [VM] * 4,
+        [BLOCK, FACE, shape_of(40, 256), FACE, shape_of(40, 256), shape_of(40, 256)],
+        scratch=[vmem(1024, 256), vmem(32, 32, 256)],
+    )(where, own, z_both, t, rows_own)
 
     edges, face, plane, halo, x_a, x_b, got_ext = call(
         functools.partial(y_kernel, counts),
@@ -760,27 +758,28 @@
 
     shared = [
         vmem(48, 256), vmem(48, 256), vmem(4, 40, 256), vmem(4, 32, 256),
-        vmem(32, 256), vmem(32, 256), vmem(32, 128), vmem(40, 256), vmem(32, 256),
+        vmem(32, 256), vmem(32, 256), vmem(32, 128),
         vmem(16, 32, 256), vmem(16, 32, 256), pltpu.SemaphoreType.DMA((2, 2)),
     ]
     force, kappa_new, part, face = call(
-        functools.partial(middle_kernel, extents),
+        middle_kernel,
         "middle",
-        [SM] + [VM] * 10,
+        [SM] + [VM] * 14,
         [BLOCK, BLOCK, shape_of(18, 32, 256), FACE],
         out_specs=[HBM, HBM, VM, VM],
         scratch=[vmem(32, 32, 256)] + shared,
-    )(where, strain, free, kappa, own, edges, halo, face, plane, face_ext, rows_three)
+    )(where, strain, free, kappa, own, edges, halo, face, plane, face_ext, *inverse, rows_three)
     force, kappa_new = call(
-        functools.partial(outer_kernel, extents),
+        functools.partial(outer_kernel, counts),
         "outer",
-        [SM] + [VM] * 11 + [HBM, HBM],
+        [SM] + [VM] * 15 + [HBM, HBM],
         [BLOCK, BLOCK],
         out_specs=[HBM, HBM],
         scratch=[vmem(7, 32, 256), vmem(6, 32, 256)] + shared,
-        input_output_aliases={12: 0, 13: 1},
+        input_output_aliases={16: 0, 17: 1},
     )(
-        where, strain, free, kappa, part, face, plane, face_ext, got_a, got_b, got_ext, rows_three,
+        where, strain, free, kappa, part, face, plane, face_ext, got_a, got_b, got_ext,
+        *inverse, rows_three,
         force, kappa_new,
     )
     return (force, kappa_new)

time: 38 us -> 37.8 us (level)
    ppermute x4, waiting for transfers between devices: 5.41 us -> 4.7 us  [swap(): lax.ppermute(second, AXES, route(1))]
  transfers between devices with their start and end apart: 9 -> 9, of which waited for: 3 -> 4; matrix products, arithmetic and copies ran while one was open for 0% -> 0% of each run, Pallas kernels for 26% -> 27%
where the time goes in v7:
time: 37.8 us; the launch traced here: 37.7 us
  Pallas kernels  19.8 us (52%)
  starting transfers between devices  11.8 us (31%)
  waiting for transfers between devices  5.06 us (13%)
  between operations  0.95 us (3%)
    ppermute x4, starting transfers between devices, swap(): lax.ppermute(second, AXES, route(1))  10.2 us
    ppermute x4, waiting for transfers between devices, swap(): lax.ppermute(second, AXES, route(1))  4.7 us
    pallas_call x1, Pallas kernels, body(): call(middle_kernel, 'middle', [SM] + [VM] * 14, [BLOCK, BLOCK, shape_of(1...  4.62 us
    pallas_call x1, Pallas kernels, body(): call(pack_kernel, 'pack', [SM] + [HBM] * 5, [shape_of(3, 32, 32, 256), BL...  4.06 us
    pallas_call x1, Pallas kernels, body(): call(functools.partial(own_rows_kernel, extents), 'own_rows', [SM] + [VM]...  2.89 us
    pallas_call x1, Pallas kernels, body(): call(inner_kernel, 'inner', [VM] * 6, [BLOCK, BLOCK, ends], scratch=[vmem...  2.71 us
    pallas_call x1, Pallas kernels, body(): call(functools.partial(outer_kernel, counts), 'outer', [SM] + [VM] * 15 +...  2.64 us
    ppermute x4, starting transfers between devices, swap(): lax.ppermute(first, AXES, route(0))  1.55 us
  transfers between devices with their start and end apart: 9, of which 4 were waited for; matrix products, arithmetic and copies ran while one was open for 0% of the time, Pallas kernels for 27%

profile of v7, /device:TPU:120, one launch (start us, length us, event | category | flops | bytes accessed | tf_op | source)
XLA Modules:
  0.0 37.7 jit_solution(2656641938534775715)
XLA Ops:
  0.6 0.1 pad_add_fusion.where_ref
  0.7 0.0 copy-start
  0.7 0.0 copy-start.2
  0.7 4.1 %pack.1 = (f32[3,32,32,256]{3,2,1,0:T(8,128)S(1)}, f32[32,32,256]{2,1,0:T(8,128)S(1)}, f32[32,32,256]{2,1,0:T(8,128)S(1)}, f32[32,32]{1,0:T(8,128)S(1)}, f32[128...) custom-call(s32[3]{0:T(128)S(1)} %pad_add_fusion.where_ref, f32[3,32,32,256]{3,2,1,0:T(8,128)} %strain_in.1, ...), custom_call_target="tpu_custom_call" | custom-call | tf_op jit(solution)/shard_map/pack/pallas_call | solution.py:715
  4.8 0.1 collective-permute-start.2
  4.9 3.5 %collective-permute-start = (f32[128,128]{1,0:T(8,128)S(1)}, f32[128,128]{1,0:T(8,128)S(1)}, u32[]{:S(2)}, u32[]{:S(2)}) collective-permute-start(f32[128,128]{1,0:T(8,128)S(1)} %get-tuple-element.41.sent_b), channel_id=1, source_target_pairs={{0,8},{1,2},{2,1},{3,4},{4,3},{5,6},{6,5},{7,15},{8,0},{9,10},{10,... | collective-permute-start | bytes 196616 | tf_op jit(solution)/shard_map/ppermute | solution.py:657
  8.4 0.0 collective-permute-start.1
  8.4 0.0 copy-done
  8.4 0.0 copy-done.2
  8.4 0.0 copy-start.1
  8.4 0.0 copy-start.5
  8.4 0.0 copy-start.6
  8.4 2.7 %inner.1 = (f32[32,32,256]{2,1,0:T(8,128)S(1)}, f32[32,32,256]{2,1,0:T(8,128)S(1)}, f32[4,32,256]{2,1,0:T(8,128)S(1)}) custom-call(f32[3,32,32,256]{3,2,1,0:T(8,128)S(1)} %get-tuple-element.34.strain, f32[32,32,256]{2,1,0:T(8,128)S(1)} %get-tuple-element.35.plastic, f32[32,32,256]{2,1,0:T(8,128)S(1)} %get-tuple-element.36.alpha, f32[32,32,256]{2,1,0:T(8,128)S(1)} %copy-done, ...), custom_call_target="tpu_custom_call" | custom-call | tf_op jit(solution)/shard_map/inner/pallas_call | solution.py:728
  11.2 0.0 copy-start.4
  11.2 0.0 copy-start.7
  11.2 0.0 copy-start.3
  11.2 2.1 %collective-permute-done.got_b = f32[128,128]{1,0:T(8,128)S(1)} collective-permute-done((f32[128,128]{1,0:T(8,128)S(1)}, f32[128,128]{1,0:T(8,128)S(1)}, u32[]{:S(2)}, u32[]{:S(2)}) %collective-permute-start) | collective-permute-done | bytes 65568 | tf_op jit(solution)/shard_map/ppermute | solution.py:657
  13.3 0.0 collective-permute-done.1.got_a
  13.3 0.0 collective-permute-done.2._.face_ext
  13.3 0.0 copy-done.1
  13.3 0.0 copy-done.5
  13.3 1.5 %along_z.1 = (f32[32,256]{1,0:T(8,128)S(1)}, f32[8,32,256]{2,1,0:T(8,128)S(1)}, f32[8,32,256]{2,1,0:T(8,128)S(1)}, f32[128,256]{1,0:T(8,128)S(1)}, f32[4,32,256]{2,1,0:T(8,128)S(1)}) custom-call(s32[3]{0:T(128)S(1)} %pad_add_fusion.where_ref, f32[32,32,256]{2,1,0:T(8,128)S(1)} %get-tuple-element.39.own, f32[4,32,256]{2,1,0:T(8,128)S(1)} %get-tuple-element.40.xext_in, ...), custom_call_target="tpu_custom_call" | custom-call | tf_op jit(solution)/shard_map/along_z/pallas_call | solution.py:733
  14.8 0.5 %collective-permute-start.3 = (f32[8,32,256]{2,1,0:T(8,128)S(1)}, f32[8,32,256]{2,1,0:T(8,128)S(1)}, u32[]{:S(2)}, u32[]{:S(2)}) collective-permute-start(f32[8,32,256]{2,1,0:T(8,128)S(1)} %get-tuple-element.48), channel_id=1, source_target_pairs={{0,32},{1,33},{2,34},{3,35},{4,36},{5,37},{6,38},{7,39},{8,16},{9,... | collective-permute-start | bytes 786440 | tf_op jit(solution)/shard_map/ppermute | solution.py:657
  15.3 0.0 collective-permute-start.4
  15.3 1.3 %collective-permute-start.6 = (f32[4,32,256]{2,1,0:T(8,128)S(1)}, f32[4,32,256]{2,1,0:T(8,128)S(1)}, u32[]{:S(2)}, u32[]{:S(2)}) collective-permute-start(f32[4,32,256]{2,1,0:T(8,128)S(1)} %get-tuple-element.50), channel_id=1, source_target_pairs={{0,32},{1,33},{2,34},{3,35},{4,36},{5,37},{6,38},{7,39},{8,40},{9,... | collective-permute-start | bytes 393224 | tf_op jit(solution)/shard_map/ppermute | solution.py:657
  16.6 3.1 %collective-permute-start.5 = (f32[4,32,256]{2,1,0:T(8,128)S(1)}, f32[4,32,256]{2,1,0:T(8,128)S(1)}, u32[]{:S(2)}, u32[]{:S(2)}) collective-permute-start(f32[4,32,256]{2,1,0:T(8,128)S(1)} %get-tuple-element.50), channel_id=1, source_target_pairs={{0,8},{1,9},{2,10},{3,11},{4,12},{5,13},{6,14},{7,15},{8,0},{9,1},... | collective-permute-start | bytes 393224 | tf_op jit(solution)/shard_map/ppermute | solution.py:657
  19.7 0.0 copy-done.6
  19.7 2.9 %own_rows.1 = (f32[32,32,256]{2,1,0:T(8,128)S(1)}, f32[32,256]{1,0:T(8,128)S(1)}, f32[40,256]{1,0:T(8,128)S(1)}, f32[32,256]{1,0:T(8,128)S(1)}, f32[40,256]{1,0:T(8,128)S(1)}, /*index=5*/f32[40,256]{1,0:T(8,128)S(1)}) custom-call(s32[3]{0:T(128)S(1)} %pad_add_fusion.where_ref, f32[32,32,256]{2,1,0:T(8,128)S(1)} %get-tuple-element.39.own, ...), custom_call_target="tpu_custom_call" | custom-call | tf_op jit(solution)/shard_map/own_rows/pallas_call | solution.py:742
  22.6 0.0 collective-permute-done.6.ext_a
  22.6 0.7 %collective-permute-done.5.ext_b = f32[4,32,256]{2,1,0:T(8,128)S(1)} collective-permute-done((f32[4,32,256]{2,1,0:T(8,128)S(1)}, f32[4,32,256]{2,1,0:T(8,128)S(1)}, u32[]{:S(2)}, u32[]{:S(2)}) %collective-permute-start.5) | collective-permute-done | bytes 131104 | tf_op jit(solution)/shard_map/ppermute | solution.py:657
  23.3 0.0 collective-permute-done.3.got_b
  23.3 0.0 collective-permute-done.4.got_a
  23.4 0.0 copy-done.4
  23.4 0.0 copy-done.7
  23.4 1.4 %along_y.1 = (f32[16,32,256]{2,1,0:T(8,128)S(1)}, f32[32,256]{1,0:T(8,128)S(1)}, f32[32,256]{1,0:T(8,128)S(1)}, f32[32,16,256]{2,1,0:T(8,128)S(1)}, f32[8,32,256...) custom-call(s32[3]{0:T(128)S(1)} %pad_add_fusion.where_ref, ...), custom_call_target="tpu_custom_call" | custom-call | tf_op jit(solution)/shard_map/along_y/pallas_call | solution.py:750
  24.8 0.3 collective-permute-start.7
  25.1 3.0 %collective-permute-start.8 = (f32[8,32,256]{2,1,0:T(8,128)S(1)}, f32[8,32,256]{2,1,0:T(8,128)S(1)}, u32[]{:S(2)}, u32[]{:S(2)}) collective-permute-start(f32[8,32,256]{2,1,0:T(8,128)S(1)} %get-tuple-element.62), channel_id=1, source_target_pairs={{0,8},{1,9},{2,10},{3,11},{4,12},{5,13},{6,14},{7,15},{8,0},{9,1},... | collective-permute-start | bytes 786440 | tf_op jit(solution)/shard_map/ppermute | solution.py:657
  28.1 0.0 copy-done.3
  28.1 4.6 %middle.1 = (f32[32,32,256]{2,1,0:T(8,128)}, f32[32,32,256]{2,1,0:T(8,128)}, f32[18,32,256]{2,1,0:T(8,128)S(1)}, f32[32,256]{1,0:T(8,128)S(1)}) custom-call(s32[3]{0:T(128)S(1)} %pad_add_fusion.where_ref, f32[3,32,32,256]{3,2,1,0:T(8,128)S(1)} %get-tuple-element.34.strain, f32[32,32,256]{2,1,0:T(8,128)S(1)} %get-tuple-element.38.free, ...), custom_call_target="tpu_custom_call" | custom-call | tf_op jit(solution)/shard_map/middle/pallas_call | solution.py:764
  32.8 0.3 collective-permute-done.7.got_a
  33.1 1.8 %collective-permute-done.8.got_b = f32[8,32,256]{2,1,0:T(8,128)S(1)} collective-permute-done((f32[8,32,256]{2,1,0:T(8,128)S(1)}, f32[8,32,256]{2,1,0:T(8,128)S(1)}, u32[]{:S(2)}, u32[]{:S(2)}) %collective-permute-start.8) | collective-permute-done | bytes 262176 | tf_op jit(solution)/shard_map/ppermute | solution.py:657
  34.9 2.6 %outer.1 = (f32[32,32,256]{2,1,0:T(8,128)}, f32[32,32,256]{2,1,0:T(8,128)}) custom-call(s32[3]{0:T(128)S(1)} %pad_add_fusion.where_ref, f32[3,32,32,256]{3,2,1,0:T(8,128)S(1)} %get-tuple-element.34.strain, f32[32,32,256]{2,1,0:T(8,128)S(1)} %get-tuple-element.38.free, f32[32,32,256]{2,1,0:T(8,128)S(1)} %copy-done, ...), custom_call_target="tpu_custom_call", output_to_operand_aliasing={{0}: (16, {}), {1}: (17, {})} | custom-call | tf_op jit(solution)/shard_map/outer/pallas_call | solution.py:772
Async XLA Ops:
  0.7 7.7 %copy-start = (f32[32,32,256]{2,1,0:T(8,128)S(1)}, f32[32,32,256]{2,1,0:T(8,128)}, u32[]{:S(2)}) copy-start(f32[32,32,256]{2,1,0:T(8,128)} %kappa.5) | copy-start | bytes 3145732
  0.7 7.7 %copy-start.2 = (f32[256,256]{1,0:T(8,128)S(1)}, f32[256,256]{1,0:T(8,128)}, u32[]{:S(2)}) copy-start(f32[256,256]{1,0:T(8,128)} %constant.26.clone.bz) | copy-start | bytes 786436
  4.8 8.6 %collective-permute-start.2 = (f32[4,32,256]{2,1,0:T(8,128)S(1)}, f32[4,32,256]{2,1,0:T(8,128)S(1)}, u32[]{:S(2)}, u32[]{:S(2)}) collective-permute-start(f32[4,32,256]{2,1,0:T(8,128)S(1)} %get-tuple-element.43), channel_id=1, source_target_pairs={{0,8},{8,16},{16,24},{24,0},{1,9},{9,17},{17,25},{25,1},{2,10},{10... | collective-permute-start | bytes 393224 | tf_op jit(solution)/shard_map/ppermute | solution.py:662
  4.9 8.5 %collective-permute-start = (f32[128,128]{1,0:T(8,128)S(1)}, f32[128,128]{1,0:T(8,128)S(1)}, u32[]{:S(2)}, u32[]{:S(2)}) collective-permute-start(f32[128,128]{1,0:T(8,128)S(1)} %get-tuple-element.41.sent_b), channel_id=1, source_target_pairs={{0,8},{1,2},{2,1},{3,4},{4,3},{5,6},{6,5},{7,15},{8,0},{9,10},{10,... | collective-permute-start | bytes 196616 | tf_op jit(solution)/shard_map/ppermute | solution.py:657
  8.4 4.9 %collective-permute-start.1 = (f32[128,128]{1,0:T(8,128)S(1)}, f32[128,128]{1,0:T(8,128)S(1)}, u32[]{:S(2)}, u32[]{:S(2)}) collective-permute-start(f32[128,128]{1,0:T(8,128)S(1)} %get-tuple-element.42.sent_a), channel_id=1, source_target_pairs={{0,1},{1,0},{2,3},{3,2},{4,5},{5,4},{6,7},{7,6},{8,9},{9,8},{10,11... | collective-permute-start | bytes 196616 | tf_op jit(solution)/shard_map/ppermute | solution.py:657
  8.4 4.9 %copy-start.1 = (f32[256,256]{1,0:T(8,128)S(1)}, f32[256,256]{1,0:T(8,128)}, u32[]{:S(2)}) copy-start(f32[256,256]{1,0:T(8,128)} %constant.27.clone.t) | copy-start | bytes 786436
  8.4 4.9 %copy-start.5 = (f32[40,256]{1,0:T(8,128)S(1)}, f32[40,256]{1,0:T(8,128)}, u32[]{:S(2)}) copy-start(f32[40,256]{1,0:T(8,128)} %constant.28.clone.w) | copy-start | bytes 122884
  8.4 11.3 %copy-start.6 = (f32[40,32]{1,0:T(8,128)S(1)}, f32[40,32]{1,0:T(8,128)}, u32[]{:S(2)}) copy-start(f32[40,32]{1,0:T(8,128)} %constant.29.clone.my) | copy-start | bytes 15364
  11.2 12.2 %copy-start.4 = (f32[128,128]{1,0:T(8,128)S(1)}, f32[128,128]{1,0:T(8,128)}, u32[]{:S(2)}) copy-start(f32[128,128]{1,0:T(8,128)} %constant.31.clone.v) | copy-start | bytes 196612
  11.2 12.2 %copy-start.7 = (f32[24,16]{1,0:T(8,128)S(1)}, f32[24,16]{1,0:T(8,128)}, u32[]{:S(2)}) copy-start(f32[24,16]{1,0:T(8,128)} %constant.30.clone.my) | copy-start | bytes 4612
  11.2 16.9 %copy-start.3 = (f32[40,128]{1,0:T(8,128)S(1)}, f32[40,128]{1,0:T(8,128)}, u32[]{:S(2)}) copy-start(f32[40,128]{1,0:T(8,128)} %constant.32.clone.my) | copy-start | bytes 61444
  14.8 8.5 %collective-permute-start.3 = (f32[8,32,256]{2,1,0:T(8,128)S(1)}, f32[8,32,256]{2,1,0:T(8,128)S(1)}, u32[]{:S(2)}, u32[]{:S(2)}) collective-permute-start(f32[8,32,256]{2,1,0:T(8,128)S(1)} %get-tuple-element.48), channel_id=1, source_target_pairs={{0,32},{1,33},{2,34},{3,35},{4,36},{5,37},{6,38},{7,39},{8,16},{9,... | collective-permute-start | bytes 786440 | tf_op jit(solution)/shard_map/ppermute | solution.py:657
  15.3 8.0 %collective-permute-start.4 = (f32[8,32,256]{2,1,0:T(8,128)S(1)}, f32[8,32,256]{2,1,0:T(8,128)S(1)}, u32[]{:S(2)}, u32[]{:S(2)}) collective-permute-start(f32[8,32,256]{2,1,0:T(8,128)S(1)} %get-tuple-element.49), channel_id=1, source_target_pairs={{0,8},{1,9},{2,10},{3,11},{4,12},{5,13},{6,14},{7,15},{8,0},{9,1},... | collective-permute-start | bytes 786440 | tf_op jit(solution)/shard_map/ppermute | solution.py:657
  15.3 7.3 %collective-permute-start.6 = (f32[4,32,256]{2,1,0:T(8,128)S(1)}, f32[4,32,256]{2,1,0:T(8,128)S(1)}, u32[]{:S(2)}, u32[]{:S(2)}) collective-permute-start(f32[4,32,256]{2,1,0:T(8,128)S(1)} %get-tuple-element.50), channel_id=1, source_target_pairs={{0,32},{1,33},{2,34},{3,35},{4,36},{5,37},{6,38},{7,39},{8,40},{9,... | collective-permute-start | bytes 393224 | tf_op jit(solution)/shard_map/ppermute | solution.py:657
  16.6 6.8 %collective-permute-start.5 = (f32[4,32,256]{2,1,0:T(8,128)S(1)}, f32[4,32,256]{2,1,0:T(8,128)S(1)}, u32[]{:S(2)}, u32[]{:S(2)}) collective-permute-start(f32[4,32,256]{2,1,0:T(8,128)S(1)} %get-tuple-element.50), channel_id=1, source_target_pairs={{0,8},{1,9},{2,10},{3,11},{4,12},{5,13},{6,14},{7,15},{8,0},{9,1},... | collective-permute-start | bytes 393224 | tf_op jit(solution)/shard_map/ppermute | solution.py:657
  24.8 8.3 %collective-permute-start.7 = (f32[8,32,256]{2,1,0:T(8,128)S(1)}, f32[8,32,256]{2,1,0:T(8,128)S(1)}, u32[]{:S(2)}, u32[]{:S(2)}) collective-permute-start(f32[8,32,256]{2,1,0:T(8,128)S(1)} %get-tuple-element.61), channel_id=1, source_target_pairs={{0,32},{1,33},{2,34},{3,35},{4,36},{5,37},{6,38},{7,39},{8,40},{9,... | collective-permute-start | bytes 786440 | tf_op jit(solution)/shard_map/ppermute | solution.py:657
  25.1 9.9 %collective-permute-start.8 = (f32[8,32,256]{2,1,0:T(8,128)S(1)}, f32[8,32,256]{2,1,0:T(8,128)S(1)}, u32[]{:S(2)}, u32[]{:S(2)}) collective-permute-start(f32[8,32,256]{2,1,0:T(8,128)S(1)} %get-tuple-element.62), channel_id=1, source_target_pairs={{0,8},{1,9},{2,10},{3,11},{4,12},{5,13},{6,14},{7,15},{8,0},{9,1},... | collective-permute-start | bytes 786440 | tf_op jit(solution)/shard_map/ppermute | solution.py:657

commit v8 on v7

--- a/solution.py
+++ b/solution.py
@@ -344,37 +344,55 @@
     inv_plane[...] = invx * (invy * at_z)
 
 
+def read_y_halo(counts, at, got_a, got_b, halo, parts, more):
+    for j in (7, 14, 15):
+        halo[:, j, :] = jnp.zeros((16, 256), F32)
+
+    def choose(upper, lower):
+        to = 0
+        for first, last in parts:
+            here = slice(to, to + last - first)
+            for j in range(7):
+                halo[here, j, :] = lower[j, first:last, :]
+            for j in range(6):
+                halo[here, 8 + j, :] = upper[j, first:last, :]
+            to += last - first
+        more(upper, lower)
+
+    by_parity(lax.rem(at, 2) == 0, got_a, got_b, choose)
+
+    @pl.when(at == 0)
+    def _():
+        halo[:, 0:8, :] = jnp.zeros((16, 8, 256), F32)
+
+    @pl.when(at == counts[1] - 1)
+    def _():
+        halo[:, 8:16, :] = jnp.zeros((16, 8, 256), F32)
+
+
 def y_kernel(
-    counts, where_ref, own, own_face, plane, got_b, got_a, face_ext, ext_b, ext_a, my, v,
-    edges, out_face, out_plane, halo, x_a, x_b, got_ext, plane_low, plane_high,
+    counts, where_ref, own, own_face, plane, got_b, got_a, face_ext, _, __, my, v,
+    edges, out_face, out_plane, x_a, x_b, halo, plane_low, plane_high,
 ):
-    def choose(upper, lower):
-        for j in range(7):
-            halo[:, j, :] = lower[j]
-        for j in range(6):
-            halo[:, 8 + j, :] = upper[j]
+    def planes(upper, lower):
         plane_low[...] = lower[7]
         plane_high[...] = upper[7]
 
-    halo[:, 7, :] = jnp.zeros((32, 256), F32)
-    halo[:, 14, :] = jnp.zeros((32, 256), F32)
-    halo[:, 15, :] = jnp.zeros((32, 256), F32)
-    by_parity(lax.rem(where_ref[1], 2) == 0, got_a, got_b, choose)
-
-    @pl.when(where_ref[1] == 0)
-    def _():
-        halo[:, 0:8, :] = jnp.zeros((32, 8, 256), F32)
+    at = where_ref[1]
+    read_y_halo(counts, at, got_a, got_b, halo, ((0, 8), (24, 32)), planes)
+
+    @pl.when(at == 0)
+    def _():
         plane_low[...] = jnp.zeros_like(plane_low)
 
-    @pl.when(where_ref[1] == counts[1] - 1)
-    def _():
-        halo[:, 8:16, :] = jnp.zeros((32, 8, 256), F32)
+    @pl.when(at == counts[1] - 1)
+    def _():
         plane_high[...] = jnp.zeros_like(plane_high)
 
     out_face[8:24, :] = own_face[8:24, :]
     for i in range(16):
         x = i if i < 8 else i + 16
-        both = dot(my[...], halo[x])
+        both = dot(my[...], halo[i])
         edges[i, 0:8, :] = own[x, 0:8, :] + both[0:8]
         edges[i, 8:24, :] = own[x, 8:24, :]
         edges[i, 24:32, :] = own[x, 24:32, :] + both[8:16]
@@ -397,26 +415,21 @@
 
     def store(upper, lower):
         for j in range(7):
-            upper[j] = edges[9 + j]
-        upper[7] = jnp.zeros((32, 256), F32)
-        upper[7, 0:8, :] = out_face[24:32, :]
+            upper[32 * j : 32 * j + 32, :] = edges[9 + j]
+        upper[224:232, :] = out_face[24:32, :]
+        upper[232:240, :] = jnp.zeros((8, 256), F32)
         for e in range(4):
             corner = face_ext[e, 31:32, :]
-            upper[7, 8 + e : 9 + e, :] = jnp.where(where_ref[1] == 0, 0.0, corner)
-        upper[7, 16:24, :] = out_plane[24:32, :]
+            upper[232 + e : 233 + e, :] = jnp.where(where_ref[1] == 0, 0.0, corner)
+        upper[240:248, :] = out_plane[24:32, :]
         for j in range(6):
-            lower[j] = edges[j]
-        lower[6] = jnp.zeros((32, 256), F32)
-        lower[7] = jnp.zeros((32, 256), F32)
-        lower[7, 0:8, :] = out_face[0:8, :]
-        lower[7, 16:24, :] = out_plane[0:8, :]
+            lower[32 * j : 32 * j + 32, :] = edges[j]
+        lower[192:224, :] = jnp.zeros((32, 256), F32)
+        lower[224:232, :] = out_face[0:8, :]
+        lower[232:240, :] = jnp.zeros((8, 256), F32)
+        lower[240:248, :] = out_plane[0:8, :]
 
     by_parity(lax.rem(where_ref[0], 2) == 0, x_a, x_b, store)
-
-    def keep(_, lower):
-        got_ext[...] = lower[...]
-
-    by_parity(lax.rem(where_ref[0], 2) == 0, ext_a, ext_b, keep)
 
 
 def fill_side(at, side, face_ext):
@@ -489,20 +502,26 @@
 
 
 def middle_kernel(
-    where_ref, strain, free, kappa, own, edges, halo, face, plane, face_ext,
+    counts, where_ref, strain, free, kappa, own, edges, y_a, y_b, ext_a, ext_b, face, plane, face_ext,
     inv_x, inv_yz, inv_face, inv_plane, my,
-    force, kappa_new, part, face_out,
-    ext, face_all, plane_all, side, before, face_e, face_a, column,
+    force, kappa_new, part, face_out, got_ext,
+    halo, ext, face_all, plane_all, side, before, face_e, face_a, column,
     force_v, kappa_v, sems,
 ):
     at = (where_ref[0], where_ref[1], where_ref[2])
+    read_y_halo(counts, at[1], y_a, y_b, halo, ((8, 24),), lambda upper, lower: None)
+
+    def keep(_, lower):
+        got_ext[...] = lower[...]
+
+    by_parity(lax.rem(at[0], 2) == 0, ext_a, ext_b, keep)
     for x in range(32):
         if x < 8:
             ext[x] = edges[x]
         elif x >= 24:
             ext[x] = edges[x - 16]
         else:
-            both = dot(my[0:24, 0:16], halo[x])
+            both = dot(my[0:24, 0:16], halo[x - 8])
             ext[x, 0:8, :] = own[x, 0:8, :] + both[0:8]
             ext[x, 8:24, :] = own[x, 8:24, :]
             ext[x, 24:32, :] = own[x, 24:32, :] + both[8:16]
@@ -566,15 +585,15 @@
 
     def choose(upper, lower):
         for j in range(7):
-            low[j] = lower[j]
+            low[j] = lower[32 * j : 32 * j + 32, :]
         for j in range(6):
-            high[j] = upper[j]
-        face_all[0:8, :] = lower[7, 0:8, :]
-        face_all[40:48, :] = upper[7, 0:8, :]
-        plane_all[0:8, :] = lower[7, 16:24, :]
-        plane_all[40:48, :] = upper[7, 16:24, :]
+            high[j] = upper[32 * j : 32 * j + 32, :]
+        face_all[0:8, :] = lower[224:232, :]
+        face_all[40:48, :] = upper[224:232, :]
+        plane_all[0:8, :] = lower[240:248, :]
+        plane_all[40:48, :] = upper[240:248, :]
         for e in range(4):
-            side[e, 32:33, :] = lower[7, 8 + e : 9 + e, :]
+            side[e, 32:33, :] = lower[232 + e : 233 + e, :]
 
     fill_side(at, side, face_ext)
     by_parity(lax.rem(at[0], 2) == 0, got_a, got_b, choose)
@@ -737,7 +756,7 @@
         [FACE, eight, eight, shape_of(128, 256), ends],
         scratch=[vmem(128, 256)] + [vmem(32, 128)] * 2 + [vmem(512, 256), vmem(2, 32, 8, 256)],
     )(where, own, xext, z_b, z_a, got_b, got_a, face_ext, t, w)
-    got_a, got_b = swap(y_a, y_b, "gy")
+    y_got_a, y_got_b = swap(y_a, y_b, "gy")
     ext_a, ext_b = swap(xext, xext, "gx")
     own, own_face, *inverse = call(
         functools.partial(own_rows_kernel, extents),
@@ -747,13 +766,13 @@
         scratch=[vmem(1024, 256), vmem(32, 32, 256)],
     )(where, own, z_both, t, rows_own)
 
-    edges, face, plane, halo, x_a, x_b, got_ext = call(
+    edges, face, plane, x_a, x_b = call(
         functools.partial(y_kernel, counts),
         "along_y",
         [SM] + [VM] * 10,
-        [shape_of(16, 32, 256), FACE, FACE, shape_of(32, 16, 256), eight, eight, ends],
-        scratch=[vmem(32, 256), vmem(32, 256)],
-    )(where, own, own_face, plane, got_b, got_a, face_ext, ext_b, ext_a, rows_halo, plane_y_matrix())
+        [shape_of(16, 32, 256), FACE, FACE] + [shape_of(248, 256)] * 2,
+        scratch=[vmem(16, 16, 256), vmem(32, 256), vmem(32, 256)],
+    )(where, own, own_face, plane, y_got_b, y_got_a, face_ext, ext_b, ext_a, rows_halo, plane_y_matrix())
     got_a, got_b = swap(x_a, x_b, "gx")
 
     shared = [
@@ -761,14 +780,15 @@
         vmem(32, 256), vmem(32, 256), vmem(32, 128),
         vmem(16, 32, 256), vmem(16, 32, 256), pltpu.SemaphoreType.DMA((2, 2)),
     ]
-    force, kappa_new, part, face = call(
-        middle_kernel,
+    force, kappa_new, part, face, got_ext = call(
+        functools.partial(middle_kernel, counts),
         "middle",
-        [SM] + [VM] * 14,
-        [BLOCK, BLOCK, shape_of(18, 32, 256), FACE],
-        out_specs=[HBM, HBM, VM, VM],
-        scratch=[vmem(32, 32, 256)] + shared,
-    )(where, strain, free, kappa, own, edges, halo, face, plane, face_ext, *inverse, rows_three)
+        [SM] + [VM] * 17,
+        [BLOCK, BLOCK, shape_of(18, 32, 256), FACE, ends],
+        out_specs=[HBM, HBM, VM, VM, VM],
+        scratch=[vmem(16, 16, 256), vmem(32, 32, 256)] + shared,
+    )(where, strain, free, kappa, own, edges, y_got_a, y_got_b, ext_a, ext_b, face, plane, face_ext,
+      *inverse, rows_three)
     force, kappa_new = call(
         functools.partial(outer_kernel, counts),
         "outer",

time: 37.8 us -> 37.3 us (0.987)
  waiting for transfers between devices: 5.06 us -> 4.56 us
  transfers between devices with their start and end apart: 9 -> 9, of which waited for: 4 -> 3; matrix products, arithmetic and copies ran while one was open for 0% -> 0% of each run, Pallas kernels for 27% -> 28%
where the time goes in v8:
time: 37.3 us; the launch traced here: 37.2 us
  Pallas kernels  19.8 us (53%)
  starting transfers between devices  11.8 us (32%)
  waiting for transfers between devices  4.56 us (12%)
  between operations  0.96 us (3%)
    ppermute x4, starting transfers between devices, swap(): lax.ppermute(second, AXES, route(1))  10.3 us
    pallas_call x1, Pallas kernels, body(): call(functools.partial(middle_kernel, counts), 'middle', [SM] + [VM] * 17...  4.76 us
    ppermute x4, waiting for transfers between devices, swap(): lax.ppermute(second, AXES, route(1))  4.54 us
    pallas_call x1, Pallas kernels, body(): call(pack_kernel, 'pack', [SM] + [HBM] * 5, [shape_of(3, 32, 32, 256), BL...  4.06 us
    pallas_call x1, Pallas kernels, body(): call(functools.partial(own_rows_kernel, extents), 'own_rows', [SM] + [VM]...  2.9 us
    pallas_call x1, Pallas kernels, body(): call(inner_kernel, 'inner', [VM] * 6, [BLOCK, BLOCK, ends], scratch=[vmem...  2.72 us
    pallas_call x1, Pallas kernels, body(): call(functools.partial(outer_kernel, counts), 'outer', [SM] + [VM] * 15 +...  2.64 us
    pallas_call x1, Pallas kernels, body(): call(functools.partial(z_kernel, counts), 'along_z', [SM] + [VM] * 9, [FA...  1.47 us
  transfers between devices with their start and end apart: 9, of which 3 were waited for; matrix products, arithmetic and copies ran while one was open for 0% of the time, Pallas kernels for 28%

profile of v8, /device:TPU:120, one launch (start us, length us, event | category | flops | bytes accessed | tf_op | source)
XLA Modules:
  0.0 37.2 jit_solution(1245680635253951051)
XLA Ops:
  0.6 0.1 pad_add_fusion.where_ref
  0.7 0.0 copy-start
  0.7 0.0 copy-start.2
  0.7 4.1 %pack.1 = (f32[3,32,32,256]{3,2,1,0:T(8,128)S(1)}, f32[32,32,256]{2,1,0:T(8,128)S(1)}, f32[32,32,256]{2,1,0:T(8,128)S(1)}, f32[32,32]{1,0:T(8,128)S(1)}, f32[128...) custom-call(s32[3]{0:T(128)S(1)} %pad_add_fusion.where_ref, f32[3,32,32,256]{3,2,1,0:T(8,128)} %strain_in.1, ...), custom_call_target="tpu_custom_call" | custom-call | tf_op jit(solution)/shard_map/pack/pallas_call | solution.py:734
  4.8 0.1 collective-permute-start.2
  4.9 3.5 %collective-permute-start = (f32[128,128]{1,0:T(8,128)S(1)}, f32[128,128]{1,0:T(8,128)S(1)}, u32[]{:S(2)}, u32[]{:S(2)}) collective-permute-start(f32[128,128]{1,0:T(8,128)S(1)} %get-tuple-element.40.sent_b), channel_id=1, source_target_pairs={{0,8},{1,2},{2,1},{3,4},{4,3},{5,6},{6,5},{7,15},{8,0},{9,10},{10,... | collective-permute-start | bytes 196616 | tf_op jit(solution)/shard_map/ppermute | solution.py:676
  8.4 0.0 collective-permute-start.1
  8.4 0.0 copy-done
  8.4 0.0 copy-done.2
  8.4 0.0 copy-start.1
  8.4 0.0 copy-start.5
  8.4 0.0 copy-start.6
  8.4 2.7 %inner.1 = (f32[32,32,256]{2,1,0:T(8,128)S(1)}, f32[32,32,256]{2,1,0:T(8,128)S(1)}, f32[4,32,256]{2,1,0:T(8,128)S(1)}) custom-call(f32[3,32,32,256]{3,2,1,0:T(8,128)S(1)} %get-tuple-element.33.strain, f32[32,32,256]{2,1,0:T(8,128)S(1)} %get-tuple-element.34.plastic, f32[32,32,256]{2,1,0:T(8,128)S(1)} %get-tuple-element.35.alpha, f32[32,32,256]{2,1,0:T(8,128)S(1)} %copy-done, ...), custom_call_target="tpu_custom_call" | custom-call | tf_op jit(solution)/shard_map/inner/pallas_call | solution.py:747
  11.2 0.0 copy-start.4
  11.2 0.0 copy-start.7
  11.2 0.0 copy-start.3
  11.2 2.1 %collective-permute-done.got_b = f32[128,128]{1,0:T(8,128)S(1)} collective-permute-done((f32[128,128]{1,0:T(8,128)S(1)}, f32[128,128]{1,0:T(8,128)S(1)}, u32[]{:S(2)}, u32[]{:S(2)}) %collective-permute-start) | collective-permute-done | bytes 65568 | tf_op jit(solution)/shard_map/ppermute | solution.py:676
  13.3 0.0 collective-permute-done.1.got_a
  13.3 0.0 collective-permute-done.2._.face_ext
  13.3 0.0 copy-done.1
  13.3 0.0 copy-done.5
  13.4 1.5 %along_z.1 = (f32[32,256]{1,0:T(8,128)S(1)}, f32[8,32,256]{2,1,0:T(8,128)S(1)}, f32[8,32,256]{2,1,0:T(8,128)S(1)}, f32[128,256]{1,0:T(8,128)S(1)}, f32[4,32,256]{2,1,0:T(8,128)S(1)}) custom-call(s32[3]{0:T(128)S(1)} %pad_add_fusion.where_ref, f32[32,32,256]{2,1,0:T(8,128)S(1)} %get-tuple-element.38.own, f32[4,32,256]{2,1,0:T(8,128)S(1)} %get-tuple-element.39.xext_in, ...), custom_call_target="tpu_custom_call" | custom-call | tf_op jit(solution)/shard_map/along_z/pallas_call | solution.py:752
  14.8 0.5 %collective-permute-start.3 = (f32[8,32,256]{2,1,0:T(8,128)S(1)}, f32[8,32,256]{2,1,0:T(8,128)S(1)}, u32[]{:S(2)}, u32[]{:S(2)}) collective-permute-start(f32[8,32,256]{2,1,0:T(8,128)S(1)} %get-tuple-element.47), channel_id=1, source_target_pairs={{0,32},{1,33},{2,34},{3,35},{4,36},{5,37},{6,38},{7,39},{8,16},{9,... | collective-permute-start | bytes 786440 | tf_op jit(solution)/shard_map/ppermute | solution.py:676
  15.3 0.0 collective-permute-start.4
  15.3 1.3 %collective-permute-start.6 = (f32[4,32,256]{2,1,0:T(8,128)S(1)}, f32[4,32,256]{2,1,0:T(8,128)S(1)}, u32[]{:S(2)}, u32[]{:S(2)}) collective-permute-start(f32[4,32,256]{2,1,0:T(8,128)S(1)} %get-tuple-element.49), channel_id=1, source_target_pairs={{0,32},{1,33},{2,34},{3,35},{4,36},{5,37},{6,38},{7,39},{8,40},{9,... | collective-permute-start | bytes 393224 | tf_op jit(solution)/shard_map/ppermute | solution.py:676
  16.6 3.1 %collective-permute-start.5 = (f32[4,32,256]{2,1,0:T(8,128)S(1)}, f32[4,32,256]{2,1,0:T(8,128)S(1)}, u32[]{:S(2)}, u32[]{:S(2)}) collective-permute-start(f32[4,32,256]{2,1,0:T(8,128)S(1)} %get-tuple-element.49), channel_id=1, source_target_pairs={{0,8},{1,9},{2,10},{3,11},{4,12},{5,13},{6,14},{7,15},{8,0},{9,1},... | collective-permute-start | bytes 393224 | tf_op jit(solution)/shard_map/ppermute | solution.py:676
  19.7 0.0 copy-done.6
  19.7 2.9 %own_rows.1 = (f32[32,32,256]{2,1,0:T(8,128)S(1)}, f32[32,256]{1,0:T(8,128)S(1)}, f32[40,256]{1,0:T(8,128)S(1)}, f32[32,256]{1,0:T(8,128)S(1)}, f32[40,256]{1,0:T(8,128)S(1)}, /*index=5*/f32[40,256]{1,0:T(8,128)S(1)}) custom-call(s32[3]{0:T(128)S(1)} %pad_add_fusion.where_ref, f32[32,32,256]{2,1,0:T(8,128)S(1)} %get-tuple-element.38.own, ...), custom_call_target="tpu_custom_call" | custom-call | tf_op jit(solution)/shard_map/own_rows/pallas_call | solution.py:761
  22.6 0.0 collective-permute-done.6.__.ext_a
  22.6 0.7 %collective-permute-done.5._.ext_b = f32[4,32,256]{2,1,0:T(8,128)S(1)} collective-permute-done((f32[4,32,256]{2,1,0:T(8,128)S(1)}, f32[4,32,256]{2,1,0:T(8,128)S(1)}, u32[]{:S(2)}, u32[]{:S(2)}) %collective-permute-start.5) | collective-permute-done | bytes 131104 | tf_op jit(solution)/shard_map/ppermute | solution.py:676
  23.4 0.0 collective-permute-done.3.got_b.y_b
  23.4 0.0 collective-permute-done.4.got_a.y_a
  23.4 0.0 copy-done.4
  23.4 0.0 copy-done.7
  23.4 1.2 %along_y.1 = (f32[16,32,256]{2,1,0:T(8,128)S(1)}, f32[32,256]{1,0:T(8,128)S(1)}, f32[32,256]{1,0:T(8,128)S(1)}, f32[248,256]{1,0:T(8,128)S(1)}, f32[248,256]{1,0:T(8,128)S(1)}) custom-call(s32[3]{0:T(128)S(1)} %pad_add_fusion.where_ref, f32[32,32,256]{2,1,0:T(8,128)S(1)} %get-tuple-element.44.own, f32[32,256]{1,0:T(8,128)S(1)} %get-tuple-element.45.own_face, ...), custom_call_target="tpu_custom_call" | custom-call | tf_op jit(solution)/shard_map/along_y/pallas_call | solution.py:769
  24.6 0.1 collective-permute-start.7
  24.7 3.2 %collective-permute-start.8 = (f32[248,256]{1,0:T(8,128)S(1)}, f32[248,256]{1,0:T(8,128)S(1)}, u32[]{:S(2)}, u32[]{:S(2)}) collective-permute-start(f32[248,256]{1,0:T(8,128)S(1)} %get-tuple-element.60), channel_id=1, source_target_pairs={{0,8},{1,9},{2,10},{3,11},{4,12},{5,13},{6,14},{7,15},{8,0},{9,1},... | collective-permute-start | bytes 761864 | tf_op jit(solution)/shard_map/ppermute | solution.py:676
  27.9 0.0 copy-done.3
  27.9 4.8 %middle.1 = (f32[32,32,256]{2,1,0:T(8,128)}, f32[32,32,256]{2,1,0:T(8,128)}, f32[18,32,256]{2,1,0:T(8,128)S(1)}, f32[32,256]{1,0:T(8,128)S(1)}, f32[4,32,256]{2,1,0:T(8,128)S(1)}) custom-call(s32[3]{0:T(128)S(1)} %pad_add_fusion.where_ref, f32[3,32,32,256]{3,2,1,0:T(8,128)S(1)} %get-tuple-element.33.strain, f32[32,32,256]{2,1,0:T(8,128)S(1)} %get-tuple-element.37.free, ...), custom_call_target="tpu_custom_call" | custom-call | tf_op jit(solution)/shard_map/middle/pallas_call | solution.py:783
  32.7 0.0 collective-permute-done.7.got_a
  32.7 1.7 %collective-permute-done.8.got_b = f32[248,256]{1,0:T(8,128)S(1)} collective-permute-done((f32[248,256]{1,0:T(8,128)S(1)}, f32[248,256]{1,0:T(8,128)S(1)}, u32[]{:S(2)}, u32[]{:S(2)}) %collective-permute-start.8) | collective-permute-done | bytes 253984 | tf_op jit(solution)/shard_map/ppermute | solution.py:676
  34.4 2.6 %outer.1 = (f32[32,32,256]{2,1,0:T(8,128)}, f32[32,32,256]{2,1,0:T(8,128)}) custom-call(s32[3]{0:T(128)S(1)} %pad_add_fusion.where_ref, f32[3,32,32,256]{3,2,1,0:T(8,128)S(1)} %get-tuple-element.33.strain, f32[32,32,256]{2,1,0:T(8,128)S(1)} %get-tuple-element.37.free, f32[32,32,256]{2,1,0:T(8,128)S(1)} %copy-done, ...), custom_call_target="tpu_custom_call", output_to_operand_aliasing={{0}: (16, {}), {1}: (17, {})} | custom-call | tf_op jit(solution)/shard_map/outer/pallas_call | solution.py:792
Async XLA Ops:
  0.7 7.7 %copy-start = (f32[32,32,256]{2,1,0:T(8,128)S(1)}, f32[32,32,256]{2,1,0:T(8,128)}, u32[]{:S(2)}) copy-start(f32[32,32,256]{2,1,0:T(8,128)} %kappa.5) | copy-start | bytes 3145732
  0.7 7.7 %copy-start.2 = (f32[256,256]{1,0:T(8,128)S(1)}, f32[256,256]{1,0:T(8,128)}, u32[]{:S(2)}) copy-start(f32[256,256]{1,0:T(8,128)} %constant.26.clone.bz) | copy-start | bytes 786436
  4.8 8.6 %collective-permute-start.2 = (f32[4,32,256]{2,1,0:T(8,128)S(1)}, f32[4,32,256]{2,1,0:T(8,128)S(1)}, u32[]{:S(2)}, u32[]{:S(2)}) collective-permute-start(f32[4,32,256]{2,1,0:T(8,128)S(1)} %get-tuple-element.42), channel_id=1, source_target_pairs={{0,8},{8,16},{16,24},{24,0},{1,9},{9,17},{17,25},{25,1},{2,10},{10... | collective-permute-start | bytes 393224 | tf_op jit(solution)/shard_map/ppermute | solution.py:681
  4.9 8.5 %collective-permute-start = (f32[128,128]{1,0:T(8,128)S(1)}, f32[128,128]{1,0:T(8,128)S(1)}, u32[]{:S(2)}, u32[]{:S(2)}) collective-permute-start(f32[128,128]{1,0:T(8,128)S(1)} %get-tuple-element.40.sent_b), channel_id=1, source_target_pairs={{0,8},{1,2},{2,1},{3,4},{4,3},{5,6},{6,5},{7,15},{8,0},{9,10},{10,... | collective-permute-start | bytes 196616 | tf_op jit(solution)/shard_map/ppermute | solution.py:676
  8.4 4.9 %collective-permute-start.1 = (f32[128,128]{1,0:T(8,128)S(1)}, f32[128,128]{1,0:T(8,128)S(1)}, u32[]{:S(2)}, u32[]{:S(2)}) collective-permute-start(f32[128,128]{1,0:T(8,128)S(1)} %get-tuple-element.41.sent_a), channel_id=1, source_target_pairs={{0,1},{1,0},{2,3},{3,2},{4,5},{5,4},{6,7},{7,6},{8,9},{9,8},{10,11... | collective-permute-start | bytes 196616 | tf_op jit(solution)/shard_map/ppermute | solution.py:676
  8.4 4.9 %copy-start.1 = (f32[256,256]{1,0:T(8,128)S(1)}, f32[256,256]{1,0:T(8,128)}, u32[]{:S(2)}) copy-start(f32[256,256]{1,0:T(8,128)} %constant.27.clone.t) | copy-start | bytes 786436
  8.4 4.9 %copy-start.5 = (f32[40,256]{1,0:T(8,128)S(1)}, f32[40,256]{1,0:T(8,128)}, u32[]{:S(2)}) copy-start(f32[40,256]{1,0:T(8,128)} %constant.28.clone.w) | copy-start | bytes 122884
  8.4 11.3 %copy-start.6 = (f32[40,32]{1,0:T(8,128)S(1)}, f32[40,32]{1,0:T(8,128)}, u32[]{:S(2)}) copy-start(f32[40,32]{1,0:T(8,128)} %constant.29.clone.my) | copy-start | bytes 15364
  11.2 12.2 %copy-start.4 = (f32[128,128]{1,0:T(8,128)S(1)}, f32[128,128]{1,0:T(8,128)}, u32[]{:S(2)}) copy-start(f32[128,128]{1,0:T(8,128)} %constant.31.clone.v) | copy-start | bytes 196612
  11.2 12.2 %copy-start.7 = (f32[24,16]{1,0:T(8,128)S(1)}, f32[24,16]{1,0:T(8,128)}, u32[]{:S(2)}) copy-start(f32[24,16]{1,0:T(8,128)} %constant.30.clone.my) | copy-start | bytes 4612
  11.2 16.7 %copy-start.3 = (f32[40,128]{1,0:T(8,128)S(1)}, f32[40,128]{1,0:T(8,128)}, u32[]{:S(2)}) copy-start(f32[40,128]{1,0:T(8,128)} %constant.32.clone.my) | copy-start | bytes 61444
  14.8 8.5 %collective-permute-start.3 = (f32[8,32,256]{2,1,0:T(8,128)S(1)}, f32[8,32,256]{2,1,0:T(8,128)S(1)}, u32[]{:S(2)}, u32[]{:S(2)}) collective-permute-start(f32[8,32,256]{2,1,0:T(8,128)S(1)} %get-tuple-element.47), channel_id=1, source_target_pairs={{0,32},{1,33},{2,34},{3,35},{4,36},{5,37},{6,38},{7,39},{8,16},{9,... | collective-permute-start | bytes 786440 | tf_op jit(solution)/shard_map/ppermute | solution.py:676
  15.3 8.0 %collective-permute-start.4 = (f32[8,32,256]{2,1,0:T(8,128)S(1)}, f32[8,32,256]{2,1,0:T(8,128)S(1)}, u32[]{:S(2)}, u32[]{:S(2)}) collective-permute-start(f32[8,32,256]{2,1,0:T(8,128)S(1)} %get-tuple-element.48), channel_id=1, source_target_pairs={{0,8},{1,9},{2,10},{3,11},{4,12},{5,13},{6,14},{7,15},{8,0},{9,1},... | collective-permute-start | bytes 786440 | tf_op jit(solution)/shard_map/ppermute | solution.py:676
  15.3 7.3 %collective-permute-start.6 = (f32[4,32,256]{2,1,0:T(8,128)S(1)}, f32[4,32,256]{2,1,0:T(8,128)S(1)}, u32[]{:S(2)}, u32[]{:S(2)}) collective-permute-start(f32[4,32,256]{2,1,0:T(8,128)S(1)} %get-tuple-element.49), channel_id=1, source_target_pairs={{0,32},{1,33},{2,34},{3,35},{4,36},{5,37},{6,38},{7,39},{8,40},{9,... | collective-permute-start | bytes 393224 | tf_op jit(solution)/shard_map/ppermute | solution.py:676
  16.6 6.8 %collective-permute-start.5 = (f32[4,32,256]{2,1,0:T(8,128)S(1)}, f32[4,32,256]{2,1,0:T(8,128)S(1)}, u32[]{:S(2)}, u32[]{:S(2)}) collective-permute-start(f32[4,32,256]{2,1,0:T(8,128)S(1)} %get-tuple-element.49), channel_id=1, source_target_pairs={{0,8},{1,9},{2,10},{3,11},{4,12},{5,13},{6,14},{7,15},{8,0},{9,1},... | collective-permute-start | bytes 393224 | tf_op jit(solution)/shard_map/ppermute | solution.py:676
  24.6 8.1 %collective-permute-start.7 = (f32[248,256]{1,0:T(8,128)S(1)}, f32[248,256]{1,0:T(8,128)S(1)}, u32[]{:S(2)}, u32[]{:S(2)}) collective-permute-start(f32[248,256]{1,0:T(8,128)S(1)} %get-tuple-element.59), channel_id=1, source_target_pairs={{0,32},{1,33},{2,34},{3,35},{4,36},{5,37},{6,38},{7,39},{8,40},{9,... | collective-permute-start | bytes 761864 | tf_op jit(solution)/shard_map/ppermute | solution.py:676
  24.7 9.7 %collective-permute-start.8 = (f32[248,256]{1,0:T(8,128)S(1)}, f32[248,256]{1,0:T(8,128)S(1)}, u32[]{:S(2)}, u32[]{:S(2)}) collective-permute-start(f32[248,256]{1,0:T(8,128)S(1)} %get-tuple-element.60), channel_id=1, source_target_pairs={{0,8},{1,9},{2,10},{3,11},{4,12},{5,13},{6,14},{7,15},{8,0},{9,1},... | collective-permute-start | bytes 761864 | tf_op jit(solution)/shard_map/ppermute | solution.py:676

commit v9 on v8

--- a/solution.py
+++ b/solution.py
@@ -106,7 +106,7 @@
 
 
 def integrity_of(kappa):
-    return jnp.exp(-jnp.maximum(kappa - 3.2, 0.0) / 3.0)
+    return jnp.exp(jnp.maximum(kappa - 3.2, 0.0) * (-1.0 / 3.0))
 
 
 def by_parity(even, first, second, use):

time: 37.3 us -> 37.3 us (level)
  no operation moved by 1% of the time
where the time goes in v9:
time: 37.3 us; the launch traced here: 37.2 us
  Pallas kernels  19.8 us (53%)
  starting transfers between devices  11.8 us (32%)
  waiting for transfers between devices  4.58 us (12%)
  between operations  0.96 us (3%)
    ppermute x4, starting transfers between devices, swap(): lax.ppermute(second, AXES, route(1))  10.3 us
    pallas_call x1, Pallas kernels, body(): call(functools.partial(middle_kernel, counts), 'middle', [SM] + [VM] * 17...  4.75 us
    ppermute x4, waiting for transfers between devices, swap(): lax.ppermute(second, AXES, route(1))  4.56 us
    pallas_call x1, Pallas kernels, body(): call(pack_kernel, 'pack', [SM] + [HBM] * 5, [shape_of(3, 32, 32, 256), BL...  4.06 us
    pallas_call x1, Pallas kernels, body(): call(functools.partial(own_rows_kernel, extents), 'own_rows', [SM] + [VM]...  2.9 us
    pallas_call x1, Pallas kernels, body(): call(inner_kernel, 'inner', [VM] * 6, [BLOCK, BLOCK, ends], scratch=[vmem...  2.72 us
    pallas_call x1, Pallas kernels, body(): call(functools.partial(outer_kernel, counts), 'outer', [SM] + [VM] * 15 +...  2.62 us
    pallas_call x1, Pallas kernels, body(): call(functools.partial(z_kernel, counts), 'along_z', [SM] + [VM] * 9, [FA...  1.47 us
  transfers between devices with their start and end apart: 9, of which 3 were waited for; matrix products, arithmetic and copies ran while one was open for 0% of the time, Pallas kernels for 28%

profile of v9, /device:TPU:120, one launch (start us, length us, event | category | flops | bytes accessed | tf_op | source)
XLA Modules:
  0.0 37.2 jit_solution(6131758874230076338)
XLA Ops:
  0.6 0.1 pad_add_fusion.where_ref
  0.7 0.0 copy-start
  0.7 0.0 copy-start.2
  0.7 4.1 %pack.1 = (f32[3,32,32,256]{3,2,1,0:T(8,128)S(1)}, f32[32,32,256]{2,1,0:T(8,128)S(1)}, f32[32,32,256]{2,1,0:T(8,128)S(1)}, f32[32,32]{1,0:T(8,128)S(1)}, f32[128...) custom-call(s32[3]{0:T(128)S(1)} %pad_add_fusion.where_ref, f32[3,32,32,256]{3,2,1,0:T(8,128)} %strain_in.1, ...), custom_call_target="tpu_custom_call" | custom-call | tf_op jit(solution)/shard_map/pack/pallas_call | solution.py:734
  4.8 0.1 collective-permute-start.2
  4.9 3.5 %collective-permute-start = (f32[128,128]{1,0:T(8,128)S(1)}, f32[128,128]{1,0:T(8,128)S(1)}, u32[]{:S(2)}, u32[]{:S(2)}) collective-permute-start(f32[128,128]{1,0:T(8,128)S(1)} %get-tuple-element.40.sent_b), channel_id=1, source_target_pairs={{0,8},{1,2},{2,1},{3,4},{4,3},{5,6},{6,5},{7,15},{8,0},{9,10},{10,... | collective-permute-start | bytes 196616 | tf_op jit(solution)/shard_map/ppermute | solution.py:676
  8.4 0.0 collective-permute-start.1
  8.4 0.0 copy-done
  8.4 0.0 copy-done.2
  8.4 0.0 copy-start.1
  8.4 0.0 copy-start.5
  8.4 0.0 copy-start.6
  8.4 2.7 %inner.1 = (f32[32,32,256]{2,1,0:T(8,128)S(1)}, f32[32,32,256]{2,1,0:T(8,128)S(1)}, f32[4,32,256]{2,1,0:T(8,128)S(1)}) custom-call(f32[3,32,32,256]{3,2,1,0:T(8,128)S(1)} %get-tuple-element.33.strain, f32[32,32,256]{2,1,0:T(8,128)S(1)} %get-tuple-element.34.plastic, f32[32,32,256]{2,1,0:T(8,128)S(1)} %get-tuple-element.35.alpha, f32[32,32,256]{2,1,0:T(8,128)S(1)} %copy-done, ...), custom_call_target="tpu_custom_call" | custom-call | tf_op jit(solution)/shard_map/inner/pallas_call | solution.py:747
  11.2 0.0 copy-start.4
  11.2 0.0 copy-start.7
  11.2 0.0 copy-start.3
  11.2 2.1 %collective-permute-done.got_b = f32[128,128]{1,0:T(8,128)S(1)} collective-permute-done((f32[128,128]{1,0:T(8,128)S(1)}, f32[128,128]{1,0:T(8,128)S(1)}, u32[]{:S(2)}, u32[]{:S(2)}) %collective-permute-start) | collective-permute-done | bytes 65568 | tf_op jit(solution)/shard_map/ppermute | solution.py:676
  13.3 0.0 collective-permute-done.1.got_a
  13.3 0.0 collective-permute-done.2._.face_ext
  13.3 0.0 copy-done.1
  13.3 0.0 copy-done.5
  13.4 1.5 %along_z.1 = (f32[32,256]{1,0:T(8,128)S(1)}, f32[8,32,256]{2,1,0:T(8,128)S(1)}, f32[8,32,256]{2,1,0:T(8,128)S(1)}, f32[128,256]{1,0:T(8,128)S(1)}, f32[4,32,256]{2,1,0:T(8,128)S(1)}) custom-call(s32[3]{0:T(128)S(1)} %pad_add_fusion.where_ref, f32[32,32,256]{2,1,0:T(8,128)S(1)} %get-tuple-element.38.own, f32[4,32,256]{2,1,0:T(8,128)S(1)} %get-tuple-element.39.xext_in, ...), custom_call_target="tpu_custom_call" | custom-call | tf_op jit(solution)/shard_map/along_z/pallas_call | solution.py:752
  14.8 0.5 %collective-permute-start.3 = (f32[8,32,256]{2,1,0:T(8,128)S(1)}, f32[8,32,256]{2,1,0:T(8,128)S(1)}, u32[]{:S(2)}, u32[]{:S(2)}) collective-permute-start(f32[8,32,256]{2,1,0:T(8,128)S(1)} %get-tuple-element.47), channel_id=1, source_target_pairs={{0,32},{1,33},{2,34},{3,35},{4,36},{5,37},{6,38},{7,39},{8,16},{9,... | collective-permute-start | bytes 786440 | tf_op jit(solution)/shard_map/ppermute | solution.py:676
  15.3 0.0 collective-permute-start.4
  15.3 1.3 %collective-permute-start.6 = (f32[4,32,256]{2,1,0:T(8,128)S(1)}, f32[4,32,256]{2,1,0:T(8,128)S(1)}, u32[]{:S(2)}, u32[]{:S(2)}) collective-permute-start(f32[4,32,256]{2,1,0:T(8,128)S(1)} %get-tuple-element.49), channel_id=1, source_target_pairs={{0,32},{1,33},{2,34},{3,35},{4,36},{5,37},{6,38},{7,39},{8,40},{9,... | collective-permute-start | bytes 393224 | tf_op jit(solution)/shard_map/ppermute | solution.py:676
  16.6 3.1 %collective-permute-start.5 = (f32[4,32,256]{2,1,0:T(8,128)S(1)}, f32[4,32,256]{2,1,0:T(8,128)S(1)}, u32[]{:S(2)}, u32[]{:S(2)}) collective-permute-start(f32[4,32,256]{2,1,0:T(8,128)S(1)} %get-tuple-element.49), channel_id=1, source_target_pairs={{0,8},{1,9},{2,10},{3,11},{4,12},{5,13},{6,14},{7,15},{8,0},{9,1},... | collective-permute-start | bytes 393224 | tf_op jit(solution)/shard_map/ppermute | solution.py:676
  19.7 0.0 copy-done.6
  19.7 2.9 %own_rows.1 = (f32[32,32,256]{2,1,0:T(8,128)S(1)}, f32[32,256]{1,0:T(8,128)S(1)}, f32[40,256]{1,0:T(8,128)S(1)}, f32[32,256]{1,0:T(8,128)S(1)}, f32[40,256]{1,0:T(8,128)S(1)}, /*index=5*/f32[40,256]{1,0:T(8,128)S(1)}) custom-call(s32[3]{0:T(128)S(1)} %pad_add_fusion.where_ref, f32[32,32,256]{2,1,0:T(8,128)S(1)} %get-tuple-element.38.own, ...), custom_call_target="tpu_custom_call" | custom-call | tf_op jit(solution)/shard_map/own_rows/pallas_call | solution.py:761
  22.6 0.0 collective-permute-done.6.__.ext_a
  22.6 0.7 %collective-permute-done.5._.ext_b = f32[4,32,256]{2,1,0:T(8,128)S(1)} collective-permute-done((f32[4,32,256]{2,1,0:T(8,128)S(1)}, f32[4,32,256]{2,1,0:T(8,128)S(1)}, u32[]{:S(2)}, u32[]{:S(2)}) %collective-permute-start.5) | collective-permute-done | bytes 131104 | tf_op jit(solution)/shard_map/ppermute | solution.py:676
  23.4 0.0 collective-permute-done.3.got_b.y_b
  23.4 0.0 collective-permute-done.4.got_a.y_a
  23.4 0.0 copy-done.4
  23.4 0.0 copy-done.7
  23.4 1.2 %along_y.1 = (f32[16,32,256]{2,1,0:T(8,128)S(1)}, f32[32,256]{1,0:T(8,128)S(1)}, f32[32,256]{1,0:T(8,128)S(1)}, f32[248,256]{1,0:T(8,128)S(1)}, f32[248,256]{1,0:T(8,128)S(1)}) custom-call(s32[3]{0:T(128)S(1)} %pad_add_fusion.where_ref, f32[32,32,256]{2,1,0:T(8,128)S(1)} %get-tuple-element.44.own, f32[32,256]{1,0:T(8,128)S(1)} %get-tuple-element.45.own_face, ...), custom_call_target="tpu_custom_call" | custom-call | tf_op jit(solution)/shard_map/along_y/pallas_call | solution.py:769
  24.6 0.1 collective-permute-start.7
  24.7 3.2 %collective-permute-start.8 = (f32[248,256]{1,0:T(8,128)S(1)}, f32[248,256]{1,0:T(8,128)S(1)}, u32[]{:S(2)}, u32[]{:S(2)}) collective-permute-start(f32[248,256]{1,0:T(8,128)S(1)} %get-tuple-element.60), channel_id=1, source_target_pairs={{0,8},{1,9},{2,10},{3,11},{4,12},{5,13},{6,14},{7,15},{8,0},{9,1},... | collective-permute-start | bytes 761864 | tf_op jit(solution)/shard_map/ppermute | solution.py:676
  27.9 0.0 copy-done.3
  27.9 4.7 %middle.1 = (f32[32,32,256]{2,1,0:T(8,128)}, f32[32,32,256]{2,1,0:T(8,128)}, f32[18,32,256]{2,1,0:T(8,128)S(1)}, f32[32,256]{1,0:T(8,128)S(1)}, f32[4,32,256]{2,1,0:T(8,128)S(1)}) custom-call(s32[3]{0:T(128)S(1)} %pad_add_fusion.where_ref, f32[3,32,32,256]{3,2,1,0:T(8,128)S(1)} %get-tuple-element.33.strain, f32[32,32,256]{2,1,0:T(8,128)S(1)} %get-tuple-element.37.free, ...), custom_call_target="tpu_custom_call" | custom-call | tf_op jit(solution)/shard_map/middle/pallas_call | solution.py:783
  32.7 0.0 collective-permute-done.7.got_a
  32.7 1.7 %collective-permute-done.8.got_b = f32[248,256]{1,0:T(8,128)S(1)} collective-permute-done((f32[248,256]{1,0:T(8,128)S(1)}, f32[248,256]{1,0:T(8,128)S(1)}, u32[]{:S(2)}, u32[]{:S(2)}) %collective-permute-start.8) | collective-permute-done | bytes 253984 | tf_op jit(solution)/shard_map/ppermute | solution.py:676
  34.4 2.6 %outer.1 = (f32[32,32,256]{2,1,0:T(8,128)}, f32[32,32,256]{2,1,0:T(8,128)}) custom-call(s32[3]{0:T(128)S(1)} %pad_add_fusion.where_ref, f32[3,32,32,256]{3,2,1,0:T(8,128)S(1)} %get-tuple-element.33.strain, f32[32,32,256]{2,1,0:T(8,128)S(1)} %get-tuple-element.37.free, f32[32,32,256]{2,1,0:T(8,128)S(1)} %copy-done, ...), custom_call_target="tpu_custom_call", output_to_operand_aliasing={{0}: (16, {}), {1}: (17, {})} | custom-call | tf_op jit(solution)/shard_map/outer/pallas_call | solution.py:792
Async XLA Ops:
  0.7 7.7 %copy-start = (f32[32,32,256]{2,1,0:T(8,128)S(1)}, f32[32,32,256]{2,1,0:T(8,128)}, u32[]{:S(2)}) copy-start(f32[32,32,256]{2,1,0:T(8,128)} %kappa.5) | copy-start | bytes 3145732
  0.7 7.7 %copy-start.2 = (f32[256,256]{1,0:T(8,128)S(1)}, f32[256,256]{1,0:T(8,128)}, u32[]{:S(2)}) copy-start(f32[256,256]{1,0:T(8,128)} %constant.26.clone.bz) | copy-start | bytes 786436
  4.8 8.6 %collective-permute-start.2 = (f32[4,32,256]{2,1,0:T(8,128)S(1)}, f32[4,32,256]{2,1,0:T(8,128)S(1)}, u32[]{:S(2)}, u32[]{:S(2)}) collective-permute-start(f32[4,32,256]{2,1,0:T(8,128)S(1)} %get-tuple-element.42), channel_id=1, source_target_pairs={{0,8},{8,16},{16,24},{24,0},{1,9},{9,17},{17,25},{25,1},{2,10},{10... | collective-permute-start | bytes 393224 | tf_op jit(solution)/shard_map/ppermute | solution.py:681
  4.9 8.5 %collective-permute-start = (f32[128,128]{1,0:T(8,128)S(1)}, f32[128,128]{1,0:T(8,128)S(1)}, u32[]{:S(2)}, u32[]{:S(2)}) collective-permute-start(f32[128,128]{1,0:T(8,128)S(1)} %get-tuple-element.40.sent_b), channel_id=1, source_target_pairs={{0,8},{1,2},{2,1},{3,4},{4,3},{5,6},{6,5},{7,15},{8,0},{9,10},{10,... | collective-permute-start | bytes 196616 | tf_op jit(solution)/shard_map/ppermute | solution.py:676
  8.4 4.9 %collective-permute-start.1 = (f32[128,128]{1,0:T(8,128)S(1)}, f32[128,128]{1,0:T(8,128)S(1)}, u32[]{:S(2)}, u32[]{:S(2)}) collective-permute-start(f32[128,128]{1,0:T(8,128)S(1)} %get-tuple-element.41.sent_a), channel_id=1, source_target_pairs={{0,1},{1,0},{2,3},{3,2},{4,5},{5,4},{6,7},{7,6},{8,9},{9,8},{10,11... | collective-permute-start | bytes 196616 | tf_op jit(solution)/shard_map/ppermute | solution.py:676
  8.4 4.9 %copy-start.1 = (f32[256,256]{1,0:T(8,128)S(1)}, f32[256,256]{1,0:T(8,128)}, u32[]{:S(2)}) copy-start(f32[256,256]{1,0:T(8,128)} %constant.27.clone.t) | copy-start | bytes 786436
  8.4 4.9 %copy-start.5 = (f32[40,256]{1,0:T(8,128)S(1)}, f32[40,256]{1,0:T(8,128)}, u32[]{:S(2)}) copy-start(f32[40,256]{1,0:T(8,128)} %constant.28.clone.w) | copy-start | bytes 122884
  8.4 11.3 %copy-start.6 = (f32[40,32]{1,0:T(8,128)S(1)}, f32[40,32]{1,0:T(8,128)}, u32[]{:S(2)}) copy-start(f32[40,32]{1,0:T(8,128)} %constant.29.clone.my) | copy-start | bytes 15364
  11.2 12.2 %copy-start.4 = (f32[128,128]{1,0:T(8,128)S(1)}, f32[128,128]{1,0:T(8,128)}, u32[]{:S(2)}) copy-start(f32[128,128]{1,0:T(8,128)} %constant.31.clone.v) | copy-start | bytes 196612
  11.2 12.2 %copy-start.7 = (f32[24,16]{1,0:T(8,128)S(1)}, f32[24,16]{1,0:T(8,128)}, u32[]{:S(2)}) copy-start(f32[24,16]{1,0:T(8,128)} %constant.30.clone.my) | copy-start | bytes 4612
  11.2 16.7 %copy-start.3 = (f32[40,128]{1,0:T(8,128)S(1)}, f32[40,128]{1,0:T(8,128)}, u32[]{:S(2)}) copy-start(f32[40,128]{1,0:T(8,128)} %constant.32.clone.my) | copy-start | bytes 61444
  14.8 8.5 %collective-permute-start.3 = (f32[8,32,256]{2,1,0:T(8,128)S(1)}, f32[8,32,256]{2,1,0:T(8,128)S(1)}, u32[]{:S(2)}, u32[]{:S(2)}) collective-permute-start(f32[8,32,256]{2,1,0:T(8,128)S(1)} %get-tuple-element.47), channel_id=1, source_target_pairs={{0,32},{1,33},{2,34},{3,35},{4,36},{5,37},{6,38},{7,39},{8,16},{9,... | collective-permute-start | bytes 786440 | tf_op jit(solution)/shard_map/ppermute | solution.py:676
  15.3 8.0 %collective-permute-start.4 = (f32[8,32,256]{2,1,0:T(8,128)S(1)}, f32[8,32,256]{2,1,0:T(8,128)S(1)}, u32[]{:S(2)}, u32[]{:S(2)}) collective-permute-start(f32[8,32,256]{2,1,0:T(8,128)S(1)} %get-tuple-element.48), channel_id=1, source_target_pairs={{0,8},{1,9},{2,10},{3,11},{4,12},{5,13},{6,14},{7,15},{8,0},{9,1},... | collective-permute-start | bytes 786440 | tf_op jit(solution)/shard_map/ppermute | solution.py:676
  15.3 7.3 %collective-permute-start.6 = (f32[4,32,256]{2,1,0:T(8,128)S(1)}, f32[4,32,256]{2,1,0:T(8,128)S(1)}, u32[]{:S(2)}, u32[]{:S(2)}) collective-permute-start(f32[4,32,256]{2,1,0:T(8,128)S(1)} %get-tuple-element.49), channel_id=1, source_target_pairs={{0,32},{1,33},{2,34},{3,35},{4,36},{5,37},{6,38},{7,39},{8,40},{9,... | collective-permute-start | bytes 393224 | tf_op jit(solution)/shard_map/ppermute | solution.py:676
  16.6 6.8 %collective-permute-start.5 = (f32[4,32,256]{2,1,0:T(8,128)S(1)}, f32[4,32,256]{2,1,0:T(8,128)S(1)}, u32[]{:S(2)}, u32[]{:S(2)}) collective-permute-start(f32[4,32,256]{2,1,0:T(8,128)S(1)} %get-tuple-element.49), channel_id=1, source_target_pairs={{0,8},{1,9},{2,10},{3,11},{4,12},{5,13},{6,14},{7,15},{8,0},{9,1},... | collective-permute-start | bytes 393224 | tf_op jit(solution)/shard_map/ppermute | solution.py:676
  24.6 8.1 %collective-permute-start.7 = (f32[248,256]{1,0:T(8,128)S(1)}, f32[248,256]{1,0:T(8,128)S(1)}, u32[]{:S(2)}, u32[]{:S(2)}) collective-permute-start(f32[248,256]{1,0:T(8,128)S(1)} %get-tuple-element.59), channel_id=1, source_target_pairs={{0,32},{1,33},{2,34},{3,35},{4,36},{5,37},{6,38},{7,39},{8,40},{9,... | collective-permute-start | bytes 761864 | tf_op jit(solution)/shard_map/ppermute | solution.py:676
  24.7 9.7 %collective-permute-start.8 = (f32[248,256]{1,0:T(8,128)S(1)}, f32[248,256]{1,0:T(8,128)S(1)}, u32[]{:S(2)}, u32[]{:S(2)}) collective-permute-start(f32[248,256]{1,0:T(8,128)S(1)} %get-tuple-element.60), channel_id=1, source_target_pairs={{0,8},{1,9},{2,10},{3,11},{4,12},{5,13},{6,14},{7,15},{8,0},{9,1},... | collective-permute-start | bytes 761864 | tf_op jit(solution)/shard_map/ppermute | solution.py:676
